TPU v7x, 512 devices: a whole 4x4x16 slice. The times are simulated.
512 devices in a mesh: cp: 32 (over z, core), hd: 4 (over x), dp: 4 (over y).
Axes of the slice: x: 4, y: 4, z: 16, core: 2. Of those that a mesh axis runs over, the one named last changes fastest.
Arguments:
- queries: bfloat16 [32768, 4096], P(('dp', 'cp'), 'hd'), parts along dimension 0, may hold values from -10 to 10
- keys: bfloat16 [32768, 512], P(('dp', 'cp'), 'hd'), parts along dimension 0, may hold values from -4.5 to 4.5
- values: bfloat16 [32768, 512], P(('dp', 'cp'), 'hd'), parts along dimension 0, may hold values from -6 to 6
- outputs: bfloat16 [32768, 4096], P(('dp', 'cp'), 'hd'), parts along dimension 0, may hold values from -6 to 6
- out_grad: bfloat16 [32768, 4096], P(('dp', 'cp'), 'hd'), parts along dimension 0, may hold values from -6 to 6
- doc_lengths: int32 [204], P('dp'), parts along dimension 0, may hold values from 1 to 1920, as said below
- block_offsets: int32 [128, 16], P(('dp', 'cp')), parts along dimension 0, may hold values from -1 to 7, as said below
Outputs:
- grad_queries: bfloat16 [32768, 4096], P(('dp', 'cp'), 'hd'), parts along dimension 0
- grad_keys: bfloat16 [32768, 512], P(('dp', 'cp'), 'hd'), parts along dimension 0
- grad_values: bfloat16 [32768, 512], P(('dp', 'cp'), 'hd'), parts along dimension 0
There are 4 independent parts, one for each index of `dp`. A program takes and returns all parts, laid end to end along the dimension named above; each array names one. Nothing has to cross between parts.
Inputs may be any that keep to these rules, and one draw needn't show every extreme that they name: `doc_lengths`: documents are whole numbers of tokens in order that sum to 8192; the longest holds exactly 1920 tokens. `block_offsets`: row b holds each of the offsets 0, 1, ..., m_b exactly once, in slots and an order drawn from the seed, and -1 in its other slots, where j <= m_b exactly when some token of block b - j shares a document with some token of block b at or before it; some row holds 7.
All inputs are finite; a program needn't handle non-finite values.
Results may differ from a plain program's by a relative error of at most 0.0049.
Values may be sent and summed in bfloat16 or wider, within the bound.
No kernel may reach another device: no remote copies, remote signals or barrier semaphores. Data moves between devices by JAX's collectives and lax.ppermute only.
A program may use at most 64 MiB of HBM per device.

v0:
```python
import jax
import jax.numpy as jnp
from jax import lax
from jax.sharding import PartitionSpec as P

HD = 128


NEG_FILL = -1e30


def passed_along(array, axis, by):
    length = lax.axis_size(axis)
    pairs = [(i, i + by) for i in range(length) if 0 <= i + by < length]
    return lax.ppermute(array, axis, pairs)


def segment_of(positions, doc_ends):
    return jnp.sum((positions[:, None] >= doc_ends[None, :]).astype(jnp.int32), axis=1)


def on_device(queries, keys, values, outputs, out_grad, doc_lengths, block_offsets):
    row_count = queries.shape[0]
    slot_count = block_offsets.shape[1]
    span_blocks = slot_count // 2
    kv_heads = keys.shape[1] // HD
    q_heads = queries.shape[1] // HD
    group_size = q_heads // kv_heads
    kv_cols = kv_heads * HD
    factor = HD ** (-0.5)
    device = lax.axis_index("cp")
    local_pair = jnp.concatenate([keys, values], axis=1)
    pieces = [local_pair]
    for distance in range(1, span_blocks):
        pieces.append(passed_along(local_pair, "cp", distance))
    window = jnp.stack(pieces)
    doc_ends = jnp.cumsum(doc_lengths)
    arange_rows = jnp.arange(row_count, dtype=jnp.int32)
    q_pos = device * row_count + arange_rows
    q_seg = segment_of(q_pos, doc_ends)
    q_split = queries.reshape(row_count, kv_heads, group_size, HD)
    grad_split = out_grad.reshape(row_count, kv_heads, group_size, HD)
    delta_rows = jnp.sum(
        (out_grad.astype(jnp.float32) * outputs.astype(jnp.float32)).reshape(
            row_count, kv_heads, group_size, HD
        ),
        axis=3,
    )
    delta_rows = jnp.transpose(delta_rows, (1, 2, 0))
    offsets_row = block_offsets[0]

    def pair_terms(offset):
        kv_block = lax.dynamic_index_in_dim(window, offset, 0, keepdims=False)
        key_part = kv_block[:, :kv_cols].reshape(row_count, kv_heads, HD)
        value_part = kv_block[:, kv_cols:].reshape(row_count, kv_heads, HD)
        k_pos = (device - offset) * row_count + arange_rows
        pair_mask = q_seg[:, None] == segment_of(k_pos, doc_ends)[None, :]
        pair_mask = pair_mask & (k_pos[None, :] <= q_pos[:, None]) & (k_pos[None, :] >= 0)
        scores = factor * jnp.einsum(
            "tkgd,ukd->kgtu", q_split, key_part, preferred_element_type=jnp.float32
        )
        return (scores, pair_mask, key_part, value_part)

    def keep_state(carried):
        return carried

    def stats_step(slot_idx, carried):
        offset = offsets_row[slot_idx]
        safe_offset = jnp.maximum(offset, 0)

        def stats_update(state):
            run_max, run_sum = state
            terms = pair_terms(safe_offset)
            masked = jnp.where(terms[1], terms[0], NEG_FILL)
            new_max = jnp.maximum(run_max, jnp.max(masked, axis=3))
            exp_terms = jnp.where(terms[1], jnp.exp(masked - new_max[..., None]), 0.0)
            return (new_max, run_sum * jnp.exp(run_max - new_max) + jnp.sum(exp_terms, axis=3))

        return lax.cond(offset >= 0, stats_update, keep_state, carried)

    start_max = jnp.full((kv_heads, group_size, row_count), NEG_FILL, jnp.float32)
    start_sum = jnp.zeros((kv_heads, group_size, row_count), jnp.float32)
    run_max, run_sum = lax.fori_loop(0, slot_count, stats_step, (start_max, start_sum))
    lse = run_max + jnp.log(run_sum)

    def grad_step(slot_idx, carried):
        offset = offsets_row[slot_idx]
        safe_offset = jnp.maximum(offset, 0)

        def grad_update(state):
            dq_acc, partials = state
            scores, pair_mask, key_part, value_part = pair_terms(safe_offset)
            probs = jnp.where(pair_mask, jnp.exp(scores - lse[..., None]), 0.0)
            probs_low = probs.astype(jnp.bfloat16)
            d_prob = jnp.einsum(
                "tkgd,ukd->kgtu", grad_split, value_part, preferred_element_type=jnp.float32
            )
            d_score = (probs * (d_prob - delta_rows[..., None])).astype(jnp.bfloat16)
            dq_acc = dq_acc + factor * jnp.einsum(
                "kgtu,ukd->tkgd", d_score, key_part, preferred_element_type=jnp.float32
            )
            d_key = factor * jnp.einsum(
                "kgtu,tkgd->ukd", d_score, q_split, preferred_element_type=jnp.float32
            )
            d_value = jnp.einsum(
                "kgtu,tkgd->ukd", probs_low, grad_split, preferred_element_type=jnp.float32
            )
            grad_piece = jnp.concatenate(
                [d_key.reshape(row_count, kv_cols), d_value.reshape(row_count, kv_cols)], axis=1
            )
            partials = lax.dynamic_update_index_in_dim(partials, grad_piece, safe_offset, 0)
            return (dq_acc, partials)

        return lax.cond(offset >= 0, grad_update, keep_state, carried)

    start_dq = jnp.zeros((row_count, kv_heads, group_size, HD), jnp.float32)
    start_parts = jnp.zeros((span_blocks, row_count, 2 * kv_cols), jnp.float32)
    dq_acc, partials = lax.fori_loop(0, slot_count, grad_step, (start_dq, start_parts))
    summed = partials[0]
    for distance in range(1, span_blocks):
        summed = summed + passed_along(partials[distance], "cp", -distance)
    grad_queries = dq_acc.reshape(row_count, q_heads * HD).astype(jnp.bfloat16)
    grad_keys = summed[:, :kv_cols].astype(jnp.bfloat16)
    grad_values = summed[:, kv_cols:].astype(jnp.bfloat16)
    return (grad_queries, grad_keys, grad_values)


def solution(mesh):
    return jax.shard_map(
        on_device,
        mesh=mesh,
        in_specs=(
            P(("dp", "cp"), "hd"),
            P(("dp", "cp"), "hd"),
            P(("dp", "cp"), "hd"),
            P(("dp", "cp"), "hd"),
            P(("dp", "cp"), "hd"),
            P("dp"),
            P(("dp", "cp"), None),
        ),
        out_specs=(P(("dp", "cp"), "hd"), P(("dp", "cp"), "hd"), P(("dp", "cp"), "hd")),
        check_vma=False,
    )
```

profile of v0, /device:TPU:165, one launch (start us, length us, event | category | flops | bytes accessed | tf_op | source)
XLA Modules:
  0.0 234.6 jit_solution(13813643664543507866)
XLA Ops:
  0.7 0.9 constant_dynamic-update-slice_fusion.1
  1.6 0.9 constant_dynamic-update-slice_fusion
  2.5 8.5 %collective-permute-start.6 = (bf16[256,256]{1,0:T(8,128)(2,1)S(1)}, bf16[256,256]{1,0:T(8,128)(2,1)S(1)}, u32[]{:S(2)}, u32[]{:S(2)}) collective-permute-start(bf16[256,256]{1,0:T(8,128)(2,1)S(1)} %constant_dynamic-update-slice_fusion), channel_id=1, source_target_pairs={{0,112},{16,128},{32,144},{48,160},{64,176},{80,192},{96,208},{112... | collective-permute-start | bytes 393224 | tf_op jit(solution)/shard_map/ppermute | solution.py:15
  11.0 3.6 %collective-permute-start.5 = (bf16[256,256]{1,0:T(8,128)(2,1)S(1)}, bf16[256,256]{1,0:T(8,128)(2,1)S(1)}, u32[]{:S(2)}, u32[]{:S(2)}) collective-permute-start(bf16[256,256]{1,0:T(8,128)(2,1)S(1)} %constant_dynamic-update-slice_fusion), channel_id=1, source_target_pairs={{0,96},{16,112},{32,128},{48,144},{64,160},{80,176},{96,192},{112,... | collective-permute-start | bytes 393224 | tf_op jit(solution)/shard_map/ppermute | solution.py:15
  14.5 3.1 %collective-permute-start.4 = (bf16[256,256]{1,0:T(8,128)(2,1)S(1)}, bf16[256,256]{1,0:T(8,128)(2,1)S(1)}, u32[]{:S(2)}, u32[]{:S(2)}) collective-permute-start(bf16[256,256]{1,0:T(8,128)(2,1)S(1)} %constant_dynamic-update-slice_fusion), channel_id=1, source_target_pairs={{0,80},{16,96},{32,112},{48,128},{64,144},{80,160},{96,176},{112,1... | collective-permute-start | bytes 393224 | tf_op jit(solution)/shard_map/ppermute | solution.py:15
  17.6 1.9 collective-permute-start.3
  19.6 2.9 %collective-permute-start = (bf16[256,256]{1,0:T(8,128)(2,1)S(1)}, bf16[256,256]{1,0:T(8,128)(2,1)S(1)}, u32[]{:S(2)}, u32[]{:S(2)}) collective-permute-start(bf16[256,256]{1,0:T(8,128)(2,1)S(1)} %constant_dynamic-update-slice_fusion), channel_id=1, source_target_pairs={{0,16},{16,32},{32,48},{48,64},{64,80},{80,96},{96,112},{112,128},... | collective-permute-start | bytes 393224 | tf_op jit(solution)/shard_map/ppermute | solution.py:15
  22.5 0.7 bitcast_dynamic-update-slice_fusion.7
  23.2 1.4 multiply_bitcast_fusion
  25.6 1.2 copy.96
  26.8 1.6 reduce_sum.50
  28.5 13.3 %collective-permute-done = bf16[256,256]{1,0:T(8,128)(2,1)S(1)} collective-permute-done((bf16[256,256]{1,0:T(8,128)(2,1)S(1)}, bf16[256,256]{1,0:T(8,128)(2,1)S(1)}, u32[]{:S(2)}, u32[]{:S(2)}) %collective-permute-start) | collective-permute-done | bytes 131104 | tf_op jit(solution)/shard_map/ppermute | solution.py:15
  41.8 3.0 %collective-permute-start.1 = (bf16[256,256]{1,0:T(8,128)(2,1)S(1)}, bf16[256,256]{1,0:T(8,128)(2,1)S(1)}, u32[]{:S(2)}, u32[]{:S(2)}) collective-permute-start(bf16[256,256]{1,0:T(8,128)(2,1)S(1)} %constant_dynamic-update-slice_fusion), channel_id=1, source_target_pairs={{0,32},{16,48},{32,64},{48,80},{64,96},{80,112},{96,128},{112,144}... | collective-permute-start | bytes 393224 | tf_op jit(solution)/shard_map/ppermute | solution.py:15
  44.8 0.7 bitcast_dynamic-update-slice_fusion.6
  45.5 2.0 collective-permute-done.1
  47.5 7.2 %collective-permute-start.2 = (bf16[256,256]{1,0:T(8,128)(2,1)S(1)}, bf16[256,256]{1,0:T(8,128)(2,1)S(1)}, u32[]{:S(2)}, u32[]{:S(2)}) collective-permute-start(bf16[256,256]{1,0:T(8,128)(2,1)S(1)} %constant_dynamic-update-slice_fusion), channel_id=1, source_target_pairs={{0,48},{16,64},{32,80},{48,96},{64,112},{80,128},{96,144},{112,160... | collective-permute-start | bytes 393224 | tf_op jit(solution)/shard_map/ppermute | solution.py:15
  54.8 0.7 bitcast_dynamic-update-slice_fusion.5
  55.4 2.6 %collective-permute-done.2 = bf16[256,256]{1,0:T(8,128)(2,1)S(1)} collective-permute-done((bf16[256,256]{1,0:T(8,128)(2,1)S(1)}, bf16[256,256]{1,0:T(8,128)(2,1)S(1)}, u32[]{:S(2)}, u32[]{:S(2)}) %collective-permute-start.2) | collective-permute-done | bytes 131104 | tf_op jit(solution)/shard_map/ppermute | solution.py:15
  58.1 0.7 bitcast_dynamic-update-slice_fusion.4
  59.4 0.7 bitcast_dynamic-update-slice_fusion.2
  60.1 0.7 bitcast_dynamic-update-slice_fusion.1
  60.7 0.7 bitcast_dynamic-update-slice_fusion
  61.4 26.9 %while.32 = (s32[]{:T(128)}, f32[1,8,256]{2,1,0:T(8,128)S(1)}, f32[1,8,256]{2,1,0:T(8,128)S(1)}, s32[16]{0:T(128)S(1)}, s32[256]{0:T(256)S(1)}, /*index=5*/s32[]...) while((s32[]{:T(128)}, f32[1,8,256]{2,1,0:T(8,128)S(1)}, ...), condition=%wide.region_8.9_spmd.clone, body=%wide.region_2.8_spmd.clone.sunk | while | flops 138717952 | bytes 5361683 | solution.py:83
  62.7 2.9 %conditional.6 = ((f32[1,8,256]{2,1,0:T(8,128)S(1)}, f32[1,8,256]{2,1,0:T(8,128)S(1)})) conditional(s32[]{:T(128)} %convert_element_type.64, (f32[1,8,256]{2,1,0:T(8,128)S(1)}, f32[1,8,256]{2,1,0:T(8,128)S(1)}) %tuple.98, (s32[256]{0:T(256)S(1)}, s32[]{:T(128)}, s32[]{:T(128)}, s32[256]{0:T(256)S(1)}, s32[51]{0:T(128)S(1)}, /*index=5*/s32[]{:T(128)}, ...), branch_computations={%region_3.3_spmd, %region_4.7_spmd} | conditional | flops 138717952 | bytes 5360404 | solution.py:79
  63.6 0.9 dynamic-slice_bitcast_fusion
  65.6 0.6 dynamic_slice.27
  66.9 0.6 dynamic_slice.27
  68.2 0.6 dynamic_slice.27
  69.6 0.6 dynamic_slice.27
  70.9 0.6 dynamic_slice.27
  72.2 2.9 %conditional.6 = ((f32[1,8,256]{2,1,0:T(8,128)S(1)}, f32[1,8,256]{2,1,0:T(8,128)S(1)})) conditional(s32[]{:T(128)} %convert_element_type.64, (f32[1,8,256]{2,1,0:T(8,128)S(1)}, f32[1,8,256]{2,1,0:T(8,128)S(1)}) %tuple.98, (s32[256]{0:T(256)S(1)}, s32[]{:T(128)}, s32[]{:T(128)}, s32[256]{0:T(256)S(1)}, s32[51]{0:T(128)S(1)}, /*index=5*/s32[]{:T(128)}, ...), branch_computations={%region_3.3_spmd, %region_4.7_spmd} | conditional | flops 138717952 | bytes 5360404 | solution.py:79
  73.1 0.9 dynamic-slice_bitcast_fusion
  75.1 0.6 dynamic_slice.27
  76.4 0.6 dynamic_slice.27
  77.7 0.6 dynamic_slice.27
  79.1 0.6 dynamic_slice.27
  80.4 0.6 dynamic_slice.27
  81.7 0.6 dynamic_slice.27
  83.0 0.6 dynamic_slice.27
  85.7 0.6 dynamic_slice.27
  88.4 1.5 broadcast_in_dim.54
  89.9 30.5 %while.33 = (s32[]{:T(128)}, f32[256,1,8,128]{0,3,2,1:T(8,128)S(1)}, f32[8,256,256]{1,2,0:T(8,128)}, s32[16]{0:T(128)S(1)}, bf16[8,256,256]{2,1,0:T(8,128)(2,1)}...) while((s32[]{:T(128)}, ...), condition=%wide.region_14.15_spmd.clone, body=%wide.region_10.14_spmd.clone.sunk | while | flops 675683072 | bytes 15036487 | solution.py:118
  91.2 5.0 %conditional.7 = ((f32[256,1,8,128]{0,3,2,1:T(8,128)S(1)}, f32[8,256,256]{1,2,0:T(8,128)})) conditional(s32[]{:T(128)} %convert_element_type.65, (f32[256,1,8,128]{0,3,2,1:T(8,128)S(1)}, f32[8,256,256]{1,2,0:T(8,128)}) %tuple.101, (s32[]{:T(128)}, bf16[8,256,256]{2,1,0:T(8,128)(2,1)}, s32[256]{0:T(256)S(1)}, s32[]{:T(128)}, s32[256]{0:T(256)S(1)}, ...), branch_computations={%region_11.11_spmd, %region_12.13_spmd} | conditional | flops 675683072 | bytes 15035160 | solution.py:114
  92.1 0.9 dynamic-slice_bitcast_fusion.1
  95.4 0.7 fusion.25
  102.5 5.0 %conditional.7 = ((f32[256,1,8,128]{0,3,2,1:T(8,128)S(1)}, f32[8,256,256]{1,2,0:T(8,128)})) conditional(s32[]{:T(128)} %convert_element_type.65, (f32[256,1,8,128]{0,3,2,1:T(8,128)S(1)}, f32[8,256,256]{1,2,0:T(8,128)}) %tuple.101, (s32[]{:T(128)}, bf16[8,256,256]{2,1,0:T(8,128)(2,1)}, s32[256]{0:T(256)S(1)}, s32[]{:T(128)}, s32[256]{0:T(256)S(1)}, ...), branch_computations={%region_11.11_spmd, %region_12.13_spmd} | conditional | flops 675683072 | bytes 15035160 | solution.py:114
  103.5 0.9 dynamic-slice_bitcast_fusion.1
  106.8 0.7 fusion.25
  120.4 2.9 %copy.80 = f32[8,256,256]{2,1,0:T(8,128)} copy(f32[8,256,256]{1,2,0:T(8,128)} %get-tuple-element.514) | data formatting | bytes 4194304 | tf_op jit(solution)/shard_map/while | solution.py:118
  123.4 1.6 slice_bitcast_fusion.13
  125.0 5.2 %collective-permute-start.7 = (f32[256,256]{1,0:T(8,128)S(1)}, f32[256,256]{1,0:T(8,128)S(1)}, u32[]{:S(2)}, u32[]{:S(2)}) collective-permute-start(f32[256,256]{1,0:T(8,128)S(1)} %get-tuple-element.697), channel_id=1, source_target_pairs={{16,0},{32,16},{48,32},{64,48},{80,64},{96,80},{112,96},{128,112},... | collective-permute-start | bytes 786440 | tf_op jit(solution)/shard_map/ppermute | solution.py:15
  130.1 19.5 %collective-permute-start.13 = (f32[256,256]{1,0:T(8,128)S(1)}, f32[256,256]{1,0:T(8,128)S(1)}, u32[]{:S(2)}, u32[]{:S(2)}) collective-permute-start(f32[256,256]{1,0:T(8,128)S(1)} %get-tuple-element.698), channel_id=1, source_target_pairs={{112,0},{128,16},{144,32},{160,48},{176,64},{192,80},{208,96},{224... | collective-permute-start | bytes 786440 | tf_op jit(solution)/shard_map/ppermute | solution.py:15
  149.7 12.5 %collective-permute-start.12 = (f32[256,256]{1,0:T(8,128)S(1)}, f32[256,256]{1,0:T(8,128)}, u32[]{:S(2)}, u32[]{:S(2)}) collective-permute-start(f32[256,256]{1,0:T(8,128)S(1)} %get-tuple-element.699), channel_id=1, source_target_pairs={{96,0},{112,16},{128,32},{144,48},{160,64},{176,80},{192,96},{208,... | collective-permute-start | bytes 786440 | tf_op jit(solution)/shard_map/ppermute | solution.py:15
  162.2 10.5 %collective-permute-start.11 = (f32[256,256]{1,0:T(8,128)S(1)}, f32[256,256]{1,0:T(8,128)}, u32[]{:S(2)}, u32[]{:S(2)}) collective-permute-start(f32[256,256]{1,0:T(8,128)S(1)} %get-tuple-element.700), channel_id=1, source_target_pairs={{80,0},{96,16},{112,32},{128,48},{144,64},{160,80},{176,96},{192,1... | collective-permute-start | bytes 786440 | tf_op jit(solution)/shard_map/ppermute | solution.py:15
  172.7 10.9 %collective-permute-start.10 = (f32[256,256]{1,0:T(8,128)S(1)}, f32[256,256]{1,0:T(8,128)}, u32[]{:S(2)}, u32[]{:S(2)}) collective-permute-start(f32[256,256]{1,0:T(8,128)S(1)} %get-tuple-element.701), channel_id=1, source_target_pairs={{64,0},{80,16},{96,32},{112,48},{128,64},{144,80},{160,96},{176,11... | collective-permute-start | bytes 786440 | tf_op jit(solution)/shard_map/ppermute | solution.py:15
  183.6 12.3 %collective-permute-start.9 = (f32[256,256]{1,0:T(8,128)S(1)}, f32[256,256]{1,0:T(8,128)}, u32[]{:S(2)}, u32[]{:S(2)}) collective-permute-start(f32[256,256]{1,0:T(8,128)S(1)} %get-tuple-element.702), channel_id=1, source_target_pairs={{48,0},{64,16},{80,32},{96,48},{112,64},{128,80},{144,96},{160,112... | collective-permute-start | bytes 786440 | tf_op jit(solution)/shard_map/ppermute | solution.py:15
  195.9 1.9 collective-permute-start.8
  197.9 1.0 copy.95
  198.9 2.4 %collective-permute-done.11 = f32[256,256]{1,0:T(8,128)} collective-permute-done((f32[256,256]{1,0:T(8,128)S(1)}, f32[256,256]{1,0:T(8,128)}, u32[]{:S(2)}, u32[]{:S(2)}) %collective-permute-start.11) | collective-permute-done | bytes 262176 | tf_op jit(solution)/shard_map/ppermute | solution.py:15
  201.4 15.0 %collective-permute-done.10 = f32[256,256]{1,0:T(8,128)} collective-permute-done((f32[256,256]{1,0:T(8,128)S(1)}, f32[256,256]{1,0:T(8,128)}, u32[]{:S(2)}, u32[]{:S(2)}) %collective-permute-start.10) | collective-permute-done | bytes 262176 | tf_op jit(solution)/shard_map/ppermute | solution.py:15
  216.3 8.3 %collective-permute-done.9 = f32[256,256]{1,0:T(8,128)} collective-permute-done((f32[256,256]{1,0:T(8,128)S(1)}, f32[256,256]{1,0:T(8,128)}, u32[]{:S(2)}, u32[]{:S(2)}) %collective-permute-start.9) | collective-permute-done | bytes 262176 | tf_op jit(solution)/shard_map/ppermute | solution.py:15
  224.6 7.9 %collective-permute-done.8 = f32[256,256]{1,0:T(8,128)} collective-permute-done((f32[256,256]{1,0:T(8,128)S(1)}, f32[256,256]{1,0:T(8,128)}, u32[]{:S(2)}, u32[]{:S(2)}) %collective-permute-start.8) | collective-permute-done | bytes 262176 | tf_op jit(solution)/shard_map/ppermute | solution.py:15
  232.5 1.5 fusion.33
  234.0 0.7 fusion.34
  (145 shorter events, 21.5 us)
Async XLA Ops:
  0.6 23.9 %copy-start = (bf16[256,1024]{1,0:T(8,128)(2,1)S(1)}, bf16[256,1024]{1,0:T(8,128)(2,1)}, u32[]{:S(2)}) copy-start(bf16[256,1024]{1,0:T(8,128)(2,1)} %param.19) | copy-start | bytes 1572868
  0.6 24.1 %copy-start.2 = (s32[51]{0:T(128)S(1)}, s32[51]{0:T(128)}, u32[]{:S(2)}) copy-start(s32[51]{0:T(128)} %param.20) | copy-start | bytes 616
  0.7 24.4 %copy-start.1 = (bf16[256,1024]{1,0:T(8,128)(2,1)S(1)}, bf16[256,1024]{1,0:T(8,128)(2,1)}, u32[]{:S(2)}) copy-start(bf16[256,1024]{1,0:T(8,128)(2,1)} %param.15) | copy-start | bytes 1572868
  2.5 58.3 %collective-permute-start.6 = (bf16[256,256]{1,0:T(8,128)(2,1)S(1)}, bf16[256,256]{1,0:T(8,128)(2,1)S(1)}, u32[]{:S(2)}, u32[]{:S(2)}) collective-permute-start(bf16[256,256]{1,0:T(8,128)(2,1)S(1)} %constant_dynamic-update-slice_fusion), channel_id=1, source_target_pairs={{0,112},{16,128},{32,144},{48,160},{64,176},{80,192},{96,208},{112... | collective-permute-start | bytes 393224 | tf_op jit(solution)/shard_map/ppermute | solution.py:15
  11.0 49.1 %collective-permute-start.5 = (bf16[256,256]{1,0:T(8,128)(2,1)S(1)}, bf16[256,256]{1,0:T(8,128)(2,1)S(1)}, u32[]{:S(2)}, u32[]{:S(2)}) collective-permute-start(bf16[256,256]{1,0:T(8,128)(2,1)S(1)} %constant_dynamic-update-slice_fusion), channel_id=1, source_target_pairs={{0,96},{16,112},{32,128},{48,144},{64,160},{80,176},{96,192},{112,... | collective-permute-start | bytes 393224 | tf_op jit(solution)/shard_map/ppermute | solution.py:15
  14.5 44.9 %collective-permute-start.4 = (bf16[256,256]{1,0:T(8,128)(2,1)S(1)}, bf16[256,256]{1,0:T(8,128)(2,1)S(1)}, u32[]{:S(2)}, u32[]{:S(2)}) collective-permute-start(bf16[256,256]{1,0:T(8,128)(2,1)S(1)} %constant_dynamic-update-slice_fusion), channel_id=1, source_target_pairs={{0,80},{16,96},{32,112},{48,128},{64,144},{80,160},{96,176},{112,1... | collective-permute-start | bytes 393224 | tf_op jit(solution)/shard_map/ppermute | solution.py:15
  17.6 41.1 %collective-permute-start.3 = (bf16[256,256]{1,0:T(8,128)(2,1)S(1)}, bf16[256,256]{1,0:T(8,128)(2,1)S(1)}, u32[]{:S(2)}, u32[]{:S(2)}) collective-permute-start(bf16[256,256]{1,0:T(8,128)(2,1)S(1)} %constant_dynamic-update-slice_fusion), channel_id=1, source_target_pairs={{0,64},{16,80},{32,96},{48,112},{64,128},{80,144},{96,160},{112,17... | collective-permute-start | bytes 393224 | tf_op jit(solution)/shard_map/ppermute | solution.py:15
  19.6 22.3 %collective-permute-start = (bf16[256,256]{1,0:T(8,128)(2,1)S(1)}, bf16[256,256]{1,0:T(8,128)(2,1)S(1)}, u32[]{:S(2)}, u32[]{:S(2)}) collective-permute-start(bf16[256,256]{1,0:T(8,128)(2,1)S(1)} %constant_dynamic-update-slice_fusion), channel_id=1, source_target_pairs={{0,16},{16,32},{32,48},{48,64},{64,80},{80,96},{96,112},{112,128},... | collective-permute-start | bytes 393224 | tf_op jit(solution)/shard_map/ppermute | solution.py:15
  26.8 34.6 %copy-start.3 = (s32[1,16]{1,0:T(1,128)S(1)}, s32[1,16]{1,0:T(1,128)}, u32[]{:S(2)}) copy-start(s32[1,16]{1,0:T(1,128)} %param.21) | copy-start | bytes 196
  41.8 5.7 %collective-permute-start.1 = (bf16[256,256]{1,0:T(8,128)(2,1)S(1)}, bf16[256,256]{1,0:T(8,128)(2,1)S(1)}, u32[]{:S(2)}, u32[]{:S(2)}) collective-permute-start(bf16[256,256]{1,0:T(8,128)(2,1)S(1)} %constant_dynamic-update-slice_fusion), channel_id=1, source_target_pairs={{0,32},{16,48},{32,64},{48,80},{64,96},{80,112},{96,128},{112,144}... | collective-permute-start | bytes 393224 | tf_op jit(solution)/shard_map/ppermute | solution.py:15
  47.5 10.6 %collective-permute-start.2 = (bf16[256,256]{1,0:T(8,128)(2,1)S(1)}, bf16[256,256]{1,0:T(8,128)(2,1)S(1)}, u32[]{:S(2)}, u32[]{:S(2)}) collective-permute-start(bf16[256,256]{1,0:T(8,128)(2,1)S(1)} %constant_dynamic-update-slice_fusion), channel_id=1, source_target_pairs={{0,48},{16,64},{32,80},{48,96},{64,112},{80,128},{96,144},{112,160... | collective-permute-start | bytes 393224 | tf_op jit(solution)/shard_map/ppermute | solution.py:15
  125.0 58.6 %collective-permute-start.7 = (f32[256,256]{1,0:T(8,128)S(1)}, f32[256,256]{1,0:T(8,128)S(1)}, u32[]{:S(2)}, u32[]{:S(2)}) collective-permute-start(f32[256,256]{1,0:T(8,128)S(1)} %get-tuple-element.697), channel_id=1, source_target_pairs={{16,0},{32,16},{48,32},{64,48},{80,64},{96,80},{112,96},{128,112},... | collective-permute-start | bytes 786440 | tf_op jit(solution)/shard_map/ppermute | solution.py:15
  130.1 65.8 %collective-permute-start.13 = (f32[256,256]{1,0:T(8,128)S(1)}, f32[256,256]{1,0:T(8,128)S(1)}, u32[]{:S(2)}, u32[]{:S(2)}) collective-permute-start(f32[256,256]{1,0:T(8,128)S(1)} %get-tuple-element.698), channel_id=1, source_target_pairs={{112,0},{128,16},{144,32},{160,48},{176,64},{192,80},{208,96},{224... | collective-permute-start | bytes 786440 | tf_op jit(solution)/shard_map/ppermute | solution.py:15
  149.7 49.2 %collective-permute-start.12 = (f32[256,256]{1,0:T(8,128)S(1)}, f32[256,256]{1,0:T(8,128)}, u32[]{:S(2)}, u32[]{:S(2)}) collective-permute-start(f32[256,256]{1,0:T(8,128)S(1)} %get-tuple-element.699), channel_id=1, source_target_pairs={{96,0},{112,16},{128,32},{144,48},{160,64},{176,80},{192,96},{208,... | collective-permute-start | bytes 786440 | tf_op jit(solution)/shard_map/ppermute | solution.py:15
  162.2 39.2 %collective-permute-start.11 = (f32[256,256]{1,0:T(8,128)S(1)}, f32[256,256]{1,0:T(8,128)}, u32[]{:S(2)}, u32[]{:S(2)}) collective-permute-start(f32[256,256]{1,0:T(8,128)S(1)} %get-tuple-element.700), channel_id=1, source_target_pairs={{80,0},{96,16},{112,32},{128,48},{144,64},{160,80},{176,96},{192,1... | collective-permute-start | bytes 786440 | tf_op jit(solution)/shard_map/ppermute | solution.py:15
  172.7 43.6 %collective-permute-start.10 = (f32[256,256]{1,0:T(8,128)S(1)}, f32[256,256]{1,0:T(8,128)}, u32[]{:S(2)}, u32[]{:S(2)}) collective-permute-start(f32[256,256]{1,0:T(8,128)S(1)} %get-tuple-element.701), channel_id=1, source_target_pairs={{64,0},{80,16},{96,32},{112,48},{128,64},{144,80},{160,96},{176,11... | collective-permute-start | bytes 786440 | tf_op jit(solution)/shard_map/ppermute | solution.py:15
  183.6 41.0 %collective-permute-start.9 = (f32[256,256]{1,0:T(8,128)S(1)}, f32[256,256]{1,0:T(8,128)}, u32[]{:S(2)}, u32[]{:S(2)}) collective-permute-start(f32[256,256]{1,0:T(8,128)S(1)} %get-tuple-element.702), channel_id=1, source_target_pairs={{48,0},{64,16},{80,32},{96,48},{112,64},{128,80},{144,96},{160,112... | collective-permute-start | bytes 786440 | tf_op jit(solution)/shard_map/ppermute | solution.py:15
  195.9 36.6 %collective-permute-start.8 = (f32[256,256]{1,0:T(8,128)S(1)}, f32[256,256]{1,0:T(8,128)}, u32[]{:S(2)}, u32[]{:S(2)}) collective-permute-start(f32[256,256]{1,0:T(8,128)S(1)} %get-tuple-element.703), channel_id=1, source_target_pairs={{32,0},{48,16},{64,32},{80,48},{96,64},{112,80},{128,96},{144,112}... | collective-permute-start | bytes 786440 | tf_op jit(solution)/shard_map/ppermute | solution.py:15
where the time goes:
time: 236 us; the launch traced here: 235 us
  starting transfers between devices  103 us (44%)
  waiting for transfers between devices  51.5 us (22%)
  local copies, waits for them, and re-layouts  40.4 us (17%)
  loops' own time  24.7 us (10%)
  other arithmetic  8.37 us (4%)
  matrix products  5.58 us (2%)
    ppermute x14, starting transfers between devices, passed_along(): return lax.ppermute(array, axis, pairs)  103 us
    ppermute x14, waiting for transfers between devices, passed_along(): return lax.ppermute(array, axis, pairs)  51.5 us
    another operation x1, loops' own time, on_device(): lax.fori_loop(0, slot_count, grad_step, (start_dq, start_parts))  10.9 us
    another operation x1, loops' own time, on_device(): lax.fori_loop(0, slot_count, stats_step, (start_max, start_sum))  10.5 us
    dynamic_slice x16, local copies, waits for them, and re-layouts, stats_step(): offset = offsets_row[slot_idx]  10.4 us
    dynamic_slice x16, local copies, waits for them, and re-layouts, grad_step(): offset = offsets_row[slot_idx]  9.37 us
    unnamed x21, local copies, waits for them, and re-layouts  7.55 us
  transfers between devices with their start and end apart: 14, of which 7 were waited for; matrix products, arithmetic and copies ran while one was open for 5% of the time, Pallas kernels for 0%

commit v1 on v0

v1 whole, which is shorter than its diff:
```python
import functools

import jax
import jax.numpy as jnp
from jax import lax
from jax.experimental import pallas as pl
from jax.experimental.pallas import tpu as pltpu
from jax.sharding import PartitionSpec as P

HD = 128
FACTOR = HD ** (-0.5)
SCORE_SCALE = FACTOR * 1.4426950408889634
MASKED = -1e30
EMPTY = -1e20
VMEM_BYTES = 32 * 1024 * 1024


def shift(array, by, parity=None):
    n = lax.axis_size("cp")
    pairs = [(i, (i + by) % n) for i in range(n) if parity is None or i % 2 == parity]
    return lax.ppermute(array, "cp", pairs)


def exchange(array):
    n = lax.axis_size("cp")
    return lax.ppermute(array, "cp", [(i, i ^ 1) for i in range(n)])


def nt_dot(a, b):
    return lax.dot_general(a, b, (((1,), (1,)), ((), ())), preferred_element_type=jnp.float32)


def nn_dot(a, b):
    return lax.dot_general(a, b, (((1,), (0,)), ((), ())), preferred_element_type=jnp.float32)


def side_block(side):
    block = lax.axis_index("cp")
    if side == 0:
        return block
    return block + 1 - 2 * lax.rem(block, 2)


def listed_pair(pay_ref, rows, side, slot):
    key_block = lax.axis_index("cp") - 2 * slot
    offset = side_block(side) - key_block
    row = pay_ref[rows:, 0:HD].astype(jnp.float32)
    hits = jnp.max((row == offset.astype(jnp.float32)).astype(jnp.float32))
    return (hits > 0.0) & (offset >= 0) & (key_block >= 0)


def write_bias(bias_ref, start_ref, side, slot):
    rows = bias_ref.shape[0]
    key_pos = (lax.axis_index("cp") - 2 * slot) * rows + lax.broadcasted_iota(jnp.int32, bias_ref.shape, 0)
    q_pos = side_block(side) * rows + lax.broadcasted_iota(jnp.int32, bias_ref.shape, 1)
    allowed = (key_pos >= start_ref[side : side + 1, :]) & (key_pos <= q_pos)
    bias_ref[...] = jnp.where(allowed, 0.0, MASKED)


def head_cols(head):
    return pl.ds(pl.multiple_of(head * HD, HD), HD)


def prep_kernel(q_ref, g_ref, o_ref, off_ref, pay_ref, delta_ref):
    rows, width = q_ref.shape
    slots = off_ref.shape[1]
    pay_ref[0:rows, 0:width] = q_ref[...]
    pay_ref[0:rows, width:] = g_ref[...]
    pay_ref[rows:, :] = jnp.full((16, 2 * width), -1.0, jnp.bfloat16)
    listed = jnp.broadcast_to(off_ref[...].astype(jnp.float32), (16, slots))
    pay_ref[rows:, 0:slots] = listed.astype(jnp.bfloat16)
    for head in range(width // HD):
        cols = slice(head * HD, (head + 1) * HD)
        product = g_ref[:, cols].astype(jnp.float32) * o_ref[:, cols].astype(jnp.float32)
        delta_ref[head : head + 1, :] = jnp.sum(product.T, axis=0, keepdims=True)


def stats_slots(slots, kv_refs, pay_refs, start_ref, m_ref, l_ref, bias_ref):
    rows = bias_ref.shape[0]
    heads = m_ref.shape[0] // 2
    for slot, kv_ref in zip(slots, kv_refs):
        for side in range(2):
            pay_ref = pay_refs[side]

            @pl.when(listed_pair(pay_ref, rows, side, slot))
            def _():
                write_bias(bias_ref, start_ref, side, slot)

                def body(head, carry):
                    row = pl.ds(side * heads + head, 1)
                    scores = nt_dot(kv_ref[:, 0:HD], pay_ref[0:rows, head_cols(head)])
                    scores = scores * SCORE_SCALE + bias_ref[...]
                    old_max = m_ref[row, :]
                    new_max = jnp.maximum(old_max, jnp.max(scores, axis=0, keepdims=True))
                    total = jnp.sum(jnp.exp2(scores - new_max), axis=0, keepdims=True)
                    l_ref[row, :] = l_ref[row, :] * jnp.exp2(old_max - new_max) + total
                    m_ref[row, :] = new_max
                    return carry

                lax.fori_loop(0, heads, body, 0, unroll=2)


def stats_near_kernel(doc_ref, own_ref, par_ref, kv0_ref, kv1_ref, kv2_ref, start_ref, m_ref, l_ref, bias_ref):
    rows = bias_ref.shape[0]
    lanes = lax.broadcasted_iota(jnp.int32, (1, rows), 1)
    positions = [side_block(side) * rows + lanes for side in range(2)]

    def step(doc, carry):
        end, first, second = carry
        end = end + doc_ref[doc]
        return (end, jnp.where(end <= positions[0], end, first), jnp.where(end <= positions[1], end, second))

    zero = jnp.zeros((1, rows), jnp.int32)
    _, first, second = lax.fori_loop(0, doc_ref.shape[0], step, (jnp.int32(0), zero, zero))
    start_ref[...] = jnp.zeros_like(start_ref)
    start_ref[0:1, :] = first
    start_ref[1:2, :] = second
    m_ref[...] = jnp.full_like(m_ref, EMPTY)
    l_ref[...] = jnp.zeros_like(l_ref)
    stats_slots((0, 1, 2), (kv0_ref, kv1_ref, kv2_ref), (own_ref, par_ref), start_ref, m_ref, l_ref, bias_ref)


def stats_far_kernel(own_ref, par_ref, start_ref, m_in, l_in, delta_ref, kv3_ref, kv4_ref, out_ref, m_ref, l_ref, bias_ref):
    m_ref[...] = m_in[...]
    l_ref[...] = l_in[...]
    stats_slots((3, 4), (kv3_ref, kv4_ref), (own_ref, par_ref), start_ref, m_ref, l_ref, bias_ref)
    stat_rows = m_ref.shape[0]
    total = l_ref[...]
    some = total > 0.0
    out_ref[0:stat_rows, :] = jnp.where(some, m_ref[...] + jnp.log2(jnp.where(some, total, 1.0)), EMPTY)
    out_ref[stat_rows:, :] = delta_ref[...]


def combine_stats(mine_ref, other_ref, lse_ref, delta_ref):
    heads = delta_ref.shape[0] // 2
    for side in range(2):
        a = mine_ref[side * heads : (side + 1) * heads, :]
        b = other_ref[(1 - side) * heads : (2 - side) * heads, :]
        top = jnp.maximum(a, b)
        lse_ref[side * heads : (side + 1) * heads, :] = top + jnp.log2(jnp.exp2(a - top) + jnp.exp2(b - top))
    delta_ref[0:heads, :] = mine_ref[2 * heads :, :]
    delta_ref[heads:, :] = other_ref[2 * heads :, :]


def grad_slot(slot, kv_ref, pay_refs, start_ref, lse_ref, delta_ref, dq_ref, bias_ref, kt_ref, dk_ref, dv_ref):
    rows = bias_ref.shape[0]
    heads = lse_ref.shape[0] // 2
    dk_ref[...] = jnp.zeros_like(dk_ref)
    dv_ref[...] = jnp.zeros_like(dv_ref)
    kt_ref[...] = kv_ref[:, 0:HD].T
    for side in range(2):
        pay_ref = pay_refs[side]
        width = pay_ref.shape[1] // 2

        @pl.when(listed_pair(pay_ref, rows, side, slot))
        def _():
            write_bias(bias_ref, start_ref, side, slot)

            def body(head, carry):
                row = pl.ds(side * heads + head, 1)
                q_head = pay_ref[0:rows, head_cols(head)]
                g_head = pay_ref[0:rows, head_cols(head + width // HD)]
                scores = nt_dot(kv_ref[:, 0:HD], q_head) * SCORE_SCALE + bias_ref[...]
                probs = jnp.exp2(scores - lse_ref[row, :])
                d_prob = nt_dot(kv_ref[:, HD:], g_head)
                d_score = (probs * (d_prob - delta_ref[row, :])).astype(jnp.bfloat16)
                dv_ref[...] += nn_dot(probs.astype(jnp.bfloat16), g_head)
                dk_ref[...] += nn_dot(d_score, q_head)
                at = pl.ds(pl.multiple_of((side * heads + head) * HD, HD), HD)
                dq_ref[at, :] += nn_dot(kt_ref[...], d_score)
                return carry

            lax.fori_loop(0, heads, body, 0, unroll=2)


def write_piece(out_ref, dk_ref, dv_ref):
    out_ref[:, 0:HD] = (dk_ref[...] * FACTOR).astype(out_ref.dtype)
    out_ref[:, HD:] = dv_ref[...].astype(out_ref.dtype)


def grad_far_kernel(own_ref, par_ref, start_ref, mine_ref, other_ref, kv3_ref, kv4_ref, p3_ref, p4_ref, dq_ref,
                    lse_ref, delta_ref, bias_ref, kt_ref, dk_ref, dv_ref):
    combine_stats(mine_ref, other_ref, lse_ref, delta_ref)
    dq_ref[...] = jnp.zeros_like(dq_ref)
    for slot, kv_ref, out_ref in ((4, kv4_ref, p4_ref), (3, kv3_ref, p3_ref)):
        grad_slot(slot, kv_ref, (own_ref, par_ref), start_ref, lse_ref, delta_ref, dq_ref, bias_ref, kt_ref, dk_ref, dv_ref)
        write_piece(out_ref, dk_ref, dv_ref)


def grad_near_kernel(own_ref, par_ref, start_ref, mine_ref, other_ref, kv0_ref, kv1_ref, kv2_ref, dq_in,
                     p0_ref, p1_ref, p2_ref, dq_own_ref, dq_par_ref,
                     lse_ref, delta_ref, bias_ref, kt_ref, dk_ref, dv_ref, dq_ref):
    combine_stats(mine_ref, other_ref, lse_ref, delta_ref)
    dq_ref[...] = dq_in[...]
    for slot, kv_ref, out_ref in ((2, kv2_ref, p2_ref), (1, kv1_ref, p1_ref), (0, kv0_ref, p0_ref)):
        grad_slot(slot, kv_ref, (own_ref, par_ref), start_ref, lse_ref, delta_ref, dq_ref, bias_ref, kt_ref, dk_ref, dv_ref)
        write_piece(out_ref, dk_ref, dv_ref)
    heads = lse_ref.shape[0] // 2
    for side, out_ref in ((0, dq_own_ref), (1, dq_par_ref)):
        for head in range(heads):
            at = (side * heads + head) * HD
            block = dq_ref[at : at + HD, :] * FACTOR
            out_ref[:, head * HD : (head + 1) * HD] = block.T.astype(out_ref.dtype)


def call(kernel, in_spaces, outs, scratch, flops, transcendentals, *args):
    moved = sum(a.size * a.dtype.itemsize for a in args) + sum(o.size * o.dtype.itemsize for o in outs)
    return pl.pallas_call(
        kernel,
        out_shape=outs,
        in_specs=[pl.BlockSpec(memory_space=space) for space in in_spaces],
        out_specs=[pl.BlockSpec(memory_space=pltpu.VMEM) for _ in outs],
        scratch_shapes=scratch,
        compiler_params=pltpu.CompilerParams(vmem_limit_bytes=VMEM_BYTES),
        cost_estimate=pl.CostEstimate(flops=flops, bytes_accessed=moved, transcendentals=transcendentals),
    )(*args)


def on_device(queries, keys, values, outputs, out_grad, doc_lengths, block_offsets):
    rows, width = queries.shape
    heads = width // HD
    struct = jax.ShapeDtypeStruct
    f32, bf16 = jnp.float32, jnp.bfloat16
    vmem, smem = pltpu.VMEM, pltpu.SMEM
    pair = 2 * heads * rows * rows

    kv = jnp.concatenate([keys, values], axis=1)
    kv2 = shift(kv, 4)
    kv1 = shift(kv, 2)
    pay, delta = call(
        prep_kernel, [vmem] * 4, [struct((rows + 16, 2 * width), bf16), struct((heads, rows), f32)], [],
        2 * rows * width, 0, queries, out_grad, outputs, block_offsets)
    par = exchange(pay)
    kv3 = shift(kv2, 2)
    kv4 = shift(kv2, 4, 1)

    stat = struct((2 * heads, rows), f32)
    bias = pltpu.VMEM((rows, rows), f32)
    start, m_near, l_near = call(
        stats_near_kernel, [smem] + [vmem] * 5, [struct((8, rows), jnp.int32), stat, stat], [bias],
        3 * pair * HD * 2, 3 * pair, doc_lengths, pay, par, kv, kv1, kv2)
    stat_scratch = pltpu.VMEM((2 * heads, rows), f32)
    (mine,) = call(
        stats_far_kernel, [vmem] * 8, [struct((3 * heads, rows), f32)], [stat_scratch, stat_scratch, bias],
        2 * pair * HD * 2, 2 * pair, pay, par, start, m_near, l_near, delta, kv3, kv4)
    other = exchange(mine)

    part = pltpu.VMEM((rows, HD), f32)
    scratch = [stat_scratch, stat_scratch, bias, pltpu.VMEM((HD, rows), bf16), part, part]
    piece16, piece32 = struct((rows, 2 * HD), bf16), struct((rows, 2 * HD), f32)
    dq_shape = (2 * width, rows)
    p3, p4, dq = call(
        grad_far_kernel, [vmem] * 7, [piece16, piece16, struct(dq_shape, f32)], scratch,
        2 * 5 * pair * HD * 2, 2 * pair, pay, par, start, mine, other, kv3, kv4)
    back4 = shift(p4, -4, 1)
    back3 = shift(p3, -2)
    p0, p1, p2, dq_own, dq_par = call(
        grad_near_kernel, [vmem] * 9,
        [piece32, piece16, piece32, struct((rows, width), f32), struct((rows, width), bf16)],
        scratch + [pltpu.VMEM(dq_shape, f32)],
        3 * 5 * pair * HD * 2, 3 * pair, pay, par, start, mine, other, kv, kv1, kv2, dq)
    back1 = shift(p1, -2)
    dq_other = exchange(dq_par)
    p2_sum = (p2 + back3.astype(f32) + back4.astype(f32)).astype(bf16)
    back2 = shift(p2_sum, -4)
    grad_queries = (dq_own + dq_other.astype(f32)).astype(bf16)
    summed = p0 + back1.astype(f32) + back2.astype(f32)
    return grad_queries, summed[:, :HD].astype(bf16), summed[:, HD:].astype(bf16)


def solution(mesh):
    tokens = P(("dp", "cp"), "hd")
    return jax.shard_map(
        on_device,
        mesh=mesh,
        in_specs=(tokens, tokens, tokens, tokens, tokens, P("dp"), P(("dp", "cp"), None)),
        out_specs=(tokens, tokens, tokens),
        check_vma=False,
    )
```

time: 236 us -> 84.8 us (0.36)
  the two profiles are of different devices: /device:TPU:165 before, /device:TPU:1 now
where the time goes in v1:
time: 84.8 us; the launch traced here: 83.8 us
  starting transfers between devices  57.8 us (68%)
  waiting for transfers between devices  11.3 us (13%)
  Pallas kernels  8.34 us (10%)
  local copies, waits for them, and re-layouts  4.48 us (5%)
  other arithmetic  1.06 us (1%)
  between operations  0.87 us (1%)
    ppermute x8, starting transfers between devices, shift(): return lax.ppermute(array, 'cp', pairs)  43.3 us
    ppermute x3, starting transfers between devices, exchange(): return lax.ppermute(array, 'cp', [(i, i ^ 1) for i in range(n)])  14.5 us
    ppermute x8, waiting for transfers between devices, shift(): return lax.ppermute(array, 'cp', pairs)  9.36 us
    pallas_call x5, Pallas kernels, call(): pl.pallas_call(kernel, out_shape=outs, in_specs=[pl.BlockSpec(memory_spac...  8.34 us
    unnamed x15, local copies, waits for them, and re-layouts  3.8 us
    ppermute x3, waiting for transfers between devices, exchange(): return lax.ppermute(array, 'cp', [(i, i ^ 1) for i in range(n)])  1.94 us
  transfers between devices with their start and end apart: 11, of which 4 were waited for; matrix products, arithmetic and copies ran while one was open for 1% of the time, Pallas kernels for 8%

profile of v1, /device:TPU:1, one launch (start us, length us, event | category | flops | bytes accessed | tf_op | source)
XLA Modules:
  0.0 83.8 jit_solution(16831615379880135364)
XLA Ops:
  0.6 0.0 copy-start
  0.6 1.0 %copy-done = bf16[256,1024]{1,0:T(8,128)(2,1)S(1)} copy-done((bf16[256,1024]{1,0:T(8,128)(2,1)S(1)}, bf16[256,1024]{1,0:T(8,128)(2,1)}, u32[]{:S(2)}) %copy-start) | copy-done | bytes 524312
  1.7 0.0 copy-start.1
  1.7 1.0 %copy-done.1 = bf16[256,1024]{1,0:T(8,128)(2,1)S(1)} copy-done((bf16[256,1024]{1,0:T(8,128)(2,1)S(1)}, bf16[256,1024]{1,0:T(8,128)(2,1)}, u32[]{:S(2)}) %copy-start.1) | copy-done | bytes 524312
  2.7 0.0 copy-start.2
  2.7 1.0 %copy-done.2 = bf16[256,1024]{1,0:T(8,128)(2,1)S(1)} copy-done((bf16[256,1024]{1,0:T(8,128)(2,1)S(1)}, bf16[256,1024]{1,0:T(8,128)(2,1)}, u32[]{:S(2)}) %copy-start.2) | copy-done | bytes 524312
  3.8 0.0 copy-start.3
  3.8 0.7 copy-done.3
  4.4 0.0 copy-start.5
  4.4 0.0 copy-start.6
  4.4 0.0 copy-start.4
  4.4 0.4 shard_map.94
  4.8 8.8 %collective-permute-start = (bf16[272,2048]{1,0:T(8,128)(2,1)S(1)}, bf16[272,2048]{1,0:T(8,128)(2,1)S(1)}, u32[]{:S(2)}, u32[]{:S(2)}) collective-permute-start(bf16[272,2048]{1,0:T(8,128)(2,1)S(1)} %get-tuple-element.16.own_ref), channel_id=1, source_target_pairs={{0,16},{16,0},{32,48},{48,32},{64,80},{80,64},{96,112},{112,96},{1... | collective-permute-start | bytes 3342344 | tf_op jit(solution)/shard_map/ppermute | solution.py:26
  13.6 0.0 copy-done.5
  13.6 0.0 copy-done.6
  13.6 1.9 %collective-permute-start.2 = (bf16[256,256]{1,0:T(8,128)(2,1)S(1)}, bf16[256,256]{1,0:T(8,128)(2,1)S(1)}, u32[]{:S(2)}, u32[]{:S(2)}) collective-permute-start(bf16[256,256]{1,0:T(8,128)(2,1)S(1)} %constant_dynamic-update-slice_fusion.kv0_ref), channel_id=1, source_target_pairs={{0,64},{16,80},{32,96},{48,112},{64,128},{80,144},{96,160},{112,17... | collective-permute-start | bytes 393224 | tf_op jit(solution)/shard_map/ppermute | solution.py:21
  15.6 1.9 %collective-permute-start.1 = (bf16[256,256]{1,0:T(8,128)(2,1)S(1)}, bf16[256,256]{1,0:T(8,128)(2,1)S(1)}, u32[]{:S(2)}, u32[]{:S(2)}) collective-permute-start(bf16[256,256]{1,0:T(8,128)(2,1)S(1)} %constant_dynamic-update-slice_fusion.kv0_ref), channel_id=1, source_target_pairs={{0,32},{16,48},{32,64},{48,80},{64,96},{80,112},{96,128},{112,144}... | collective-permute-start | bytes 393224 | tf_op jit(solution)/shard_map/ppermute | solution.py:21
  17.5 6.8 %collective-permute-done.2.kv2_ref = bf16[256,256]{1,0:T(8,128)(2,1)S(1)} collective-permute-done((bf16[256,256]{1,0:T(8,128)(2,1)S(1)}, bf16[256,256]{1,0:T(8,128)(2,1)S(1)}, u32[]{:S(2)}, u32[]{:S(2)}) %collective-permute-start.2) | collective-permute-done | bytes 131104 | tf_op jit(solution)/shard_map/ppermute | solution.py:21
  24.3 1.9 %collective-permute-start.4 = (bf16[256,256]{1,0:T(8,128)(2,1)S(1)}, bf16[256,256]{1,0:T(8,128)(2,1)S(1)}, u32[]{:S(2)}, u32[]{:S(2)}) collective-permute-start(bf16[256,256]{1,0:T(8,128)(2,1)S(1)} %collective-permute-done.2.kv2_ref), channel_id=1, source_target_pairs={{16,80},{48,112},{80,144},{112,176},{144,208},{176,240},{208,272},... | collective-permute-start | bytes 393224 | tf_op jit(solution)/shard_map/ppermute | solution.py:21
  26.2 4.9 %collective-permute-start.3 = (bf16[256,256]{1,0:T(8,128)(2,1)S(1)}, bf16[256,256]{1,0:T(8,128)(2,1)S(1)}, u32[]{:S(2)}, u32[]{:S(2)}) collective-permute-start(bf16[256,256]{1,0:T(8,128)(2,1)S(1)} %collective-permute-done.2.kv2_ref), channel_id=1, source_target_pairs={{0,32},{16,48},{32,64},{48,80},{64,96},{80,112},{96,128},{112,144}... | collective-permute-start | bytes 393224 | tf_op jit(solution)/shard_map/ppermute | solution.py:21
  31.1 0.0 collective-permute-done.1.kv1_ref
  31.1 0.0 collective-permute-done.par_ref
  31.1 0.0 copy-done.4
  31.1 3.0 %shard_map.95 = (s32[8,256]{1,0:T(8,128)S(1)}, f32[16,256]{1,0:T(8,128)S(1)}, f32[16,256]{1,0:T(8,128)S(1)}) custom-call(s32[51]{0:T(128)S(1)} %copy-done.4, bf16[272,2048]{1,0:T(8,128)(2,1)S(1)} %get-tuple-element.16.own_ref, bf16[272,2048]{1,0:T(8,128)(2,1)S(1)} %collective-permute-done.par_ref, ...), custom_call_target="tpu_custom_call" | custom-call | flops 805306368 | bytes 2662604 | tf_op jit(solution)/shard_map/pallas_call | solution.py:208
  34.1 0.0 collective-permute-done.4.kv4_ref
  34.1 2.6 %collective-permute-done.3.kv3_ref = bf16[256,256]{1,0:T(8,128)(2,1)S(1)} collective-permute-done((bf16[256,256]{1,0:T(8,128)(2,1)S(1)}, bf16[256,256]{1,0:T(8,128)(2,1)S(1)}, u32[]{:S(2)}, u32[]{:S(2)}) %collective-permute-start.3) | collective-permute-done | bytes 131104 | tf_op jit(solution)/shard_map/ppermute | solution.py:21
  36.7 0.5 shard_map.96.mine_ref
  37.2 1.9 %collective-permute-start.5 = (f32[24,256]{1,0:T(8,128)S(1)}, f32[24,256]{1,0:T(8,128)S(1)}, u32[]{:S(2)}, u32[]{:S(2)}) collective-permute-start(f32[24,256]{1,0:T(8,128)S(1)} %shard_map.96.mine_ref), channel_id=1, source_target_pairs={{0,16},{16,0},{32,48},{48,32},{64,80},{80,64},{96,112},{112,96},{1... | collective-permute-start | bytes 73736 | tf_op jit(solution)/shard_map/ppermute | solution.py:26
  39.1 1.2 %collective-permute-done.5.other_ref = f32[24,256]{1,0:T(8,128)S(1)} collective-permute-done((f32[24,256]{1,0:T(8,128)S(1)}, f32[24,256]{1,0:T(8,128)S(1)}, u32[]{:S(2)}, u32[]{:S(2)}) %collective-permute-start.5) | collective-permute-done | bytes 24608 | tf_op jit(solution)/shard_map/ppermute | solution.py:26
  40.3 0.6 shard_map.97
  40.9 3.1 %collective-permute-start.8 = (bf16[256,256]{1,0:T(8,128)(2,1)S(1)}, bf16[256,256]{1,0:T(8,128)(2,1)S(1)}, u32[]{:S(2)}, u32[]{:S(2)}) collective-permute-start(bf16[256,256]{1,0:T(8,128)(2,1)S(1)} %get-tuple-element.27), channel_id=1, source_target_pairs={{0,480},{16,496},{32,0},{48,16},{64,32},{80,48},{96,64},{112,80},{... | collective-permute-start | bytes 393224 | tf_op jit(solution)/shard_map/ppermute | solution.py:21
  44.0 15.3 %collective-permute-start.9 = (bf16[256,256]{1,0:T(8,128)(2,1)S(1)}, bf16[256,256]{1,0:T(8,128)(2,1)S(1)}, u32[]{:S(2)}, u32[]{:S(2)}) collective-permute-start(bf16[256,256]{1,0:T(8,128)(2,1)S(1)} %get-tuple-element.28), channel_id=1, source_target_pairs={{16,464},{48,496},{80,16},{112,48},{144,80},{176,112},{208,144},{2... | collective-permute-start | bytes 393224 | tf_op jit(solution)/shard_map/ppermute | solution.py:21
  59.3 3.9 %shard_map.98 = (f32[256,256]{1,0:T(8,128)S(1)}, bf16[256,256]{1,0:T(8,128)(2,1)S(1)}, f32[256,256]{1,0:T(8,128)S(1)}, f32[256,1024]{1,0:T(8,128)S(1)}, bf16[256,1024]{1,0:T(8,128)(2,1)S(1)}) custom-call(bf16[272,2048]{1,0:T(8,128)(2,1)S(1)} %get-tuple-element.16.own_ref, bf16[272,2048]{1,0:T(8,128)(2,1)S(1)} %collective-permute-done.par_ref, ...), custom_call_target="tpu_custom_call" | custom-call | flops 4026531840 | bytes 7004160 | tf_op jit(solution)/shard_map/pallas_call | solution.py:208
  63.2 2.2 %collective-permute-start.7 = (bf16[256,256]{1,0:T(8,128)(2,1)S(1)}, bf16[256,256]{1,0:T(8,128)(2,1)S(1)}, u32[]{:S(2)}, u32[]{:S(2)}) collective-permute-start(bf16[256,256]{1,0:T(8,128)(2,1)S(1)} %get-tuple-element.25), channel_id=1, source_target_pairs={{0,480},{16,496},{32,0},{48,16},{64,32},{80,48},{96,64},{112,80},{... | collective-permute-start | bytes 393224 | tf_op jit(solution)/shard_map/ppermute | solution.py:21
  65.4 0.0 collective-permute-done.8
  65.4 0.0 collective-permute-done.9
  65.5 12.1 %collective-permute-start.10 = (bf16[256,256]{1,0:T(8,128)(2,1)S(1)}, bf16[256,256]{1,0:T(8,128)(2,1)S(1)}, u32[]{:S(2)}, u32[]{:S(2)}) collective-permute-start(bf16[256,256]{1,0:T(8,128)(2,1)S(1)} %add_convert_fusion.2), channel_id=1, source_target_pairs={{0,448},{16,464},{32,480},{48,496},{64,0},{80,16},{96,32},{112,48}... | collective-permute-start | bytes 393224 | tf_op jit(solution)/shard_map/ppermute | solution.py:21
  77.6 3.8 %collective-permute-start.6 = (bf16[256,1024]{1,0:T(8,128)(2,1)S(1)}, bf16[256,1024]{1,0:T(8,128)(2,1)S(1)}, u32[]{:S(2)}, u32[]{:S(2)}) collective-permute-start(bf16[256,1024]{1,0:T(8,128)(2,1)S(1)} %get-tuple-element.23), channel_id=1, source_target_pairs={{0,16},{16,0},{32,48},{48,32},{64,80},{80,64},{96,112},{112,96},{1... | collective-permute-start | bytes 1572872 | tf_op jit(solution)/shard_map/ppermute | solution.py:26
  81.3 0.0 collective-permute-done.7
  81.4 0.0 collective-permute-done.10
  81.4 0.7 fusion
  82.1 0.8 collective-permute-done.6
  82.9 1.0 %add_convert_fusion = bf16[256,1024]{1,0:T(8,128)(2,1)} fusion(f32[256,1024]{1,0:T(8,128)S(1)} %get-tuple-element.22, bf16[256,1024]{1,0:T(8,128)(2,1)S(1)} %collective-permute-done.6), kind=kLoop, calls=%fused_computation | loop fusion | flops 786432 | bytes 2097152 | tf_op jit(solution)/shard_map/convert_element_type | solution.py:266
  (4 shorter events, 0.1 us)
Async XLA Ops:
  0.6 1.0 %copy-start = (bf16[256,1024]{1,0:T(8,128)(2,1)S(1)}, bf16[256,1024]{1,0:T(8,128)(2,1)}, u32[]{:S(2)}) copy-start(bf16[256,1024]{1,0:T(8,128)(2,1)} %q_ref.1) | copy-start | bytes 1572868
  1.7 1.0 %copy-start.1 = (bf16[256,1024]{1,0:T(8,128)(2,1)S(1)}, bf16[256,1024]{1,0:T(8,128)(2,1)}, u32[]{:S(2)}) copy-start(bf16[256,1024]{1,0:T(8,128)(2,1)} %g_ref.1) | copy-start | bytes 1572868
  2.7 1.0 %copy-start.2 = (bf16[256,1024]{1,0:T(8,128)(2,1)S(1)}, bf16[256,1024]{1,0:T(8,128)(2,1)}, u32[]{:S(2)}) copy-start(bf16[256,1024]{1,0:T(8,128)(2,1)} %o_ref.1) | copy-start | bytes 1572868
  3.8 0.7 copy-start.3
  4.4 9.2 %copy-start.5 = (bf16[256,128]{1,0:T(8,128)(2,1)S(1)}, bf16[256,128]{1,0:T(8,128)(2,1)}, u32[]{:S(2)}) copy-start(bf16[256,128]{1,0:T(8,128)(2,1)} %param.8) | copy-start | bytes 196612
  4.4 9.2 %copy-start.6 = (bf16[256,128]{1,0:T(8,128)(2,1)S(1)}, bf16[256,128]{1,0:T(8,128)(2,1)}, u32[]{:S(2)}) copy-start(bf16[256,128]{1,0:T(8,128)(2,1)} %param.9) | copy-start | bytes 196612
  4.4 26.7 %copy-start.4 = (s32[51]{0:T(128)S(1)}, s32[51]{0:T(128)}, u32[]{:S(2)}) copy-start(s32[51]{0:T(128)} %doc_ref.1) | copy-start | bytes 616
  4.8 26.3 %collective-permute-start = (bf16[272,2048]{1,0:T(8,128)(2,1)S(1)}, bf16[272,2048]{1,0:T(8,128)(2,1)S(1)}, u32[]{:S(2)}, u32[]{:S(2)}) collective-permute-start(bf16[272,2048]{1,0:T(8,128)(2,1)S(1)} %get-tuple-element.16.own_ref), channel_id=1, source_target_pairs={{0,16},{16,0},{32,48},{48,32},{64,80},{80,64},{96,112},{112,96},{1... | collective-permute-start | bytes 3342344 | tf_op jit(solution)/shard_map/ppermute | solution.py:26
  13.6 10.6 %collective-permute-start.2 = (bf16[256,256]{1,0:T(8,128)(2,1)S(1)}, bf16[256,256]{1,0:T(8,128)(2,1)S(1)}, u32[]{:S(2)}, u32[]{:S(2)}) collective-permute-start(bf16[256,256]{1,0:T(8,128)(2,1)S(1)} %constant_dynamic-update-slice_fusion.kv0_ref), channel_id=1, source_target_pairs={{0,64},{16,80},{32,96},{48,112},{64,128},{80,144},{96,160},{112,17... | collective-permute-start | bytes 393224 | tf_op jit(solution)/shard_map/ppermute | solution.py:21
  15.6 15.5 %collective-permute-start.1 = (bf16[256,256]{1,0:T(8,128)(2,1)S(1)}, bf16[256,256]{1,0:T(8,128)(2,1)S(1)}, u32[]{:S(2)}, u32[]{:S(2)}) collective-permute-start(bf16[256,256]{1,0:T(8,128)(2,1)S(1)} %constant_dynamic-update-slice_fusion.kv0_ref), channel_id=1, source_target_pairs={{0,32},{16,48},{32,64},{48,80},{64,96},{80,112},{96,128},{112,144}... | collective-permute-start | bytes 393224 | tf_op jit(solution)/shard_map/ppermute | solution.py:21
  24.3 9.8 %collective-permute-start.4 = (bf16[256,256]{1,0:T(8,128)(2,1)S(1)}, bf16[256,256]{1,0:T(8,128)(2,1)S(1)}, u32[]{:S(2)}, u32[]{:S(2)}) collective-permute-start(bf16[256,256]{1,0:T(8,128)(2,1)S(1)} %collective-permute-done.2.kv2_ref), channel_id=1, source_target_pairs={{16,80},{48,112},{80,144},{112,176},{144,208},{176,240},{208,272},... | collective-permute-start | bytes 393224 | tf_op jit(solution)/shard_map/ppermute | solution.py:21
  26.2 10.5 %collective-permute-start.3 = (bf16[256,256]{1,0:T(8,128)(2,1)S(1)}, bf16[256,256]{1,0:T(8,128)(2,1)S(1)}, u32[]{:S(2)}, u32[]{:S(2)}) collective-permute-start(bf16[256,256]{1,0:T(8,128)(2,1)S(1)} %collective-permute-done.2.kv2_ref), channel_id=1, source_target_pairs={{0,32},{16,48},{32,64},{48,80},{64,96},{80,112},{96,128},{112,144}... | collective-permute-start | bytes 393224 | tf_op jit(solution)/shard_map/ppermute | solution.py:21
  37.2 3.1 %collective-permute-start.5 = (f32[24,256]{1,0:T(8,128)S(1)}, f32[24,256]{1,0:T(8,128)S(1)}, u32[]{:S(2)}, u32[]{:S(2)}) collective-permute-start(f32[24,256]{1,0:T(8,128)S(1)} %shard_map.96.mine_ref), channel_id=1, source_target_pairs={{0,16},{16,0},{32,48},{48,32},{64,80},{80,64},{96,112},{112,96},{1... | collective-permute-start | bytes 73736 | tf_op jit(solution)/shard_map/ppermute | solution.py:26
  40.9 24.5 %collective-permute-start.8 = (bf16[256,256]{1,0:T(8,128)(2,1)S(1)}, bf16[256,256]{1,0:T(8,128)(2,1)S(1)}, u32[]{:S(2)}, u32[]{:S(2)}) collective-permute-start(bf16[256,256]{1,0:T(8,128)(2,1)S(1)} %get-tuple-element.27), channel_id=1, source_target_pairs={{0,480},{16,496},{32,0},{48,16},{64,32},{80,48},{96,64},{112,80},{... | collective-permute-start | bytes 393224 | tf_op jit(solution)/shard_map/ppermute | solution.py:21
  44.0 21.4 %collective-permute-start.9 = (bf16[256,256]{1,0:T(8,128)(2,1)S(1)}, bf16[256,256]{1,0:T(8,128)(2,1)S(1)}, u32[]{:S(2)}, u32[]{:S(2)}) collective-permute-start(bf16[256,256]{1,0:T(8,128)(2,1)S(1)} %get-tuple-element.28), channel_id=1, source_target_pairs={{16,464},{48,496},{80,16},{112,48},{144,80},{176,112},{208,144},{2... | collective-permute-start | bytes 393224 | tf_op jit(solution)/shard_map/ppermute | solution.py:21
  63.2 18.2 %collective-permute-start.7 = (bf16[256,256]{1,0:T(8,128)(2,1)S(1)}, bf16[256,256]{1,0:T(8,128)(2,1)S(1)}, u32[]{:S(2)}, u32[]{:S(2)}) collective-permute-start(bf16[256,256]{1,0:T(8,128)(2,1)S(1)} %get-tuple-element.25), channel_id=1, source_target_pairs={{0,480},{16,496},{32,0},{48,16},{64,32},{80,48},{96,64},{112,80},{... | collective-permute-start | bytes 393224 | tf_op jit(solution)/shard_map/ppermute | solution.py:21
  65.5 15.9 %collective-permute-start.10 = (bf16[256,256]{1,0:T(8,128)(2,1)S(1)}, bf16[256,256]{1,0:T(8,128)(2,1)S(1)}, u32[]{:S(2)}, u32[]{:S(2)}) collective-permute-start(bf16[256,256]{1,0:T(8,128)(2,1)S(1)} %add_convert_fusion.2), channel_id=1, source_target_pairs={{0,448},{16,464},{32,480},{48,496},{64,0},{80,16},{96,32},{112,48}... | collective-permute-start | bytes 393224 | tf_op jit(solution)/shard_map/ppermute | solution.py:21
  77.6 5.3 %collective-permute-start.6 = (bf16[256,1024]{1,0:T(8,128)(2,1)S(1)}, bf16[256,1024]{1,0:T(8,128)(2,1)S(1)}, u32[]{:S(2)}, u32[]{:S(2)}) collective-permute-start(bf16[256,1024]{1,0:T(8,128)(2,1)S(1)} %get-tuple-element.23), channel_id=1, source_target_pairs={{0,16},{16,0},{32,48},{48,32},{64,80},{80,64},{96,112},{112,96},{1... | collective-permute-start | bytes 1572872 | tf_op jit(solution)/shard_map/ppermute | solution.py:26

commit v2 on v1

v2 whole, which is shorter than its diff:
```python
import jax
import jax.numpy as jnp
from jax import lax
from jax.experimental import pallas as pl
from jax.experimental.pallas import tpu as pltpu
from jax.sharding import PartitionSpec as P

HD = 128
FACTOR = HD ** (-0.5)
SCORE_SCALE = FACTOR * 1.4426950408889634
MASKED = -1e30
EMPTY = -1e20
VMEM_BYTES = 32 * 1024 * 1024


def shift(array, by, parity=None):
    n = lax.axis_size("cp")
    pairs = [(i, (i + by) % n) for i in range(n) if parity is None or i % 2 == parity]
    return lax.ppermute(array, "cp", pairs)


def exchange(array):
    n = lax.axis_size("cp")
    return lax.ppermute(array, "cp", [(i, i ^ 1) for i in range(n)])


def nt_dot(a, b):
    return lax.dot_general(a, b, (((1,), (1,)), ((), ())), preferred_element_type=jnp.float32)


def nn_dot(a, b):
    return lax.dot_general(a, b, (((1,), (0,)), ((), ())), preferred_element_type=jnp.float32)


def side_block(side):
    block = lax.axis_index("cp")
    if side == 0:
        return block
    return block + 1 - 2 * lax.rem(block, 2)


def side_refs(ref):
    core = lax.rem(lax.axis_index("cp"), 2)
    return ref.at[core], ref.at[1 - core]


def listed_pair(off_ref, side, slot):
    key_block = lax.axis_index("cp") - 2 * slot
    block = side_block(side)
    hits = jnp.max((off_ref[lax.rem(block, 2)] == block - key_block).astype(jnp.float32))
    return (hits > 0.0) & (block >= key_block) & (key_block >= 0)


def write_bias(bias_ref, start_ref, side, slot):
    rows = bias_ref.shape[0]
    key_pos = (lax.axis_index("cp") - 2 * slot) * rows + lax.broadcasted_iota(jnp.int32, bias_ref.shape, 0)
    q_pos = side_block(side) * rows + lax.broadcasted_iota(jnp.int32, bias_ref.shape, 1)
    allowed = (key_pos >= start_ref[side : side + 1, :]) & (key_pos <= q_pos)
    bias_ref[...] = jnp.where(allowed, 0.0, MASKED)


def prep_kernel(doc_ref, gs_ref, o_ref, start_ref, delta_ref):
    g_ref = side_refs(gs_ref)[0]
    rows, width = o_ref.shape
    lanes = lax.broadcasted_iota(jnp.int32, (1, rows), 1)
    positions = [side_block(side) * rows + lanes for side in range(2)]

    def step(doc, carry):
        end, first, second = carry
        end = end + doc_ref[doc]
        return (end, jnp.where(end <= positions[0], end, first), jnp.where(end <= positions[1], end, second))

    zero = jnp.zeros((1, rows), jnp.int32)
    _, first, second = lax.fori_loop(0, doc_ref.shape[0], step, (jnp.int32(0), zero, zero))
    start_ref[...] = jnp.zeros_like(start_ref)
    start_ref[0:1, :] = first
    start_ref[1:2, :] = second
    for head in range(width // HD):
        cols = slice(head * HD, (head + 1) * HD)
        product = g_ref[:, cols].astype(jnp.float32) * o_ref[:, cols].astype(jnp.float32)
        delta_ref[head : head + 1, :] = jnp.sum(product.T, axis=0, keepdims=True)


def stats_slots(first, kv_ref, q_refs, off_ref, start_ref, m_ref, l_ref, bias_ref):
    rows = bias_ref.shape[0]
    heads = m_ref.shape[0] // 2
    for side, q_ref in enumerate(q_refs):

        def step(i, carry, side=side, q_ref=q_ref):
            @pl.when(listed_pair(off_ref, side, first + i))
            def _():
                write_bias(bias_ref, start_ref, side, first + i)
                keys = kv_ref[i, 0]

                def products(head):
                    return nt_dot(keys, q_ref[:, head * HD : (head + 1) * HD])

                ahead = products(0)
                for head in range(heads):
                    scores = ahead * SCORE_SCALE + bias_ref[...]
                    if head + 1 < heads:
                        ahead = products(head + 1)
                    row = slice(side * heads + head, side * heads + head + 1)
                    old_max = m_ref[row, :]
                    new_max = jnp.maximum(old_max, jnp.max(scores, axis=0, keepdims=True))
                    total = jnp.sum(jnp.exp2(scores - new_max), axis=0, keepdims=True)
                    l_ref[row, :] = l_ref[row, :] * jnp.exp2(old_max - new_max) + total
                    m_ref[row, :] = new_max

            return carry

        lax.fori_loop(0, kv_ref.shape[0], step, 0)


def stats_near_kernel(qs_ref, off_ref, start_ref, kv0_ref, kv1_ref, kv2_ref, m_ref, l_ref, bias_ref, kv_ref):
    m_ref[...] = jnp.full_like(m_ref, EMPTY)
    l_ref[...] = jnp.zeros_like(l_ref)
    for i, ref in enumerate((kv0_ref, kv1_ref, kv2_ref)):
        kv_ref[i] = ref[...]
    stats_slots(0, kv_ref, side_refs(qs_ref), off_ref, start_ref, m_ref, l_ref, bias_ref)


def stats_far_kernel(qs_ref, off_ref, start_ref, m_in, l_in, delta_ref, kv3_ref, kv4_ref, out_ref,
                     m_ref, l_ref, bias_ref, kv_ref):
    m_ref[...] = m_in[...]
    l_ref[...] = l_in[...]
    kv_ref[0] = kv3_ref[...]
    kv_ref[1] = kv4_ref[...]
    stats_slots(3, kv_ref, side_refs(qs_ref), off_ref, start_ref, m_ref, l_ref, bias_ref)
    stat_rows = m_ref.shape[0]
    total = l_ref[...]
    some = total > 0.0
    out_ref[0:stat_rows, :] = jnp.where(some, m_ref[...] + jnp.log2(jnp.where(some, total, 1.0)), EMPTY)
    out_ref[stat_rows:, :] = delta_ref[...]


def combine_stats(stats_ref, lse_ref, delta_ref):
    heads = delta_ref.shape[0] // 2
    core = lax.rem(lax.axis_index("cp"), 2)
    mine, other = stats_ref[core], stats_ref[1 - core]
    for side in range(2):
        a = mine[side * heads : (side + 1) * heads]
        b = other[(1 - side) * heads : (2 - side) * heads]
        top = jnp.maximum(a, b)
        lse_ref[side * heads : (side + 1) * heads, :] = top + jnp.log2(jnp.exp2(a - top) + jnp.exp2(b - top))
    delta_ref[0:heads, :] = mine[2 * heads :]
    delta_ref[heads:, :] = other[2 * heads :]


def grad_slots(first, kv_ref, q_refs, g_refs, off_ref, start_ref, lse_ref, delta_ref, dq_ref, bias_ref, part_ref):
    rows = bias_ref.shape[0]
    heads = lse_ref.shape[0] // 2
    part_ref[...] = jnp.zeros_like(part_ref)
    for side, (q_ref, g_ref) in enumerate(zip(q_refs, g_refs)):

        def step(i, carry, side=side, q_ref=q_ref, g_ref=g_ref):
            @pl.when(listed_pair(off_ref, side, first + i))
            def _():
                write_bias(bias_ref, start_ref, side, first + i)
                keys = kv_ref[i, 0]
                values = kv_ref[i, 1]
                keys_t = keys.T

                def q_head(head):
                    return q_ref[:, head * HD : (head + 1) * HD]

                def g_head(head):
                    return g_ref[:, head * HD : (head + 1) * HD]

                def products(head):
                    return nt_dot(keys, q_head(head)), nt_dot(values, g_head(head))

                def weights(head, ahead):
                    row = slice(side * heads + head, side * heads + head + 1)
                    probs = jnp.exp2(ahead[0] * SCORE_SCALE + bias_ref[...] - lse_ref[row, :])
                    d_score = probs * (ahead[1] - delta_ref[row, :])
                    return probs.astype(jnp.bfloat16), d_score.astype(jnp.bfloat16)

                def sums(head, pair, acc):
                    at = (side * heads + head) * HD
                    dq_ref[at : at + HD, :] += nn_dot(keys_t, pair[1])
                    return acc[0] + nn_dot(pair[1], q_head(head)), acc[1] + nn_dot(pair[0], g_head(head))

                acc = (part_ref[i, :, 0:HD], part_ref[i, :, HD:])
                ahead, pair = products(0), None
                for head in range(heads):
                    following = products(head + 1) if head + 1 < heads else None
                    if pair is not None:
                        acc = sums(head - 1, pair, acc)
                    pair, ahead = weights(head, ahead), following
                acc = sums(heads - 1, pair, acc)
                part_ref[i, :, 0:HD] = acc[0]
                part_ref[i, :, HD:] = acc[1]

            return carry

        lax.fori_loop(0, kv_ref.shape[0], step, 0)


def write_piece(out_ref, part):
    out_ref[:, 0:HD] = (part[:, 0:HD] * FACTOR).astype(out_ref.dtype)
    out_ref[:, HD:] = part[:, HD:].astype(out_ref.dtype)


def grad_far_kernel(qs_ref, gs_ref, off_ref, start_ref, stats_ref, kv3_ref, kv4_ref, p3_ref, p4_ref, dq_ref,
                    lse_ref, delta_ref, bias_ref, kv_ref, part_ref):
    combine_stats(stats_ref, lse_ref, delta_ref)
    dq_ref[...] = jnp.zeros_like(dq_ref)
    kv_ref[0] = kv3_ref[...]
    kv_ref[1] = kv4_ref[...]
    grad_slots(3, kv_ref, side_refs(qs_ref), side_refs(gs_ref), off_ref, start_ref, lse_ref, delta_ref, dq_ref, bias_ref, part_ref)
    write_piece(p3_ref, part_ref[0])
    write_piece(p4_ref, part_ref[1])


def grad_mid_kernel(qs_ref, gs_ref, off_ref, start_ref, stats_ref, kv1_ref, kv2_ref, dq_in, p1_ref, p2_ref, dq_ref,
                    lse_ref, delta_ref, bias_ref, kv_ref, part_ref):
    combine_stats(stats_ref, lse_ref, delta_ref)
    dq_ref[...] = dq_in[...]
    kv_ref[0] = kv1_ref[...]
    kv_ref[1] = kv2_ref[...]
    grad_slots(1, kv_ref, side_refs(qs_ref), side_refs(gs_ref), off_ref, start_ref, lse_ref, delta_ref, dq_ref, bias_ref, part_ref)
    write_piece(p1_ref, part_ref[0])
    write_piece(p2_ref, part_ref[1])


def grad_own_kernel(qs_ref, gs_ref, off_ref, start_ref, stats_ref, kv0_ref, dq_in, p0_ref, dq_own_ref, dq_par_ref,
                    lse_ref, delta_ref, bias_ref, kv_ref, part_ref, dq_ref):
    combine_stats(stats_ref, lse_ref, delta_ref)
    dq_ref[...] = dq_in[...]
    kv_ref[0] = kv0_ref[...]
    grad_slots(0, kv_ref, side_refs(qs_ref), side_refs(gs_ref), off_ref, start_ref, lse_ref, delta_ref, dq_ref, bias_ref, part_ref)
    write_piece(p0_ref, part_ref[0])
    heads = lse_ref.shape[0] // 2
    for side, out_ref in ((0, dq_own_ref), (1, dq_par_ref)):
        for head in range(heads):
            at = (side * heads + head) * HD
            block = dq_ref[at : at + HD, :] * FACTOR
            out_ref[:, head * HD : (head + 1) * HD] = block.T.astype(out_ref.dtype)


def call(kernel, in_spaces, outs, scratch, flops, transcendentals, *args):
    moved = sum(a.size * a.dtype.itemsize for a in args) + sum(o.size * o.dtype.itemsize for o in outs)
    return pl.pallas_call(
        kernel,
        out_shape=outs,
        in_specs=[pl.BlockSpec(memory_space=space) for space in in_spaces],
        out_specs=[pl.BlockSpec(memory_space=pltpu.VMEM) for _ in outs],
        scratch_shapes=scratch,
        compiler_params=pltpu.CompilerParams(vmem_limit_bytes=VMEM_BYTES),
        cost_estimate=pl.CostEstimate(flops=flops, bytes_accessed=moved, transcendentals=transcendentals),
    )(*args)


def on_device(queries, keys, values, outputs, out_grad, doc_lengths, block_offsets):
    rows, width = queries.shape
    heads = width // HD
    struct = jax.ShapeDtypeStruct
    f32, bf16 = jnp.float32, jnp.bfloat16
    vmem, smem = pltpu.VMEM, pltpu.SMEM
    pair = 2 * heads * rows * rows

    pairs = [[i, i + 1] for i in range(0, lax.axis_size("cp"), 2)]
    which = lax.broadcasted_iota(jnp.int32, (2, rows, HD), 0)
    kv = jnp.where(which == 0, keys[None], values[None])
    kv2 = shift(kv, 4)
    kv1 = shift(kv, 2)
    offsets = lax.all_gather(block_offsets, "cp", axis_index_groups=pairs)
    qs = lax.all_gather(queries, "cp", axis_index_groups=pairs)
    gs = lax.all_gather(out_grad, "cp", axis_index_groups=pairs)
    kv2, kv1, qs, gs, offsets = lax.optimization_barrier((kv2, kv1, qs, gs, offsets))
    stat = struct((2 * heads, rows), f32)
    stat_scratch = pltpu.VMEM((2 * heads, rows), f32)
    bias = pltpu.VMEM((rows, rows), f32)

    def stack(count):
        return pltpu.VMEM((count, 2, rows, HD), bf16)

    def parts(count):
        return pltpu.VMEM((count, rows, 2 * HD), f32)

    start, delta = call(
        prep_kernel, [smem] + [vmem] * 2, [struct((8, rows), jnp.int32), struct((heads, rows), f32)], [],
        2 * rows * width, 0, doc_lengths, gs, outputs)
    kv3 = shift(kv2, 2)
    kv4 = shift(kv2, 4, 1)
    q_side = (qs, offsets, start)
    m_near, l_near = call(
        stats_near_kernel, [vmem] * 6, [stat, stat], [bias, stack(3)],
        3 * pair * HD * 2, 3 * pair, *q_side, kv, kv1, kv2)
    (mine,) = call(
        stats_far_kernel, [vmem] * 8, [struct((3 * heads, rows), f32)], [stat_scratch, stat_scratch, bias, stack(2)],
        2 * pair * HD * 2, 2 * pair, *q_side, m_near, l_near, delta, kv3, kv4)
    stats = lax.all_gather(mine, "cp", axis_index_groups=pairs)

    scratch = [stat_scratch, stat_scratch, bias]
    piece16, piece32 = struct((rows, 2 * HD), bf16), struct((rows, 2 * HD), f32)
    dq_shape = (2 * width, rows)
    sides = (qs, gs, offsets, start, stats)
    p3, p4, dq = call(
        grad_far_kernel, [vmem] * 7, [piece16, piece16, struct(dq_shape, f32)], scratch + [stack(2), parts(2)],
        2 * 5 * pair * HD * 2, 2 * pair, *sides, kv3, kv4)
    back4 = shift(p4, -4, 1)
    back3 = shift(p3, -2)
    p1, p2, dq = call(
        grad_mid_kernel, [vmem] * 8, [piece16, piece32, struct(dq_shape, f32)], scratch + [stack(2), parts(2)],
        2 * 5 * pair * HD * 2, 2 * pair, *sides, kv1, kv2, dq)
    p2_sum = (p2 + back3.astype(f32) + back4.astype(f32)).astype(bf16)
    back2 = shift(p2_sum, -4)
    back1 = shift(p1, -2)
    p0, dq_own, dq_par = call(
        grad_own_kernel, [vmem] * 7, [piece32, struct((rows, width), f32), struct((rows, width), bf16)],
        scratch + [stack(1), parts(1), pltpu.VMEM(dq_shape, f32)],
        5 * pair * HD * 2, pair, *sides, kv, dq)
    dq_other = exchange(dq_par)
    grad_queries = (dq_own + dq_other.astype(f32)).astype(bf16)
    summed = p0 + back1.astype(f32) + back2.astype(f32)
    return grad_queries, summed[:, :HD].astype(bf16), summed[:, HD:].astype(bf16)


def solution(mesh):
    tokens = P(("dp", "cp"), "hd")
    return jax.shard_map(
        on_device,
        mesh=mesh,
        in_specs=(tokens, tokens, tokens, tokens, tokens, P("dp"), P(("dp", "cp"), None)),
        out_specs=(tokens, tokens, tokens),
        check_vma=False,
    )
```

time: 84.8 us -> 115 us (1.36)
  the two profiles are of different devices: /device:TPU:1 before, /device:TPU:129 now
where the time goes in v2:
time: 115 us
  waiting for transfers between devices  47 us (41%)
  starting transfers between devices  25.5 us (22%)
  Pallas kernels  16.7 us (15%)
  between operations  14.2 us (12%)
  local copies, waits for them, and re-layouts  4.8 us (4%)
  blocking collectives  4.68 us (4%)
  other arithmetic  2.01 us (2%)
    ppermute x8, starting transfers between devices, shift(): return lax.ppermute(array, 'cp', pairs)  23.5 us
    all_gather x1, waiting for transfers between devices, on_device(): gs = lax.all_gather(out_grad, 'cp', axis_index_groups=pairs)  22.9 us
    pallas_call x6, Pallas kernels, call(): pl.pallas_call(kernel, out_shape=outs, in_specs=[pl.BlockSpec(memory_spac...  16.7 us
    all_gather x1, waiting for transfers between devices, on_device(): qs = lax.all_gather(queries, 'cp', axis_index_groups=pairs)  11.6 us
    ppermute x8, waiting for transfers between devices, shift(): return lax.ppermute(array, 'cp', pairs)  11 us
    unnamed x12, local copies, waits for them, and re-layouts  4.14 us
    all_gather x1, blocking collectives, on_device(): offsets = lax.all_gather(block_offsets, 'cp', axis_index_groups=pairs)  2.84 us
  transfers between devices with their start and end apart: 11, of which 7 were waited for; matrix products, arithmetic and copies ran while one was open for 1% of the time, Pallas kernels for 13%

profile of v2, /device:TPU:129, one launch (start us, length us, event | category | flops | bytes accessed | tf_op | source)
XLA Modules:
  0.0 114.8 jit_solution(15868493522897967289)
XLA Ops:
  7.2 0.0 all-gather.8.cloned.1.call-start
  7.2 0.7 all-gather.8.cloned.1.call-update
  7.9 0.0 all-gather.10.cloned.1.call-start
  7.9 0.7 all-gather.10.cloned.1.call-update
  8.7 1.0 broadcast_select_fusion.kv0_ref
  9.6 3.5 %collective-permute-start.1 = (bf16[2,256,128]{2,1,0:T(8,128)(2,1)S(1)}, bf16[2,256,128]{2,1,0:T(8,128)(2,1)S(1)}, u32[]{:S(2)}, u32[]{:S(2)}) collective-permute-start(bf16[2,256,128]{2,1,0:T(8,128)(2,1)S(1)} %broadcast_select_fusion.kv0_ref), channel_id=1, source_target_pairs={{0,32},{16,48},{32,64},{48,80},{64,96},{80,112},{96,128},{112,144}... | collective-permute-start | bytes 393224 | tf_op jit(solution)/shard_map/ppermute | solution.py:19
  13.2 4.9 %collective-permute-start = (bf16[2,256,128]{2,1,0:T(8,128)(2,1)S(1)}, bf16[2,256,128]{2,1,0:T(8,128)(2,1)S(1)}, u32[]{:S(2)}, u32[]{:S(2)}) collective-permute-start(bf16[2,256,128]{2,1,0:T(8,128)(2,1)S(1)} %broadcast_select_fusion.kv0_ref), channel_id=1, source_target_pairs={{0,64},{16,80},{32,96},{48,112},{64,128},{80,144},{96,160},{112,17... | collective-permute-start | bytes 393224 | tf_op jit(solution)/shard_map/ppermute | solution.py:19
  18.1 2.8 %all-gather.4.off_ref = s32[2,1,16]{2,1,0:T(1,128)S(1)} all-gather(s32[1,1,16]{2,1,0:T(1,128)} %bitcast.16), channel_id=4, replica_groups={{0,16},{32,48},{64,80},{96,112},{128,144},{160,176},{192,208},{224,240}..., dimensions={0}, use_global_device_ids=true | all-gather | bytes 192 | tf_op jit(solution)/shard_map/all_gather | solution.py:268
  20.9 0.0 collective-permute-done.1.kv1_ref
  20.9 0.6 collective-permute-done.kv2_ref
  21.5 11.6 %all-gather.8.cloned.1.call-done = bf16[512,1024]{1,0:T(8,128)(2,1)} async-done(((bf16[256,1024]{1,0:T(8,128)(2,1)}), bf16[512,1024]{1,0:T(8,128)(2,1)}) %all-gather.8.cloned.1.call-update) | async-done | bytes 1048592 | tf_op jit(solution)/shard_map/all_gather | solution.py:269
  33.1 22.9 %all-gather.10.cloned.1.call-done = bf16[512,1024]{1,0:T(8,128)(2,1)} async-done(((bf16[256,1024]{1,0:T(8,128)(2,1)}), bf16[512,1024]{1,0:T(8,128)(2,1)}) %all-gather.10.cloned.1.call-update) | async-done | bytes 1048592 | tf_op jit(solution)/shard_map/all_gather | solution.py:270
  56.1 4.2 %collective-permute-start.3 = (bf16[2,256,128]{2,1,0:T(8,128)(2,1)S(1)}, bf16[2,256,128]{2,1,0:T(8,128)(2,1)S(1)}, u32[]{:S(2)}, u32[]{:S(2)}) collective-permute-start(bf16[2,256,128]{2,1,0:T(8,128)(2,1)S(1)} %collective-permute-done.kv2_ref), channel_id=1, source_target_pairs={{16,80},{48,112},{80,144},{112,176},{144,208},{176,240},{208,272},... | collective-permute-start | bytes 393224 | tf_op jit(solution)/shard_map/ppermute | solution.py:19
  60.2 3.2 %collective-permute-start.2 = (bf16[2,256,128]{2,1,0:T(8,128)(2,1)S(1)}, bf16[2,256,128]{2,1,0:T(8,128)(2,1)S(1)}, u32[]{:S(2)}, u32[]{:S(2)}) collective-permute-start(bf16[2,256,128]{2,1,0:T(8,128)(2,1)S(1)} %collective-permute-done.kv2_ref), channel_id=1, source_target_pairs={{0,32},{16,48},{32,64},{48,80},{64,96},{80,112},{96,128},{112,144}... | collective-permute-start | bytes 393224 | tf_op jit(solution)/shard_map/ppermute | solution.py:19
  63.4 0.0 copy-start
  63.4 1.2 %copy-done = bf16[512,1024]{1,0:T(8,128)(2,1)S(1)} copy-done((bf16[512,1024]{1,0:T(8,128)(2,1)S(1)}, bf16[512,1024]{1,0:T(8,128)(2,1)}, u32[]{:S(2)}) %copy-start) | copy-done | bytes 1048600
  64.6 0.0 copy-start.2
  64.6 1.0 copy-done.2
  65.7 0.0 copy-start.3
  65.7 0.7 copy-done.3
  66.3 1.3 %shard_map.94 = (s32[8,256]{1,0:T(8,128)S(1)}, f32[8,256]{1,0:T(8,128)S(1)}) custom-call(s32[51]{0:T(128)S(1)} %copy-done.3, bf16[2,256,1024]{2,1,0:T(8,128)(2,1)S(1)} %bitcast.4, bf16[256,1024]{1,0:T(8,128)(2,1)S(1)} %copy-done.2), custom_call_target="tpu_custom_call" | custom-call | flops 524288 | bytes 1589452 | tf_op jit(solution)/shard_map/pallas_call | solution.py:244
  67.6 0.0 copy-start.4
  67.6 1.2 %copy-done.4 = bf16[512,1024]{1,0:T(8,128)(2,1)S(1)} copy-done((bf16[512,1024]{1,0:T(8,128)(2,1)S(1)}, bf16[512,1024]{1,0:T(8,128)(2,1)}, u32[]{:S(2)}) %copy-start.4) | copy-done | bytes 1048600
  68.8 0.0 copy-start.5
  68.8 4.6 %shard_map.95 = (f32[16,256]{1,0:T(8,128)S(1)}, f32[16,256]{1,0:T(8,128)S(1)}) custom-call(bf16[2,256,1024]{2,1,0:T(8,128)(2,1)S(1)} %bitcast.11, s32[2,1,16]{2,1,0:T(1,128)S(1)} %all-gather.4.off_ref, s32[8,256]{1,0:T(8,128)S(1)} %get-tuple-element.24.start_ref, bf16[2,256,128]{2,1,0:T(8,128)(2,1)S(1)} %broadcast_select_fusion.kv0_ref, ...), custom_call_target="tpu_custom_call" | custom-call | flops 805306368 | bytes 1482880 | tf_op jit(solution)/shard_map/pallas_call | solution.py:244
  73.4 0.0 copy-start.1
  73.4 0.0 collective-permute-done.3.kv4_ref
  73.4 0.0 collective-permute-done.2.kv3_ref
  73.4 0.0 copy-done.5
  73.4 0.6 shard_map.96
  74.0 1.8 %all-gather.3 = f32[48,256]{1,0:T(8,128)S(1)} all-gather(f32[24,256]{1,0:T(8,128)S(1)} %shard_map.96), channel_id=5, replica_groups={{0,16},{32,48},{64,80},{96,112},{128,144},{160,176},{192,208},{224,240}..., dimensions={0}, use_global_device_ids=true | all-gather | bytes 73728 | tf_op jit(solution)/shard_map/all_gather | solution.py:294
  75.8 0.0 copy-done.1
  75.8 0.8 shard_map.97
  76.6 1.9 %collective-permute-start.6 = (bf16[256,256]{1,0:T(8,128)(2,1)S(1)}, bf16[256,256]{1,0:T(8,128)(2,1)S(1)}, u32[]{:S(2)}, u32[]{:S(2)}) collective-permute-start(bf16[256,256]{1,0:T(8,128)(2,1)S(1)} %get-tuple-element.37), channel_id=1, source_target_pairs={{0,480},{16,496},{32,0},{48,16},{64,32},{80,48},{96,64},{112,80},{... | collective-permute-start | bytes 393224 | tf_op jit(solution)/shard_map/ppermute | solution.py:19
  78.5 1.9 %collective-permute-start.7 = (bf16[256,256]{1,0:T(8,128)(2,1)S(1)}, bf16[256,256]{1,0:T(8,128)(2,1)S(1)}, u32[]{:S(2)}, u32[]{:S(2)}) collective-permute-start(bf16[256,256]{1,0:T(8,128)(2,1)S(1)} %get-tuple-element.38), channel_id=1, source_target_pairs={{16,464},{48,496},{80,16},{112,48},{144,80},{176,112},{208,144},{2... | collective-permute-start | bytes 393224 | tf_op jit(solution)/shard_map/ppermute | solution.py:19
  80.5 6.9 %shard_map.98 = (bf16[256,256]{1,0:T(8,128)(2,1)S(1)}, f32[256,256]{1,0:T(8,128)S(1)}, f32[2048,256]{1,0:T(8,128)S(1)}) custom-call(bf16[2,256,1024]{2,1,0:T(8,128)(2,1)S(1)} %bitcast.14, bf16[2,256,1024]{2,1,0:T(8,128)(2,1)S(1)} %bitcast.6, s32[2,1,16]{2,1,0:T(1,128)S(1)} %all-gather.4.off_ref, s32[8,256]{1,0:T(8,128)S(1)} %get-tuple-element.24.start_ref, ...), custom_call_target="tpu_custom_call" | custom-call | flops 2684354560 | bytes 7004288 | tf_op jit(solution)/shard_map/pallas_call | solution.py:244
  87.4 1.9 %collective-permute-start.5 = (bf16[256,256]{1,0:T(8,128)(2,1)S(1)}, bf16[256,256]{1,0:T(8,128)(2,1)S(1)}, u32[]{:S(2)}, u32[]{:S(2)}) collective-permute-start(bf16[256,256]{1,0:T(8,128)(2,1)S(1)} %get-tuple-element.35), channel_id=1, source_target_pairs={{0,480},{16,496},{32,0},{48,16},{64,32},{80,48},{96,64},{112,80},{... | collective-permute-start | bytes 393224 | tf_op jit(solution)/shard_map/ppermute | solution.py:19
  89.3 0.1 collective-permute-done.6
  89.4 3.9 %collective-permute-done.7 = bf16[256,256]{1,0:T(8,128)(2,1)S(1)} collective-permute-done((bf16[256,256]{1,0:T(8,128)(2,1)S(1)}, bf16[256,256]{1,0:T(8,128)(2,1)S(1)}, u32[]{:S(2)}, u32[]{:S(2)}) %collective-permute-start.7) | collective-permute-done | bytes 131104 | tf_op jit(solution)/shard_map/ppermute | solution.py:19
  93.4 1.9 %collective-permute-start.8 = (bf16[256,256]{1,0:T(8,128)(2,1)S(1)}, bf16[256,256]{1,0:T(8,128)(2,1)S(1)}, u32[]{:S(2)}, u32[]{:S(2)}) collective-permute-start(bf16[256,256]{1,0:T(8,128)(2,1)S(1)} %add_convert_fusion.2), channel_id=1, source_target_pairs={{0,448},{16,464},{32,480},{48,496},{64,0},{80,16},{96,32},{112,48}... | collective-permute-start | bytes 393224 | tf_op jit(solution)/shard_map/ppermute | solution.py:19
  95.3 2.6 %shard_map.99 = (f32[256,256]{1,0:T(8,128)S(1)}, f32[256,1024]{1,0:T(8,128)S(1)}, bf16[256,1024]{1,0:T(8,128)(2,1)S(1)}) custom-call(bf16[2,256,1024]{2,1,0:T(8,128)(2,1)S(1)} %bitcast.15, bf16[2,256,1024]{2,1,0:T(8,128)(2,1)S(1)} %bitcast.7, s32[2,1,16]{2,1,0:T(1,128)S(1)} %all-gather.4.off_ref, s32[8,256]{1,0:T(8,128)S(1)} %get-tuple-element.24.start_ref, ...), custom_call_target="tpu_custom_call" | custom-call | flops 1342177280 | bytes 6217856 | tf_op jit(solution)/shard_map/pallas_call | solution.py:244
  97.9 1.9 %collective-permute-start.4 = (bf16[256,1024]{1,0:T(8,128)(2,1)S(1)}, bf16[256,1024]{1,0:T(8,128)(2,1)S(1)}, u32[]{:S(2)}, u32[]{:S(2)}) collective-permute-start(bf16[256,1024]{1,0:T(8,128)(2,1)S(1)} %get-tuple-element.33), channel_id=1, source_target_pairs={{0,16},{16,0},{32,48},{48,32},{64,80},{80,64},{96,112},{112,96},{1... | collective-permute-start | bytes 1572872 | tf_op jit(solution)/shard_map/ppermute | solution.py:24
  99.8 0.2 collective-permute-done.5
  100.0 6.3 %collective-permute-done.8 = bf16[256,256]{1,0:T(8,128)(2,1)S(1)} collective-permute-done((bf16[256,256]{1,0:T(8,128)(2,1)S(1)}, bf16[256,256]{1,0:T(8,128)(2,1)S(1)}, u32[]{:S(2)}, u32[]{:S(2)}) %collective-permute-start.8) | collective-permute-done | bytes 131104 | tf_op jit(solution)/shard_map/ppermute | solution.py:19
  106.3 0.1 add_convert_fusion.1
  106.3 0.7 fusion
  107.0 0.0 collective-permute-done.4
  107.0 1.0 add_convert_fusion
  (2 shorter events, 0.1 us)
Async XLA Ops:
  7.2 25.9 %all-gather.8.cloned.1.call-start = ((), (), s32[]{:S(2)}) async-start(), calls=%async_computation | async-start | bytes 1572864 | tf_op jit(solution)/shard_map/all_gather | solution.py:269
  7.9 48.2 %all-gather.10.cloned.1.call-start = ((), (), s32[]{:S(2)}) async-start(), calls=%async_computation.1 | async-start | bytes 1572864 | tf_op jit(solution)/shard_map/all_gather | solution.py:270
  9.6 11.3 %collective-permute-start.1 = (bf16[2,256,128]{2,1,0:T(8,128)(2,1)S(1)}, bf16[2,256,128]{2,1,0:T(8,128)(2,1)S(1)}, u32[]{:S(2)}, u32[]{:S(2)}) collective-permute-start(bf16[2,256,128]{2,1,0:T(8,128)(2,1)S(1)} %broadcast_select_fusion.kv0_ref), channel_id=1, source_target_pairs={{0,32},{16,48},{32,64},{48,80},{64,96},{80,112},{96,128},{112,144}... | collective-permute-start | bytes 393224 | tf_op jit(solution)/shard_map/ppermute | solution.py:19
  13.2 8.3 %collective-permute-start = (bf16[2,256,128]{2,1,0:T(8,128)(2,1)S(1)}, bf16[2,256,128]{2,1,0:T(8,128)(2,1)S(1)}, u32[]{:S(2)}, u32[]{:S(2)}) collective-permute-start(bf16[2,256,128]{2,1,0:T(8,128)(2,1)S(1)} %broadcast_select_fusion.kv0_ref), channel_id=1, source_target_pairs={{0,64},{16,80},{32,96},{48,112},{64,128},{80,144},{96,160},{112,17... | collective-permute-start | bytes 393224 | tf_op jit(solution)/shard_map/ppermute | solution.py:19
  56.1 17.4 %collective-permute-start.3 = (bf16[2,256,128]{2,1,0:T(8,128)(2,1)S(1)}, bf16[2,256,128]{2,1,0:T(8,128)(2,1)S(1)}, u32[]{:S(2)}, u32[]{:S(2)}) collective-permute-start(bf16[2,256,128]{2,1,0:T(8,128)(2,1)S(1)} %collective-permute-done.kv2_ref), channel_id=1, source_target_pairs={{16,80},{48,112},{80,144},{112,176},{144,208},{176,240},{208,272},... | collective-permute-start | bytes 393224 | tf_op jit(solution)/shard_map/ppermute | solution.py:19
  60.2 13.2 %collective-permute-start.2 = (bf16[2,256,128]{2,1,0:T(8,128)(2,1)S(1)}, bf16[2,256,128]{2,1,0:T(8,128)(2,1)S(1)}, u32[]{:S(2)}, u32[]{:S(2)}) collective-permute-start(bf16[2,256,128]{2,1,0:T(8,128)(2,1)S(1)} %collective-permute-done.kv2_ref), channel_id=1, source_target_pairs={{0,32},{16,48},{32,64},{48,80},{64,96},{80,112},{96,128},{112,144}... | collective-permute-start | bytes 393224 | tf_op jit(solution)/shard_map/ppermute | solution.py:19
  63.4 1.2 %copy-start = (bf16[512,1024]{1,0:T(8,128)(2,1)S(1)}, bf16[512,1024]{1,0:T(8,128)(2,1)}, u32[]{:S(2)}) copy-start(bf16[512,1024]{1,0:T(8,128)(2,1)} %all-gather.10.cloned.1.call-done) | copy-start | bytes 3145732
  64.6 1.0 copy-start.2
  65.7 0.7 copy-start.3
  67.6 1.2 %copy-start.4 = (bf16[512,1024]{1,0:T(8,128)(2,1)S(1)}, bf16[512,1024]{1,0:T(8,128)(2,1)}, u32[]{:S(2)}) copy-start(bf16[512,1024]{1,0:T(8,128)(2,1)} %all-gather.8.cloned.1.call-done) | copy-start | bytes 3145732
  68.8 4.6 %copy-start.5 = (bf16[512,1024]{1,0:T(8,128)(2,1)S(1)}, bf16[512,1024]{1,0:T(8,128)(2,1)}, u32[]{:S(2)}) copy-start(bf16[512,1024]{1,0:T(8,128)(2,1)} %all-gather.8.cloned.1.call-done) | copy-start | bytes 3145732
  73.4 2.4 %copy-start.1 = (bf16[512,1024]{1,0:T(8,128)(2,1)S(1)}, bf16[512,1024]{1,0:T(8,128)(2,1)}, u32[]{:S(2)}) copy-start(bf16[512,1024]{1,0:T(8,128)(2,1)} %all-gather.10.cloned.1.call-done) | copy-start | bytes 3145732
  76.6 12.8 %collective-permute-start.6 = (bf16[256,256]{1,0:T(8,128)(2,1)S(1)}, bf16[256,256]{1,0:T(8,128)(2,1)S(1)}, u32[]{:S(2)}, u32[]{:S(2)}) collective-permute-start(bf16[256,256]{1,0:T(8,128)(2,1)S(1)} %get-tuple-element.37), channel_id=1, source_target_pairs={{0,480},{16,496},{32,0},{48,16},{64,32},{80,48},{96,64},{112,80},{... | collective-permute-start | bytes 393224 | tf_op jit(solution)/shard_map/ppermute | solution.py:19
  78.5 14.8 %collective-permute-start.7 = (bf16[256,256]{1,0:T(8,128)(2,1)S(1)}, bf16[256,256]{1,0:T(8,128)(2,1)S(1)}, u32[]{:S(2)}, u32[]{:S(2)}) collective-permute-start(bf16[256,256]{1,0:T(8,128)(2,1)S(1)} %get-tuple-element.38), channel_id=1, source_target_pairs={{16,464},{48,496},{80,16},{112,48},{144,80},{176,112},{208,144},{2... | collective-permute-start | bytes 393224 | tf_op jit(solution)/shard_map/ppermute | solution.py:19
  87.4 12.6 %collective-permute-start.5 = (bf16[256,256]{1,0:T(8,128)(2,1)S(1)}, bf16[256,256]{1,0:T(8,128)(2,1)S(1)}, u32[]{:S(2)}, u32[]{:S(2)}) collective-permute-start(bf16[256,256]{1,0:T(8,128)(2,1)S(1)} %get-tuple-element.35), channel_id=1, source_target_pairs={{0,480},{16,496},{32,0},{48,16},{64,32},{80,48},{96,64},{112,80},{... | collective-permute-start | bytes 393224 | tf_op jit(solution)/shard_map/ppermute | solution.py:19
  93.4 12.9 %collective-permute-start.8 = (bf16[256,256]{1,0:T(8,128)(2,1)S(1)}, bf16[256,256]{1,0:T(8,128)(2,1)S(1)}, u32[]{:S(2)}, u32[]{:S(2)}) collective-permute-start(bf16[256,256]{1,0:T(8,128)(2,1)S(1)} %add_convert_fusion.2), channel_id=1, source_target_pairs={{0,448},{16,464},{32,480},{48,496},{64,0},{80,16},{96,32},{112,48}... | collective-permute-start | bytes 393224 | tf_op jit(solution)/shard_map/ppermute | solution.py:19
  97.9 9.1 %collective-permute-start.4 = (bf16[256,1024]{1,0:T(8,128)(2,1)S(1)}, bf16[256,1024]{1,0:T(8,128)(2,1)S(1)}, u32[]{:S(2)}, u32[]{:S(2)}) collective-permute-start(bf16[256,1024]{1,0:T(8,128)(2,1)S(1)} %get-tuple-element.33), channel_id=1, source_target_pairs={{0,16},{16,0},{32,48},{48,32},{64,80},{80,64},{96,112},{112,96},{1... | collective-permute-start | bytes 1572872 | tf_op jit(solution)/shard_map/ppermute | solution.py:24
Sparse Core Ops, SparseCore 0:
  10.1 22.9 all-gather.7
  35.2 20.8 all-gather.9

commit v3 on v0

v3 whole, which is shorter than its diff:
```python
import jax
import jax.numpy as jnp
from jax import lax
from jax.experimental import pallas as pl
from jax.experimental.pallas import tpu as pltpu
from jax.sharding import PartitionSpec as P

HD = 128
FACTOR = HD ** (-0.5)
SCORE_SCALE = FACTOR * 1.4426950408889634
MASKED = -1e30
EMPTY = -1e20
VMEM_BYTES = 32 * 1024 * 1024


def shift(array, by, parity=None):
    n = lax.axis_size("cp")
    pairs = [(i, (i + by) % n) for i in range(n) if parity is None or i % 2 == parity]
    return lax.ppermute(array, "cp", pairs)


def gather_pair(array):
    n = lax.axis_size("cp")
    return lax.all_gather(array, "cp", axis_index_groups=[[i, i + 1] for i in range(0, n, 2)])


def nt_dot(a, b):
    return lax.dot_general(a, b, (((1,), (1,)), ((), ())), preferred_element_type=jnp.float32)


def nn_dot(a, b):
    return lax.dot_general(a, b, (((1,), (0,)), ((), ())), preferred_element_type=jnp.float32)


def core_parity():
    return lax.rem(lax.axis_index("cp"), 2)


def key_block(slot, entry):
    return lax.axis_index("cp") - core_parity() + 1 - 2 * slot - entry


def listed(off_ref, slot, entry):
    block = lax.axis_index("cp")
    key = key_block(slot, entry)
    hits = jnp.max((off_ref[...] == block - key).astype(jnp.float32))
    return (hits > 0.0) & (block >= key) & (key >= 0)


def write_bias(bias_ref, start_ref, slot, entry):
    rows = bias_ref.shape[0]
    key_pos = key_block(slot, entry) * rows + lax.broadcasted_iota(jnp.int32, bias_ref.shape, 0)
    q_pos = lax.axis_index("cp") * rows + lax.broadcasted_iota(jnp.int32, bias_ref.shape, 1)
    allowed = (key_pos >= start_ref[0:1, :]) & (key_pos <= q_pos)
    bias_ref[...] = jnp.where(allowed, 0.0, MASKED)


def prep_kernel(doc_ref, g_ref, o_ref, start_ref, delta_ref):
    rows, width = g_ref.shape
    positions = lax.axis_index("cp") * rows + lax.broadcasted_iota(jnp.int32, (8, rows), 1)

    def step(doc, carry):
        end, first = carry
        end = end + doc_ref[doc]
        return (end, jnp.where(end <= positions, end, first))

    _, first = lax.fori_loop(0, doc_ref.shape[0], step, (jnp.int32(0), jnp.zeros((8, rows), jnp.int32)))
    start_ref[...] = first
    for head in range(width // HD):
        cols = slice(head * HD, (head + 1) * HD)
        product = g_ref[:, cols].astype(jnp.float32) * o_ref[:, cols].astype(jnp.float32)
        delta_ref[head : head + 1, :] = jnp.sum(product.T, axis=0, keepdims=True)


def load_entries(kv_ref, gathered):
    for i in range(kv_ref.shape[0]):
        pair = gathered[i // 2]
        kv_ref[i] = pair[1 - i % 2] if len(pair.shape) == 4 else pair[...]


def stats_entries(slot, kv_ref, q_ref, off_ref, start_ref, m_ref, l_ref, bias_ref):
    heads = m_ref.shape[0]

    def step(entry, carry):
        @pl.when(listed(off_ref, slot, entry))
        def _():
            write_bias(bias_ref, start_ref, slot, entry)
            keys = kv_ref[entry, 0]

            def products(head):
                return nt_dot(keys, q_ref[:, head * HD : (head + 1) * HD])

            ahead = products(0)
            for head in range(heads):
                scores = ahead * SCORE_SCALE + bias_ref[...]
                if head + 1 < heads:
                    ahead = products(head + 1)
                row = slice(head, head + 1)
                old_max = m_ref[row, :]
                new_max = jnp.maximum(old_max, jnp.max(scores, axis=0, keepdims=True))
                total = jnp.sum(jnp.exp2(scores - new_max), axis=0, keepdims=True)
                l_ref[row, :] = l_ref[row, :] * jnp.exp2(old_max - new_max) + total
                m_ref[row, :] = new_max

        return carry

    lax.fori_loop(0, kv_ref.shape[0], step, 0)


def stats_own_kernel(q_ref, off_ref, start_ref, kv0, m_ref, l_ref, bias_ref, kv_ref):
    m_ref[...] = jnp.full_like(m_ref, EMPTY)
    l_ref[...] = jnp.zeros_like(l_ref)
    load_entries(kv_ref, (kv0,))
    stats_entries(0, kv_ref, q_ref, off_ref, start_ref, m_ref, l_ref, bias_ref)


def stats_mid_kernel(q_ref, off_ref, start_ref, m_in, l_in, kv1, kv2, m_ref, l_ref, bias_ref, kv_ref):
    m_ref[...] = m_in[...]
    l_ref[...] = l_in[...]
    load_entries(kv_ref, (kv1, kv2))
    stats_entries(1, kv_ref, q_ref, off_ref, start_ref, m_ref, l_ref, bias_ref)


def grad_entries(slot, kv_ref, q_ref, g_ref, off_ref, start_ref, lse_ref, delta_ref, dq_ref, bias_ref, part_ref):
    heads = lse_ref.shape[0]
    part_ref[...] = jnp.zeros_like(part_ref)

    def step(entry, carry):
        @pl.when(listed(off_ref, slot, entry))
        def _():
            write_bias(bias_ref, start_ref, slot, entry)
            keys = kv_ref[entry, 0]
            values = kv_ref[entry, 1]
            keys_t = keys.T

            def q_head(head):
                return q_ref[:, head * HD : (head + 1) * HD]

            def g_head(head):
                return g_ref[:, head * HD : (head + 1) * HD]

            def products(head):
                return nt_dot(keys, q_head(head)), nt_dot(values, g_head(head))

            def weights(head, ahead):
                row = slice(head, head + 1)
                probs = jnp.exp2(ahead[0] * SCORE_SCALE + bias_ref[...] - lse_ref[row, :])
                d_score = probs * (ahead[1] - delta_ref[row, :])
                return probs.astype(jnp.bfloat16), d_score.astype(jnp.bfloat16)

            def sums(head, pair, acc):
                at = head * HD
                dq_ref[at : at + HD, :] += nn_dot(keys_t, pair[1])
                d_key = nn_dot(pair[1], q_head(head))
                d_value = nn_dot(pair[0], g_head(head))
                return (d_key, d_value) if acc is None else (acc[0] + d_key, acc[1] + d_value)

            acc = None
            ahead, pair = products(0), None
            for head in range(heads):
                following = products(head + 1) if head + 1 < heads else None
                if pair is not None:
                    acc = sums(head - 1, pair, acc)
                pair, ahead = weights(head, ahead), following
            acc = sums(heads - 1, pair, acc)
            part_ref[entry, :, 0:HD] = acc[0] * FACTOR
            part_ref[entry, :, HD:] = acc[1]

        return carry

    lax.fori_loop(0, kv_ref.shape[0], step, 0)


def grad_far_kernel(q_ref, g_ref, off_ref, start_ref, delta_ref, m_in, l_in, kv3, kv4,
                    p3_own, p3_other, p4_ref, dq_ref, lse_ref, m_ref, l_ref, bias_ref, kv_ref, part_ref):
    m_ref[...] = m_in[...]
    l_ref[...] = l_in[...]
    load_entries(kv_ref, (kv3, kv4))
    stats_entries(3, kv_ref, q_ref, off_ref, start_ref, m_ref, l_ref, bias_ref)
    lse_ref[...] = m_ref[...] + jnp.log2(l_ref[...])
    dq_ref[...] = jnp.zeros_like(dq_ref)
    grad_entries(3, kv_ref, q_ref, g_ref, off_ref, start_ref, lse_ref, delta_ref, dq_ref, bias_ref, part_ref)
    core = core_parity()
    p3_own[...] = part_ref[1 - core]
    p3_other[...] = part_ref[core].astype(p3_other.dtype)
    p4_ref[...] = part_ref[2].astype(p4_ref.dtype)


def grad_mid_kernel(q_ref, g_ref, off_ref, start_ref, delta_ref, lse_ref, kv1, kv2, dq_in,
                    p_own, p_other, dq_ref, bias_ref, kv_ref, part_ref):
    load_entries(kv_ref, (kv1, kv2))
    dq_ref[...] = dq_in[...]
    grad_entries(1, kv_ref, q_ref, g_ref, off_ref, start_ref, lse_ref, delta_ref, dq_ref, bias_ref, part_ref)
    core = core_parity()
    for i in range(2):
        p_own[i] = part_ref[2 * i + 1 - core]
        p_other[i] = part_ref[2 * i + core].astype(p_other.dtype)


def grad_own_kernel(q_ref, g_ref, off_ref, start_ref, delta_ref, lse_ref, kv0, dq_in,
                    p_own, p_other, out_ref, bias_ref, kv_ref, part_ref, dq_ref):
    load_entries(kv_ref, (kv0,))
    dq_ref[...] = dq_in[...]
    grad_entries(0, kv_ref, q_ref, g_ref, off_ref, start_ref, lse_ref, delta_ref, dq_ref, bias_ref, part_ref)
    core = core_parity()
    p_own[...] = part_ref[1 - core]
    p_other[...] = part_ref[core].astype(p_other.dtype)
    for head in range(lse_ref.shape[0]):
        at = slice(head * HD, (head + 1) * HD)
        out_ref[:, at] = (dq_ref[at, :] * FACTOR).T.astype(out_ref.dtype)


def merge_far_kernel(own_ref, gathered_ref, out_ref):
    total = own_ref[...] + gathered_ref[1 - core_parity()].astype(jnp.float32)
    out_ref[...] = total.astype(out_ref.dtype)


def merge_mid_kernel(own_ref, gathered_ref, back3_ref, back4_ref, p1_ref, p2_ref):
    other = gathered_ref.at[1 - core_parity()]
    p1_ref[...] = (own_ref[0] + other[0].astype(jnp.float32)).astype(p1_ref.dtype)
    total = own_ref[1] + other[1].astype(jnp.float32)
    total += back3_ref[...].astype(jnp.float32) + back4_ref[...].astype(jnp.float32)
    p2_ref[...] = total.astype(p2_ref.dtype)


def final_kernel(own_ref, gathered_ref, back1_ref, back2_ref, dk_ref, dv_ref):
    total = own_ref[...] + gathered_ref[1 - core_parity()].astype(jnp.float32)
    total += back1_ref[...].astype(jnp.float32) + back2_ref[...].astype(jnp.float32)
    dk_ref[...] = total[:, 0:HD].astype(dk_ref.dtype)
    dv_ref[...] = total[:, HD:].astype(dv_ref.dtype)


def call(kernel, outs, scratch, units, *args, smem_args=0):
    pair = 2 * 8 * 256 * 256
    moved = sum(a.size * a.dtype.itemsize for a in args) + sum(o.size * o.dtype.itemsize for o in outs)
    spaces = [pltpu.SMEM] * smem_args + [pltpu.VMEM] * (len(args) - smem_args)
    return pl.pallas_call(
        kernel,
        out_shape=outs,
        in_specs=[pl.BlockSpec(memory_space=space) for space in spaces],
        out_specs=[pl.BlockSpec(memory_space=pltpu.VMEM) for _ in outs],
        scratch_shapes=scratch,
        compiler_params=pltpu.CompilerParams(vmem_limit_bytes=VMEM_BYTES),
        cost_estimate=pl.CostEstimate(flops=units * pair * HD, bytes_accessed=moved, transcendentals=pair),
    )(*args)


def on_device(queries, keys, values, outputs, out_grad, doc_lengths, block_offsets):
    rows, width = queries.shape
    heads = width // HD
    struct = jax.ShapeDtypeStruct
    f32, bf16 = jnp.float32, jnp.bfloat16
    stat = struct((heads, rows), f32)
    piece16, piece32 = struct((rows, 2 * HD), bf16), struct((rows, 2 * HD), f32)
    dq_part = struct((width, rows), f32)
    bias = pltpu.VMEM((rows, rows), f32)
    row_stat = pltpu.VMEM((heads, rows), f32)

    def stack(count):
        return pltpu.VMEM((count, 2, rows, HD), bf16)

    def parts(count):
        return pltpu.VMEM((count, rows, 2 * HD), f32)

    which = lax.broadcasted_iota(jnp.int32, (2, rows, HD), 0)
    kv = jnp.where(which == 0, keys[None], values[None])
    kv2 = shift(kv, 4)
    kv1 = shift(kv, 2)
    both0 = gather_pair(kv)
    start, delta = call(
        prep_kernel, [struct((8, rows), jnp.int32), stat], [], 1, doc_lengths, out_grad, outputs, smem_args=1)
    m, l = call(
        stats_own_kernel, [stat, stat], [bias, stack(2)], 2, queries, block_offsets, start, both0)
    kv1, kv2, m, l, delta = lax.optimization_barrier((kv1, kv2, m, l, delta))
    kv3 = shift(kv2, 2)
    kv4 = shift(kv2, 3, 1)
    both1, both2 = gather_pair(kv1), gather_pair(kv2)
    m, l = call(
        stats_mid_kernel, [stat, stat], [bias, stack(4)], 4, queries, block_offsets, start, m, l, both1, both2)
    both3 = gather_pair(kv3)

    known = (queries, out_grad, block_offsets, start, delta)
    p3_own, p3_other, p4, dq, lse = call(
        grad_far_kernel, [piece32, piece16, piece16, dq_part, stat], [row_stat, row_stat, bias, stack(3), parts(3)],
        18, *known, m, l, both3, kv4)
    back4 = shift(p4, -3, 0)
    (p3,) = call(merge_far_kernel, [piece16], [], 0, p3_own, gather_pair(p3_other))
    back3 = shift(p3, -2)
    p12_own, p12_other, dq = call(
        grad_mid_kernel, [struct((2, rows, 2 * HD), f32), struct((2, rows, 2 * HD), bf16), dq_part],
        [bias, stack(4), parts(4)], 20, *known, lse, both1, both2, dq)
    p1, p2 = call(merge_mid_kernel, [piece16, piece16], [], 0, p12_own, gather_pair(p12_other), back3, back4)
    back2 = shift(p2, -4)
    back1 = shift(p1, -2)
    p0_own, p0_other, grad_queries = call(
        grad_own_kernel, [piece32, piece16, struct((rows, width), bf16)],
        [bias, stack(2), parts(2), pltpu.VMEM((width, rows), f32)], 10, *known, lse, both0, dq)
    piece = struct((rows, HD), bf16)
    grad_keys, grad_values = call(
        final_kernel, [piece, piece], [], 0, p0_own, gather_pair(p0_other), back1, back2)
    return grad_queries, grad_keys, grad_values


def solution(mesh):
    tokens = P(("dp", "cp"), "hd")
    return jax.shard_map(
        on_device,
        mesh=mesh,
        in_specs=(tokens, tokens, tokens, tokens, tokens, P("dp"), P(("dp", "cp"), None)),
        out_specs=(tokens, tokens, tokens),
        check_vma=False,
    )
```

time: 236 us -> 71.9 us (0.30)
  the two profiles are of different devices: /device:TPU:165 before, /device:TPU:162 now
where the time goes in v3:
time: 71.9 us; the launch traced here: 71.4 us
  starting transfers between devices  21.5 us (30%)
  Pallas kernels  20 us (28%)
  blocking collectives  18.3 us (25%)
  waiting for transfers between devices  7.09 us (10%)
  other arithmetic  1.97 us (3%)
  local copies, waits for them, and re-layouts  1.71 us (2%)
  between operations  0.82 us (1%)
    ppermute x8, starting transfers between devices, shift(): return lax.ppermute(array, 'cp', pairs)  21.5 us
    pallas_call x9, Pallas kernels, call(): pl.pallas_call(kernel, out_shape=outs, in_specs=[pl.BlockSpec(memory_spac...  20 us
    all_gather x7, blocking collectives, gather_pair(): lax.all_gather(array, 'cp', axis_index_groups=[[i, i + 1] for i in range(...  18.3 us
    ppermute x8, waiting for transfers between devices, shift(): return lax.ppermute(array, 'cp', pairs)  7.09 us
    select_n x2, other arithmetic, on_device(): kv = jnp.where(which == 0, keys[None], values[None])  1.97 us
    unnamed x12, local copies, waits for them, and re-layouts  1.71 us
  transfers between devices with their start and end apart: 8, of which 2 were waited for; matrix products, arithmetic and copies ran while one was open for 1% of the time, Pallas kernels for 22%

profile of v3, /device:TPU:162, one launch (start us, length us, event | category | flops | bytes accessed | tf_op | source)
XLA Modules:
  0.0 71.4 jit_solution(567977041108016797)
XLA Ops:
  0.6 0.0 copy-start
  0.7 1.0 %broadcast_select_fusion.1 = bf16[2,256,128]{2,1,0:T(8,128)(2,1)S(1)} fusion(pred[2]{0:T(512)(128)(4,1)S(1)} %iota_compare_fusion, bf16[256,128]{1,0:T(8,128)(2,1)} %param.9, bf16[256,128]{1,0:T(8,128)(2,1)} %param.8), kind=kLoop, calls=%fused_computation.1 | loop fusion | flops 65536 | bytes 262146 | tf_op jit(solution)/shard_map/jit(_where)/select_n | solution.py:266
  1.7 0.0 copy-start.4
  1.7 5.2 %collective-permute-start.1 = (bf16[2,256,128]{2,1,0:T(8,128)(2,1)S(1)}, bf16[2,256,128]{2,1,0:T(8,128)(2,1)S(1)}, u32[]{:S(2)}, u32[]{:S(2)}) collective-permute-start(bf16[2,256,128]{2,1,0:T(8,128)(2,1)S(1)} %broadcast_select_fusion.1), channel_id=1, source_target_pairs={{0,64},{16,80},{32,96},{48,112},{64,128},{80,144},{96,160},{112,17... | collective-permute-start | bytes 393224 | tf_op jit(solution)/shard_map/ppermute | solution.py:19
  6.9 5.0 %collective-permute-start = (bf16[2,256,128]{2,1,0:T(8,128)(2,1)S(1)}, bf16[2,256,128]{2,1,0:T(8,128)(2,1)S(1)}, u32[]{:S(2)}, u32[]{:S(2)}) collective-permute-start(bf16[2,256,128]{2,1,0:T(8,128)(2,1)S(1)} %broadcast_select_fusion.1), channel_id=1, source_target_pairs={{0,32},{16,48},{32,64},{48,80},{64,96},{80,112},{96,128},{112,144}... | collective-permute-start | bytes 393224 | tf_op jit(solution)/shard_map/ppermute | solution.py:19
  11.9 1.0 %broadcast_select_fusion = bf16[1,2,256,128]{3,2,1,0:T(8,128)(2,1)S(1)} fusion(pred[2]{0:T(512)(128)(4,1)S(1)} %iota_compare_fusion, bf16[256,128]{1,0:T(8,128)(2,1)} %param.9, bf16[256,128]{1,0:T(8,128)(2,1)} %param.8), kind=kLoop, calls=%fused_computation | loop fusion | flops 65536 | bytes 262146 | tf_op jit(solution)/shard_map/jit(_where)/select_n | solution.py:266
  12.9 0.0 copy-done
  12.9 0.0 copy-done.4
  12.9 0.0 copy-start.2
  12.9 1.0 %copy-done.2 = bf16[256,1024]{1,0:T(8,128)(2,1)S(1)} copy-done((bf16[256,1024]{1,0:T(8,128)(2,1)S(1)}, bf16[256,1024]{1,0:T(8,128)(2,1)}, u32[]{:S(2)}) %copy-start.2) | copy-done | bytes 524312
  13.9 0.0 copy-start.1
  13.9 1.2 %shard_map.94 = (s32[8,256]{1,0:T(8,128)S(1)}, f32[8,256]{1,0:T(8,128)S(1)}) custom-call(s32[51]{0:T(128)S(1)} %copy-done.4, bf16[256,1024]{1,0:T(8,128)(2,1)S(1)} %copy-done.2, bf16[256,1024]{1,0:T(8,128)(2,1)S(1)} %copy-done), custom_call_target="tpu_custom_call" | custom-call | flops 134217728 | bytes 1065164 | tf_op jit(solution)/shard_map/pallas_call | solution.py:237
  15.1 2.0 %all_gather.40.kv0 = bf16[2,2,256,128]{3,2,1,0:T(8,128)(2,1)S(1)} all-gather(bf16[1,2,256,128]{3,2,1,0:T(8,128)(2,1)S(1)} %broadcast_select_fusion), channel_id=1, replica_groups={{0,16},{32,48},{64,80},{96,112},{128,144},{160,176},{192,208},{224,240}..., dimensions={0}, use_global_device_ids=true | all-gather | bytes 393216 | tf_op jit(solution)/shard_map/all_gather | solution.py:24
  17.1 0.0 copy-start.5
  17.1 0.0 copy-done.1
  17.1 0.7 copy-done.5
  17.8 1.1 %shard_map.95 = (f32[8,256]{1,0:T(8,128)S(1)}, f32[8,256]{1,0:T(8,128)S(1)}) custom-call(bf16[256,1024]{1,0:T(8,128)(2,1)S(1)} %copy-done.1, s32[1,16]{1,0:T(1,128)S(1)} %copy-done.5, s32[8,256]{1,0:T(8,128)S(1)} %get-tuple-element.29.start_ref, bf16[2,2,256,128]{3,2,1,0:T(8,128)(2,1)S(1)} %all_gather.40.kv0), custom_call_target="tpu_custom_call" | custom-call | flops 268435456 | bytes 811072 | tf_op jit(solution)/shard_map/pallas_call | solution.py:237
  18.9 0.0 collective-permute-done.1
  18.9 0.0 collective-permute-done
  18.9 1.3 %collective-permute-start.3 = (bf16[2,256,128]{2,1,0:T(8,128)(2,1)S(1)}, bf16[2,256,128]{2,1,0:T(8,128)(2,1)S(1)}, u32[]{:S(2)}, u32[]{:S(2)}) collective-permute-start(bf16[2,256,128]{2,1,0:T(8,128)(2,1)S(1)} %collective-permute-done.1), channel_id=1, source_target_pairs={{16,64},{48,96},{80,128},{112,160},{144,192},{176,224},{208,256},{... | collective-permute-start | bytes 393224 | tf_op jit(solution)/shard_map/ppermute | solution.py:19
  20.2 2.9 %collective-permute-start.2 = (bf16[2,256,128]{2,1,0:T(8,128)(2,1)S(1)}, bf16[2,256,128]{2,1,0:T(8,128)(2,1)S(1)}, u32[]{:S(2)}, u32[]{:S(2)}) collective-permute-start(bf16[2,256,128]{2,1,0:T(8,128)(2,1)S(1)} %collective-permute-done.1), channel_id=1, source_target_pairs={{0,32},{16,48},{32,64},{48,80},{64,96},{80,112},{96,128},{112,144}... | collective-permute-start | bytes 393224 | tf_op jit(solution)/shard_map/ppermute | solution.py:19
  23.1 4.7 %all-gather.1 = bf16[4,256,128]{2,1,0:T(8,128)(2,1)S(1)} all-gather(bf16[2,256,128]{2,1,0:T(8,128)(2,1)S(1)} %collective-permute-done.1), channel_id=3, replica_groups={{0,16},{32,48},{64,80},{96,112},{128,144},{160,176},{192,208},{224,240}..., dimensions={0}, use_global_device_ids=true | all-gather | bytes 393216 | tf_op jit(solution)/shard_map/all_gather | solution.py:24
  27.8 2.0 %all-gather = bf16[4,256,128]{2,1,0:T(8,128)(2,1)S(1)} all-gather(bf16[2,256,128]{2,1,0:T(8,128)(2,1)S(1)} %collective-permute-done), channel_id=2, replica_groups={{0,16},{32,48},{64,80},{96,112},{128,144},{160,176},{192,208},{224,240}..., dimensions={0}, use_global_device_ids=true | all-gather | bytes 393216 | tf_op jit(solution)/shard_map/all_gather | solution.py:24
  29.8 0.0 copy-start.3
  29.8 3.6 %shard_map.96 = (f32[8,256]{1,0:T(8,128)S(1)}, f32[8,256]{1,0:T(8,128)S(1)}) custom-call(bf16[256,1024]{1,0:T(8,128)(2,1)S(1)} %copy-done.1, s32[1,16]{1,0:T(1,128)S(1)} %copy-done.5, s32[8,256]{1,0:T(8,128)S(1)} %get-tuple-element.29.start_ref, f32[8,256]{1,0:T(8,128)S(1)} %get-tuple-element.34.m_in, f32[8,256]{1,0:T(8,128)S(1)} %get-tuple-element.35.l_in, ...), custom_call_target="tpu_custom_call" | custom-call | flops 536870912 | bytes 1089600 | tf_op jit(solution)/shard_map/pallas_call | solution.py:237
  33.4 0.0 collective-permute-done.2
  33.4 2.0 %all-gather.2 = bf16[4,256,128]{2,1,0:T(8,128)(2,1)S(1)} all-gather(bf16[2,256,128]{2,1,0:T(8,128)(2,1)S(1)} %collective-permute-done.2), channel_id=4, replica_groups={{0,16},{32,48},{64,80},{96,112},{128,144},{160,176},{192,208},{224,240}..., dimensions={0}, use_global_device_ids=true | all-gather | bytes 393216 | tf_op jit(solution)/shard_map/all_gather | solution.py:24
  35.4 0.0 collective-permute-done.3.kv4
  35.4 0.0 copy-done.3
  35.4 3.3 %shard_map.97 = (f32[256,256]{1,0:T(8,128)S(1)}, bf16[256,256]{1,0:T(8,128)(2,1)S(1)}, bf16[256,256]{1,0:T(8,128)(2,1)S(1)}, f32[1024,256]{1,0:T(8,128)S(1)}, f32[8,256]{1,0:T(8,128)S(1)}) custom-call(bf16[256,1024]{1,0:T(8,128)(2,1)S(1)} %copy-done.1, bf16[256,1024]{1,0:T(8,128)(2,1)S(1)} %copy-done.3, s32[1,16]{1,0:T(1,128)S(1)} %copy-done.5, ...), custom_call_target="tpu_custom_call" | custom-call | flops 2415919104 | bytes 3055680 | tf_op jit(solution)/shard_map/pallas_call | solution.py:237
  38.8 1.3 %collective-permute-start.5 = (bf16[256,256]{1,0:T(8,128)(2,1)S(1)}, bf16[256,256]{1,0:T(8,128)(2,1)S(1)}, u32[]{:S(2)}, u32[]{:S(2)}) collective-permute-start(bf16[256,256]{1,0:T(8,128)(2,1)S(1)} %get-tuple-element.50), channel_id=1, source_target_pairs={{0,464},{32,496},{64,16},{96,48},{128,80},{160,112},{192,144},{224... | collective-permute-start | bytes 393224 | tf_op jit(solution)/shard_map/ppermute | solution.py:19
  40.1 2.0 %all-gather.5 = bf16[512,256]{1,0:T(8,128)(2,1)S(1)} all-gather(bf16[256,256]{1,0:T(8,128)(2,1)S(1)} %get-tuple-element.49), channel_id=7, replica_groups={{0,16},{32,48},{64,80},{96,112},{128,144},{160,176},{192,208},{224,240}..., dimensions={0}, use_global_device_ids=true | all-gather | bytes 393216 | tf_op jit(solution)/shard_map/all_gather | solution.py:24
  42.1 1.9 %collective-permute-start.4 = (bf16[256,256]{1,0:T(8,128)(2,1)S(1)}, bf16[256,256]{1,0:T(8,128)(2,1)S(1)}, u32[]{:S(2)}, u32[]{:S(2)}) collective-permute-start(bf16[256,256]{1,0:T(8,128)(2,1)S(1)} %shard_map.100), channel_id=1, source_target_pairs={{0,480},{16,496},{32,0},{48,16},{64,32},{80,48},{96,64},{112,80},{... | collective-permute-start | bytes 393224 | tf_op jit(solution)/shard_map/ppermute | solution.py:19
  44.0 7.0 %shard_map.98 = (f32[2,256,256]{2,1,0:T(8,128)S(1)}, bf16[2,256,256]{2,1,0:T(8,128)(2,1)S(1)}, f32[1024,256]{1,0:T(8,128)S(1)}) custom-call(bf16[256,1024]{1,0:T(8,128)(2,1)S(1)} %copy-done.1, bf16[256,1024]{1,0:T(8,128)(2,1)S(1)} %copy-done.3, s32[1,16]{1,0:T(1,128)S(1)} %copy-done.5, s32[8,256]{1,0:T(8,128)S(1)} %get-tuple-element.29.start_ref, ...), custom_call_target="tpu_custom_call" | custom-call | flops 2684354560 | bytes 4481088 | tf_op jit(solution)/shard_map/pallas_call | solution.py:237
  51.0 2.2 %all-gather.4 = bf16[4,256,256]{2,1,0:T(8,128)(2,1)S(1)} all-gather(bf16[2,256,256]{2,1,0:T(8,128)(2,1)S(1)} %get-tuple-element.47), channel_id=6, replica_groups={{0,16},{32,48},{64,80},{96,112},{128,144},{160,176},{192,208},{224,240}..., dimensions={0}, use_global_device_ids=true | all-gather | bytes 786432 | tf_op jit(solution)/shard_map/all_gather | solution.py:24
  53.2 0.0 collective-permute-done.5.back4_ref
  53.2 0.0 collective-permute-done.4.back3_ref
  53.2 0.1 shard_map.101
  53.3 1.9 %collective-permute-start.6 = (bf16[256,256]{1,0:T(8,128)(2,1)S(1)}, bf16[256,256]{1,0:T(8,128)(2,1)S(1)}, u32[]{:S(2)}, u32[]{:S(2)}) collective-permute-start(bf16[256,256]{1,0:T(8,128)(2,1)S(1)} %get-tuple-element.51), channel_id=1, source_target_pairs={{0,480},{16,496},{32,0},{48,16},{64,32},{80,48},{96,64},{112,80},{... | collective-permute-start | bytes 393224 | tf_op jit(solution)/shard_map/ppermute | solution.py:19
  55.2 1.9 %collective-permute-start.7 = (bf16[256,256]{1,0:T(8,128)(2,1)S(1)}, bf16[256,256]{1,0:T(8,128)(2,1)S(1)}, u32[]{:S(2)}, u32[]{:S(2)}) collective-permute-start(bf16[256,256]{1,0:T(8,128)(2,1)S(1)} %get-tuple-element.52), channel_id=1, source_target_pairs={{0,448},{16,464},{32,480},{48,496},{64,0},{80,16},{96,32},{112,48}... | collective-permute-start | bytes 393224 | tf_op jit(solution)/shard_map/ppermute | solution.py:19
  57.2 2.9 %shard_map.99 = (f32[256,256]{1,0:T(8,128)S(1)}, bf16[256,256]{1,0:T(8,128)(2,1)S(1)}, bf16[256,1024]{1,0:T(8,128)(2,1)}) custom-call(bf16[256,1024]{1,0:T(8,128)(2,1)S(1)} %copy-done.1, bf16[256,1024]{1,0:T(8,128)(2,1)S(1)} %copy-done.3, s32[1,16]{1,0:T(1,128)S(1)} %copy-done.5, s32[8,256]{1,0:T(8,128)S(1)} %get-tuple-element.29.start_ref, ...), custom_call_target="tpu_custom_call" | custom-call | flops 1342177280 | bytes 3301440 | tf_op jit(solution)/shard_map/pallas_call | solution.py:237
  60.1 3.5 %all-gather.3 = bf16[512,256]{1,0:T(8,128)(2,1)S(1)} all-gather(bf16[256,256]{1,0:T(8,128)(2,1)S(1)} %get-tuple-element.45), channel_id=5, replica_groups={{0,16},{32,48},{64,80},{96,112},{128,144},{160,176},{192,208},{224,240}..., dimensions={0}, use_global_device_ids=true | all-gather | bytes 393216 | tf_op jit(solution)/shard_map/all_gather | solution.py:24
  63.6 0.9 %collective-permute-done.6.back1_ref = bf16[256,256]{1,0:T(8,128)(2,1)S(1)} collective-permute-done((bf16[256,256]{1,0:T(8,128)(2,1)S(1)}, bf16[256,256]{1,0:T(8,128)(2,1)S(1)}, u32[]{:S(2)}, u32[]{:S(2)}) %collective-permute-start.6) | collective-permute-done | bytes 131104 | tf_op jit(solution)/shard_map/ppermute | solution.py:19
  64.5 6.2 %collective-permute-done.7.back2_ref = bf16[256,256]{1,0:T(8,128)(2,1)S(1)} collective-permute-done((bf16[256,256]{1,0:T(8,128)(2,1)S(1)}, bf16[256,256]{1,0:T(8,128)(2,1)S(1)}, u32[]{:S(2)}, u32[]{:S(2)}) %collective-permute-start.7) | collective-permute-done | bytes 131104 | tf_op jit(solution)/shard_map/ppermute | solution.py:19
  70.7 0.7 shard_map.102
  (2 shorter events, 0.0 us)
Async XLA Ops:
  0.6 12.2 %copy-start = (bf16[256,1024]{1,0:T(8,128)(2,1)S(1)}, bf16[256,1024]{1,0:T(8,128)(2,1)}, u32[]{:S(2)}) copy-start(bf16[256,1024]{1,0:T(8,128)(2,1)} %o_ref.1) | copy-start | bytes 1572868
  1.7 11.2 %copy-start.4 = (s32[51]{0:T(128)S(1)}, s32[51]{0:T(128)}, u32[]{:S(2)}) copy-start(s32[51]{0:T(128)} %doc_ref.1) | copy-start | bytes 616
  1.7 17.2 %collective-permute-start.1 = (bf16[2,256,128]{2,1,0:T(8,128)(2,1)S(1)}, bf16[2,256,128]{2,1,0:T(8,128)(2,1)S(1)}, u32[]{:S(2)}, u32[]{:S(2)}) collective-permute-start(bf16[2,256,128]{2,1,0:T(8,128)(2,1)S(1)} %broadcast_select_fusion.1), channel_id=1, source_target_pairs={{0,64},{16,80},{32,96},{48,112},{64,128},{80,144},{96,160},{112,17... | collective-permute-start | bytes 393224 | tf_op jit(solution)/shard_map/ppermute | solution.py:19
  6.9 12.0 %collective-permute-start = (bf16[2,256,128]{2,1,0:T(8,128)(2,1)S(1)}, bf16[2,256,128]{2,1,0:T(8,128)(2,1)S(1)}, u32[]{:S(2)}, u32[]{:S(2)}) collective-permute-start(bf16[2,256,128]{2,1,0:T(8,128)(2,1)S(1)} %broadcast_select_fusion.1), channel_id=1, source_target_pairs={{0,32},{16,48},{32,64},{48,80},{64,96},{80,112},{96,128},{112,144}... | collective-permute-start | bytes 393224 | tf_op jit(solution)/shard_map/ppermute | solution.py:19
  12.9 1.0 %copy-start.2 = (bf16[256,1024]{1,0:T(8,128)(2,1)S(1)}, bf16[256,1024]{1,0:T(8,128)(2,1)}, u32[]{:S(2)}) copy-start(bf16[256,1024]{1,0:T(8,128)(2,1)} %g_ref.7) | copy-start | bytes 1572868
  13.9 3.2 %copy-start.1 = (bf16[256,1024]{1,0:T(8,128)(2,1)S(1)}, bf16[256,1024]{1,0:T(8,128)(2,1)}, u32[]{:S(2)}) copy-start(bf16[256,1024]{1,0:T(8,128)(2,1)} %q_ref.9) | copy-start | bytes 1572868
  17.1 0.7 copy-start.5
  18.9 16.5 %collective-permute-start.3 = (bf16[2,256,128]{2,1,0:T(8,128)(2,1)S(1)}, bf16[2,256,128]{2,1,0:T(8,128)(2,1)S(1)}, u32[]{:S(2)}, u32[]{:S(2)}) collective-permute-start(bf16[2,256,128]{2,1,0:T(8,128)(2,1)S(1)} %collective-permute-done.1), channel_id=1, source_target_pairs={{16,64},{48,96},{80,128},{112,160},{144,192},{176,224},{208,256},{... | collective-permute-start | bytes 393224 | tf_op jit(solution)/shard_map/ppermute | solution.py:19
  20.2 13.2 %collective-permute-start.2 = (bf16[2,256,128]{2,1,0:T(8,128)(2,1)S(1)}, bf16[2,256,128]{2,1,0:T(8,128)(2,1)S(1)}, u32[]{:S(2)}, u32[]{:S(2)}) collective-permute-start(bf16[2,256,128]{2,1,0:T(8,128)(2,1)S(1)} %collective-permute-done.1), channel_id=1, source_target_pairs={{0,32},{16,48},{32,64},{48,80},{64,96},{80,112},{96,128},{112,144}... | collective-permute-start | bytes 393224 | tf_op jit(solution)/shard_map/ppermute | solution.py:19
  29.8 5.7 %copy-start.3 = (bf16[256,1024]{1,0:T(8,128)(2,1)S(1)}, bf16[256,1024]{1,0:T(8,128)(2,1)}, u32[]{:S(2)}) copy-start(bf16[256,1024]{1,0:T(8,128)(2,1)} %g_ref.7) | copy-start | bytes 1572868
  38.8 14.4 %collective-permute-start.5 = (bf16[256,256]{1,0:T(8,128)(2,1)S(1)}, bf16[256,256]{1,0:T(8,128)(2,1)S(1)}, u32[]{:S(2)}, u32[]{:S(2)}) collective-permute-start(bf16[256,256]{1,0:T(8,128)(2,1)S(1)} %get-tuple-element.50), channel_id=1, source_target_pairs={{0,464},{32,496},{64,16},{96,48},{128,80},{160,112},{192,144},{224... | collective-permute-start | bytes 393224 | tf_op jit(solution)/shard_map/ppermute | solution.py:19
  42.1 11.1 %collective-permute-start.4 = (bf16[256,256]{1,0:T(8,128)(2,1)S(1)}, bf16[256,256]{1,0:T(8,128)(2,1)S(1)}, u32[]{:S(2)}, u32[]{:S(2)}) collective-permute-start(bf16[256,256]{1,0:T(8,128)(2,1)S(1)} %shard_map.100), channel_id=1, source_target_pairs={{0,480},{16,496},{32,0},{48,16},{64,32},{80,48},{96,64},{112,80},{... | collective-permute-start | bytes 393224 | tf_op jit(solution)/shard_map/ppermute | solution.py:19
  53.3 11.2 %collective-permute-start.6 = (bf16[256,256]{1,0:T(8,128)(2,1)S(1)}, bf16[256,256]{1,0:T(8,128)(2,1)S(1)}, u32[]{:S(2)}, u32[]{:S(2)}) collective-permute-start(bf16[256,256]{1,0:T(8,128)(2,1)S(1)} %get-tuple-element.51), channel_id=1, source_target_pairs={{0,480},{16,496},{32,0},{48,16},{64,32},{80,48},{96,64},{112,80},{... | collective-permute-start | bytes 393224 | tf_op jit(solution)/shard_map/ppermute | solution.py:19
  55.2 15.5 %collective-permute-start.7 = (bf16[256,256]{1,0:T(8,128)(2,1)S(1)}, bf16[256,256]{1,0:T(8,128)(2,1)S(1)}, u32[]{:S(2)}, u32[]{:S(2)}) collective-permute-start(bf16[256,256]{1,0:T(8,128)(2,1)S(1)} %get-tuple-element.52), channel_id=1, source_target_pairs={{0,448},{16,464},{32,480},{48,496},{64,0},{80,16},{96,32},{112,48}... | collective-permute-start | bytes 393224 | tf_op jit(solution)/shard_map/ppermute | solution.py:19

commit v4 on v3

--- a/solution.py
+++ b/solution.py
@@ -40,16 +40,28 @@
     return lax.axis_index("cp") - core_parity() + 1 - 2 * slot - entry
 
 
-def listed(off_ref, slot, entry):
+def listed_bits(off_ref):
+    offsets = off_ref[...]
+    bits = jnp.where(offsets >= 0, lax.shift_left(jnp.ones_like(offsets), jnp.maximum(offsets, 0)), 0)
+    return jnp.sum(bits.astype(jnp.float32)).astype(jnp.int32)
+
+
+def pick(values, i):
+    chosen = values[0]
+    for j in range(1, len(values)):
+        chosen = jnp.where(i == j, values[j], chosen)
+    return chosen
+
+
+def listed(bits, key):
     block = lax.axis_index("cp")
-    key = key_block(slot, entry)
-    hits = jnp.max((off_ref[...] == block - key).astype(jnp.float32))
-    return (hits > 0.0) & (block >= key) & (key >= 0)
-
-
-def write_bias(bias_ref, start_ref, slot, entry):
+    bit = lax.shift_right_logical(bits, jnp.maximum(block - key, 0)) & 1
+    return (bit == 1) & (block >= key) & (key >= 0)
+
+
+def write_bias(bias_ref, start_ref, key):
     rows = bias_ref.shape[0]
-    key_pos = key_block(slot, entry) * rows + lax.broadcasted_iota(jnp.int32, bias_ref.shape, 0)
+    key_pos = key * rows + lax.broadcasted_iota(jnp.int32, bias_ref.shape, 0)
     q_pos = lax.axis_index("cp") * rows + lax.broadcasted_iota(jnp.int32, bias_ref.shape, 1)
     allowed = (key_pos >= start_ref[0:1, :]) & (key_pos <= q_pos)
     bias_ref[...] = jnp.where(allowed, 0.0, MASKED)
@@ -72,20 +84,16 @@
         delta_ref[head : head + 1, :] = jnp.sum(product.T, axis=0, keepdims=True)
 
 
-def load_entries(kv_ref, gathered):
-    for i in range(kv_ref.shape[0]):
-        pair = gathered[i // 2]
-        kv_ref[i] = pair[1 - i % 2] if len(pair.shape) == 4 else pair[...]
-
-
-def stats_entries(slot, kv_ref, q_ref, off_ref, start_ref, m_ref, l_ref, bias_ref):
+def stats_entries(key_blocks, bits, kv_ref, q_ref, start_ref, m_ref, l_ref, bias_ref):
     heads = m_ref.shape[0]
 
-    def step(entry, carry):
-        @pl.when(listed(off_ref, slot, entry))
+    def step(i, carry):
+        key = pick(key_blocks, i)
+
+        @pl.when(listed(bits, key))
         def _():
-            write_bias(bias_ref, start_ref, slot, entry)
-            keys = kv_ref[entry, 0]
+            write_bias(bias_ref, start_ref, key)
+            keys = kv_ref[i, 0]
 
             def products(head):
                 return nt_dot(keys, q_ref[:, head * HD : (head + 1) * HD])
@@ -104,33 +112,39 @@
 
         return carry
 
-    lax.fori_loop(0, kv_ref.shape[0], step, 0)
+    lax.fori_loop(0, len(key_blocks), step, 0)
 
 
 def stats_own_kernel(q_ref, off_ref, start_ref, kv0, m_ref, l_ref, bias_ref, kv_ref):
     m_ref[...] = jnp.full_like(m_ref, EMPTY)
     l_ref[...] = jnp.zeros_like(l_ref)
-    load_entries(kv_ref, (kv0,))
-    stats_entries(0, kv_ref, q_ref, off_ref, start_ref, m_ref, l_ref, bias_ref)
-
-
-def stats_mid_kernel(q_ref, off_ref, start_ref, m_in, l_in, kv1, kv2, m_ref, l_ref, bias_ref, kv_ref):
+    kv_ref[0] = kv0[1]
+    kv_ref[1] = kv0[0]
+    keys = [key_block(0, 0), key_block(0, 1)]
+    stats_entries(keys, listed_bits(off_ref), kv_ref, q_ref, start_ref, m_ref, l_ref, bias_ref)
+
+
+def stats_mid_kernel(q_ref, off_ref, start_ref, m_in, l_in, kv12, m_ref, l_ref, bias_ref, kv_ref):
     m_ref[...] = m_in[...]
     l_ref[...] = l_in[...]
-    load_entries(kv_ref, (kv1, kv2))
-    stats_entries(1, kv_ref, q_ref, off_ref, start_ref, m_ref, l_ref, bias_ref)
-
-
-def grad_entries(slot, kv_ref, q_ref, g_ref, off_ref, start_ref, lse_ref, delta_ref, dq_ref, bias_ref, part_ref):
+    for i in range(4):
+        kv_ref[i] = kv12[1 - i % 2, i // 2]
+    keys = [key_block(1, i) for i in range(4)]
+    stats_entries(keys, listed_bits(off_ref), kv_ref, q_ref, start_ref, m_ref, l_ref, bias_ref)
+
+
+def grad_entries(key_blocks, bits, kv_ref, q_ref, g_ref, start_ref, lse_ref, delta_ref, dq_ref, bias_ref, part_ref):
     heads = lse_ref.shape[0]
     part_ref[...] = jnp.zeros_like(part_ref)
 
-    def step(entry, carry):
-        @pl.when(listed(off_ref, slot, entry))
+    def step(i, carry):
+        key = pick(key_blocks, i)
+
+        @pl.when(listed(bits, key))
         def _():
-            write_bias(bias_ref, start_ref, slot, entry)
-            keys = kv_ref[entry, 0]
-            values = kv_ref[entry, 1]
+            write_bias(bias_ref, start_ref, key)
+            keys = kv_ref[i, 0]
+            values = kv_ref[i, 1]
             keys_t = keys.T
 
             def q_head(head):
@@ -163,55 +177,66 @@
                     acc = sums(head - 1, pair, acc)
                 pair, ahead = weights(head, ahead), following
             acc = sums(heads - 1, pair, acc)
-            part_ref[entry, :, 0:HD] = acc[0] * FACTOR
-            part_ref[entry, :, HD:] = acc[1]
+            part_ref[i, :, 0:HD] = acc[0] * FACTOR
+            part_ref[i, :, HD:] = acc[1]
 
         return carry
 
-    lax.fori_loop(0, kv_ref.shape[0], step, 0)
-
-
-def grad_far_kernel(q_ref, g_ref, off_ref, start_ref, delta_ref, m_in, l_in, kv3, kv4,
-                    p3_own, p3_other, p4_ref, dq_ref, lse_ref, m_ref, l_ref, bias_ref, kv_ref, part_ref):
+    lax.fori_loop(0, len(key_blocks), step, 0)
+
+
+def grad_far_kernel(q_ref, g_ref, off_ref, start_ref, delta_ref, m_in, l_in, kv0, kv3, kv4,
+                    p3_own, p_other, p4_ref, dq_ref, lse_ref, m_ref, l_ref, bias_ref, kv_ref, part_ref):
+    core = core_parity()
+    bits = listed_bits(off_ref)
     m_ref[...] = m_in[...]
     l_ref[...] = l_in[...]
-    load_entries(kv_ref, (kv3, kv4))
-    stats_entries(3, kv_ref, q_ref, off_ref, start_ref, m_ref, l_ref, bias_ref)
+    kv_ref[0] = kv3[1]
+    kv_ref[1] = kv3[0]
+    kv_ref[2] = kv4[...]
+    kv_ref[3] = kv0[0]
+    far = [key_block(3, 0), key_block(3, 1), key_block(3, 2)]
+    stats_entries(far, bits, kv_ref, q_ref, start_ref, m_ref, l_ref, bias_ref)
     lse_ref[...] = m_ref[...] + jnp.log2(l_ref[...])
     dq_ref[...] = jnp.zeros_like(dq_ref)
-    grad_entries(3, kv_ref, q_ref, g_ref, off_ref, start_ref, lse_ref, delta_ref, dq_ref, bias_ref, part_ref)
-    core = core_parity()
+    bits = jnp.where(core == 1, bits, bits & -2)
+    keys = far + [key_block(0, 1)]
+    grad_entries(keys, bits, kv_ref, q_ref, g_ref, start_ref, lse_ref, delta_ref, dq_ref, bias_ref, part_ref)
     p3_own[...] = part_ref[1 - core]
-    p3_other[...] = part_ref[core].astype(p3_other.dtype)
+    p_other[0] = part_ref[core].astype(p_other.dtype)
+    p_other[1] = part_ref[3].astype(p_other.dtype)
     p4_ref[...] = part_ref[2].astype(p4_ref.dtype)
 
 
-def grad_mid_kernel(q_ref, g_ref, off_ref, start_ref, delta_ref, lse_ref, kv1, kv2, dq_in,
+def grad_mid_kernel(q_ref, g_ref, off_ref, start_ref, delta_ref, lse_ref, kv12, dq_in,
                     p_own, p_other, dq_ref, bias_ref, kv_ref, part_ref):
-    load_entries(kv_ref, (kv1, kv2))
+    for i in range(4):
+        kv_ref[i] = kv12[1 - i % 2, i // 2]
     dq_ref[...] = dq_in[...]
-    grad_entries(1, kv_ref, q_ref, g_ref, off_ref, start_ref, lse_ref, delta_ref, dq_ref, bias_ref, part_ref)
+    keys = [key_block(1, i) for i in range(4)]
+    bits = listed_bits(off_ref)
+    grad_entries(keys, bits, kv_ref, q_ref, g_ref, start_ref, lse_ref, delta_ref, dq_ref, bias_ref, part_ref)
     core = core_parity()
     for i in range(2):
         p_own[i] = part_ref[2 * i + 1 - core]
         p_other[i] = part_ref[2 * i + core].astype(p_other.dtype)
 
 
-def grad_own_kernel(q_ref, g_ref, off_ref, start_ref, delta_ref, lse_ref, kv0, dq_in,
-                    p_own, p_other, out_ref, bias_ref, kv_ref, part_ref, dq_ref):
-    load_entries(kv_ref, (kv0,))
+def grad_own_kernel(q_ref, g_ref, off_ref, start_ref, delta_ref, lse_ref, kv_in, dq_in,
+                    p_own, out_ref, bias_ref, kv_ref, part_ref, dq_ref):
+    kv_ref[0] = kv_in[...]
     dq_ref[...] = dq_in[...]
-    grad_entries(0, kv_ref, q_ref, g_ref, off_ref, start_ref, lse_ref, delta_ref, dq_ref, bias_ref, part_ref)
-    core = core_parity()
-    p_own[...] = part_ref[1 - core]
-    p_other[...] = part_ref[core].astype(p_other.dtype)
+    keys = [lax.axis_index("cp")]
+    bits = listed_bits(off_ref)
+    grad_entries(keys, bits, kv_ref, q_ref, g_ref, start_ref, lse_ref, delta_ref, dq_ref, bias_ref, part_ref)
+    p_own[...] = part_ref[0]
     for head in range(lse_ref.shape[0]):
         at = slice(head * HD, (head + 1) * HD)
         out_ref[:, at] = (dq_ref[at, :] * FACTOR).T.astype(out_ref.dtype)
 
 
 def merge_far_kernel(own_ref, gathered_ref, out_ref):
-    total = own_ref[...] + gathered_ref[1 - core_parity()].astype(jnp.float32)
+    total = own_ref[...] + gathered_ref[1 - core_parity(), 0].astype(jnp.float32)
     out_ref[...] = total.astype(out_ref.dtype)
 
 
@@ -223,8 +248,8 @@
     p2_ref[...] = total.astype(p2_ref.dtype)
 
 
-def final_kernel(own_ref, gathered_ref, back1_ref, back2_ref, dk_ref, dv_ref):
-    total = own_ref[...] + gathered_ref[1 - core_parity()].astype(jnp.float32)
+def final_kernel(own_ref, gathered_ref, back2_ref, back1_ref, dk_ref, dv_ref):
+    total = own_ref[...] + gathered_ref[1 - core_parity(), 1].astype(jnp.float32)
     total += back1_ref[...].astype(jnp.float32) + back2_ref[...].astype(jnp.float32)
     dk_ref[...] = total[:, 0:HD].astype(dk_ref.dtype)
     dv_ref[...] = total[:, HD:].astype(dv_ref.dtype)
@@ -264,40 +289,43 @@
 
     which = lax.broadcasted_iota(jnp.int32, (2, rows, HD), 0)
     kv = jnp.where(which == 0, keys[None], values[None])
+    kv = lax.optimization_barrier(kv)
     kv2 = shift(kv, 4)
-    kv1 = shift(kv, 2)
     both0 = gather_pair(kv)
     start, delta = call(
         prep_kernel, [struct((8, rows), jnp.int32), stat], [], 1, doc_lengths, out_grad, outputs, smem_args=1)
     m, l = call(
         stats_own_kernel, [stat, stat], [bias, stack(2)], 2, queries, block_offsets, start, both0)
-    kv1, kv2, m, l, delta = lax.optimization_barrier((kv1, kv2, m, l, delta))
+    kv, m, l, delta = lax.optimization_barrier((kv, m, l, delta))
+    kv1 = shift(kv, 2)
+    kv2, m, l, delta = lax.optimization_barrier((kv2, m, l, delta))
     kv3 = shift(kv2, 2)
     kv4 = shift(kv2, 3, 1)
-    both1, both2 = gather_pair(kv1), gather_pair(kv2)
+    both12 = gather_pair(jnp.stack([kv1, kv2]))
     m, l = call(
-        stats_mid_kernel, [stat, stat], [bias, stack(4)], 4, queries, block_offsets, start, m, l, both1, both2)
+        stats_mid_kernel, [stat, stat], [bias, stack(4)], 4, queries, block_offsets, start, m, l, both12)
     both3 = gather_pair(kv3)
 
     known = (queries, out_grad, block_offsets, start, delta)
-    p3_own, p3_other, p4, dq, lse = call(
-        grad_far_kernel, [piece32, piece16, piece16, dq_part, stat], [row_stat, row_stat, bias, stack(3), parts(3)],
-        18, *known, m, l, both3, kv4)
+    pair16 = struct((2, rows, 2 * HD), bf16)
+    p3_own, far_other, p4, dq, lse = call(
+        grad_far_kernel, [piece32, pair16, piece16, dq_part, stat], [row_stat, row_stat, bias, stack(4), parts(4)],
+        20, *known, m, l, both0, both3, kv4)
     back4 = shift(p4, -3, 0)
-    (p3,) = call(merge_far_kernel, [piece16], [], 0, p3_own, gather_pair(p3_other))
+    far_both = gather_pair(far_other)
+    (p3,) = call(merge_far_kernel, [piece16], [], 0, p3_own, far_both)
     back3 = shift(p3, -2)
-    p12_own, p12_other, dq = call(
-        grad_mid_kernel, [struct((2, rows, 2 * HD), f32), struct((2, rows, 2 * HD), bf16), dq_part],
-        [bias, stack(4), parts(4)], 20, *known, lse, both1, both2, dq)
-    p1, p2 = call(merge_mid_kernel, [piece16, piece16], [], 0, p12_own, gather_pair(p12_other), back3, back4)
+    p12_own, mid_other, dq = call(
+        grad_mid_kernel, [struct((2, rows, 2 * HD), f32), pair16, dq_part],
+        [bias, stack(4), parts(4)], 20, *known, lse, both12, dq)
+    p1, p2 = call(merge_mid_kernel, [piece16, piece16], [], 0, p12_own, gather_pair(mid_other), back3, back4)
     back2 = shift(p2, -4)
     back1 = shift(p1, -2)
-    p0_own, p0_other, grad_queries = call(
-        grad_own_kernel, [piece32, piece16, struct((rows, width), bf16)],
-        [bias, stack(2), parts(2), pltpu.VMEM((width, rows), f32)], 10, *known, lse, both0, dq)
+    p0_own, grad_queries = call(
+        grad_own_kernel, [piece32, struct((rows, width), bf16)],
+        [bias, stack(1), parts(1), pltpu.VMEM((width, rows), f32)], 5, *known, lse, kv, dq)
     piece = struct((rows, HD), bf16)
-    grad_keys, grad_values = call(
-        final_kernel, [piece, piece], [], 0, p0_own, gather_pair(p0_other), back1, back2)
+    grad_keys, grad_values = call(final_kernel, [piece, piece], [], 0, p0_own, far_both, back2, back1)
     return grad_queries, grad_keys, grad_values
 
 

time: 71.9 us -> 70.2 us (0.976)
  the two profiles are of different devices: /device:TPU:162 before, /device:TPU:1 now
where the time goes in v4:
time: 70.2 us; the launch traced here: 69.8 us
  starting transfers between devices  35.2 us (50%)
  blocking collectives  15.8 us (23%)
  Pallas kernels  9.05 us (13%)
  waiting for transfers between devices  6.15 us (9%)
  local copies, waits for them, and re-layouts  1.7 us (2%)
  other arithmetic  1.04 us (1%)
  between operations  0.81 us (1%)
    ppermute x8, starting transfers between devices, shift(): return lax.ppermute(array, 'cp', pairs)  35.2 us
    all_gather x5, blocking collectives, gather_pair(): lax.all_gather(array, 'cp', axis_index_groups=[[i, i + 1] for i in range(...  15.8 us
    pallas_call x9, Pallas kernels, call(): pl.pallas_call(kernel, out_shape=outs, in_specs=[pl.BlockSpec(memory_spac...  9.05 us
    ppermute x8, waiting for transfers between devices, shift(): return lax.ppermute(array, 'cp', pairs)  6.15 us
    unnamed x12, local copies, waits for them, and re-layouts  1.7 us
  transfers between devices with their start and end apart: 8, of which 2 were waited for; matrix products, arithmetic and copies ran while one was open for 0% of the time, Pallas kernels for 9%

profile of v4, /device:TPU:1, one launch (start us, length us, event | category | flops | bytes accessed | tf_op | source)
XLA Modules:
  0.0 69.8 jit_solution(883790590188837420)
XLA Ops:
  0.6 0.0 copy-start
  0.7 1.0 %broadcast_select_fusion.kv_in = bf16[2,256,128]{2,1,0:T(8,128)(2,1)S(1)} fusion(pred[2]{0:T(512)(128)(4,1)S(1)} %iota_compare_fusion, bf16[256,128]{1,0:T(8,128)(2,1)} %param.9, bf16[256,128]{1,0:T(8,128)(2,1)} %param.8), kind=kLoop, calls=%fused_computation.1 | loop fusion | flops 65536 | bytes 262146 | tf_op jit(solution)/shard_map/jit(_where)/select_n | solution.py:291
  1.7 0.0 copy-start.4
  1.7 5.7 %collective-permute-start = (bf16[2,256,128]{2,1,0:T(8,128)(2,1)S(1)}, bf16[2,256,128]{2,1,0:T(8,128)(2,1)S(1)}, u32[]{:S(2)}, u32[]{:S(2)}) collective-permute-start(bf16[2,256,128]{2,1,0:T(8,128)(2,1)S(1)} %broadcast_select_fusion.kv_in), channel_id=1, source_target_pairs={{0,64},{16,80},{32,96},{48,112},{64,128},{80,144},{96,160},{112,17... | collective-permute-start | bytes 393224 | tf_op jit(solution)/shard_map/ppermute | solution.py:19
  7.4 4.7 %all-gather = bf16[4,256,128]{2,1,0:T(8,128)(2,1)S(1)} all-gather(bf16[2,256,128]{2,1,0:T(8,128)(2,1)S(1)} %broadcast_select_fusion.kv_in), channel_id=2, replica_groups={{0,16},{32,48},{64,80},{96,112},{128,144},{160,176},{192,208},{224,240}..., dimensions={0}, use_global_device_ids=true | all-gather | bytes 393216 | tf_op jit(solution)/shard_map/all_gather | solution.py:24
  12.1 0.0 copy-done
  12.1 0.0 copy-done.4
  12.1 0.0 copy-start.2
  12.1 1.0 %copy-done.2 = bf16[256,1024]{1,0:T(8,128)(2,1)S(1)} copy-done((bf16[256,1024]{1,0:T(8,128)(2,1)S(1)}, bf16[256,1024]{1,0:T(8,128)(2,1)}, u32[]{:S(2)}) %copy-start.2) | copy-done | bytes 524312
  13.2 0.0 copy-start.1
  13.2 1.2 %shard_map.94 = (s32[8,256]{1,0:T(8,128)S(1)}, f32[8,256]{1,0:T(8,128)S(1)}) custom-call(s32[51]{0:T(128)S(1)} %copy-done.4, bf16[256,1024]{1,0:T(8,128)(2,1)S(1)} %copy-done.2, bf16[256,1024]{1,0:T(8,128)(2,1)S(1)} %copy-done), custom_call_target="tpu_custom_call" | custom-call | flops 134217728 | bytes 1065164 | tf_op jit(solution)/shard_map/pallas_call | solution.py:262
  14.4 0.0 copy-start.5
  14.4 0.0 copy-done.1
  14.4 0.6 copy-done.5
  15.0 1.7 %shard_map.95 = (f32[8,256]{1,0:T(8,128)S(1)}, f32[8,256]{1,0:T(8,128)S(1)}) custom-call(bf16[256,1024]{1,0:T(8,128)(2,1)S(1)} %copy-done.1, s32[1,16]{1,0:T(1,128)S(1)} %copy-done.5, s32[8,256]{1,0:T(8,128)S(1)} %get-tuple-element.31.start_ref, bf16[2,2,256,128]{3,2,1,0:T(8,128)(2,1)S(1)} %bitcast.12), custom_call_target="tpu_custom_call" | custom-call | flops 268435456 | bytes 811072 | tf_op jit(solution)/shard_map/pallas_call | solution.py:262
  16.7 1.9 %collective-permute-start.1 = (bf16[2,256,128]{2,1,0:T(8,128)(2,1)S(1)}, bf16[2,256,128]{2,1,0:T(8,128)(2,1)S(1)}, u32[]{:S(2)}, u32[]{:S(2)}) collective-permute-start(bf16[2,256,128]{2,1,0:T(8,128)(2,1)S(1)} %broadcast_select_fusion.kv_in), channel_id=1, source_target_pairs={{0,32},{16,48},{32,64},{48,80},{64,96},{80,112},{96,128},{112,144}... | collective-permute-start | bytes 393224 | tf_op jit(solution)/shard_map/ppermute | solution.py:19
  18.7 0.0 collective-permute-done
  18.7 5.4 %collective-permute-start.3 = (bf16[2,256,128]{2,1,0:T(8,128)(2,1)S(1)}, bf16[2,256,128]{2,1,0:T(8,128)(2,1)S(1)}, u32[]{:S(2)}, u32[]{:S(2)}) collective-permute-start(bf16[2,256,128]{2,1,0:T(8,128)(2,1)S(1)} %collective-permute-done), channel_id=1, source_target_pairs={{16,64},{48,96},{80,128},{112,160},{144,192},{176,224},{208,256},{... | collective-permute-start | bytes 393224 | tf_op jit(solution)/shard_map/ppermute | solution.py:19
  24.1 3.6 %collective-permute-start.2 = (bf16[2,256,128]{2,1,0:T(8,128)(2,1)S(1)}, bf16[2,256,128]{2,1,0:T(8,128)(2,1)S(1)}, u32[]{:S(2)}, u32[]{:S(2)}) collective-permute-start(bf16[2,256,128]{2,1,0:T(8,128)(2,1)S(1)} %collective-permute-done), channel_id=1, source_target_pairs={{0,32},{16,48},{32,64},{48,80},{64,96},{80,112},{96,128},{112,144}... | collective-permute-start | bytes 393224 | tf_op jit(solution)/shard_map/ppermute | solution.py:19
  27.6 0.0 collective-permute-done.1
  27.7 2.2 %all-gather.1 = bf16[4,2,256,128]{3,2,1,0:T(8,128)(2,1)S(1)} all-gather(bf16[2,2,256,128]{3,2,1,0:T(8,128)(2,1)S(1)} %pad_maximum_fusion), channel_id=3, replica_groups={{0,16},{32,48},{64,80},{96,112},{128,144},{160,176},{192,208},{224,240}..., dimensions={0}, use_global_device_ids=true | all-gather | bytes 786432 | tf_op jit(solution)/shard_map/all_gather | solution.py:24
  29.8 0.0 copy-start.3
  29.8 0.2 shard_map.96
  30.1 2.8 %collective-permute-done.2 = bf16[2,256,128]{2,1,0:T(8,128)(2,1)S(1)} collective-permute-done((bf16[2,256,128]{2,1,0:T(8,128)(2,1)S(1)}, bf16[2,256,128]{2,1,0:T(8,128)(2,1)S(1)}, u32[]{:S(2)}, u32[]{:S(2)}) %collective-permute-start.2) | collective-permute-done | bytes 131104 | tf_op jit(solution)/shard_map/ppermute | solution.py:19
  32.8 2.0 %all-gather.2 = bf16[4,256,128]{2,1,0:T(8,128)(2,1)S(1)} all-gather(bf16[2,256,128]{2,1,0:T(8,128)(2,1)S(1)} %collective-permute-done.2), channel_id=4, replica_groups={{0,16},{32,48},{64,80},{96,112},{128,144},{160,176},{192,208},{224,240}..., dimensions={0}, use_global_device_ids=true | all-gather | bytes 393216 | tf_op jit(solution)/shard_map/all_gather | solution.py:24
  34.8 0.0 collective-permute-done.3.kv4
  34.8 0.0 copy-done.3
  34.8 2.0 %shard_map.97 = (f32[256,256]{1,0:T(8,128)S(1)}, bf16[2,256,256]{2,1,0:T(8,128)(2,1)S(1)}, bf16[256,256]{1,0:T(8,128)(2,1)S(1)}, f32[1024,256]{1,0:T(8,128)S(1)}, f32[8,256]{1,0:T(8,128)S(1)}) custom-call(bf16[256,1024]{1,0:T(8,128)(2,1)S(1)} %copy-done.1, bf16[256,1024]{1,0:T(8,128)(2,1)S(1)} %copy-done.3, s32[1,16]{1,0:T(1,128)S(1)} %copy-done.5, ...), custom_call_target="tpu_custom_call" | custom-call | flops 2684354560 | bytes 3448896 | tf_op jit(solution)/shard_map/pallas_call | solution.py:262
  36.8 1.3 %collective-permute-start.5 = (bf16[256,256]{1,0:T(8,128)(2,1)S(1)}, bf16[256,256]{1,0:T(8,128)(2,1)S(1)}, u32[]{:S(2)}, u32[]{:S(2)}) collective-permute-start(bf16[256,256]{1,0:T(8,128)(2,1)S(1)} %get-tuple-element.54), channel_id=1, source_target_pairs={{0,464},{32,496},{64,16},{96,48},{128,80},{160,112},{192,144},{224... | collective-permute-start | bytes 393224 | tf_op jit(solution)/shard_map/ppermute | solution.py:19
  38.1 4.5 %all-gather.3 = bf16[4,256,256]{2,1,0:T(8,128)(2,1)S(1)} all-gather(bf16[2,256,256]{2,1,0:T(8,128)(2,1)S(1)} %get-tuple-element.50), channel_id=5, replica_groups={{0,16},{32,48},{64,80},{96,112},{128,144},{160,176},{192,208},{224,240}..., dimensions={0}, use_global_device_ids=true | all-gather | bytes 786432 | tf_op jit(solution)/shard_map/all_gather | solution.py:24
  42.7 8.2 %collective-permute-start.4 = (bf16[256,256]{1,0:T(8,128)(2,1)S(1)}, bf16[256,256]{1,0:T(8,128)(2,1)S(1)}, u32[]{:S(2)}, u32[]{:S(2)}) collective-permute-start(bf16[256,256]{1,0:T(8,128)(2,1)S(1)} %shard_map.100), channel_id=1, source_target_pairs={{0,480},{16,496},{32,0},{48,16},{64,32},{80,48},{96,64},{112,80},{... | collective-permute-start | bytes 393224 | tf_op jit(solution)/shard_map/ppermute | solution.py:19
  50.9 0.4 shard_map.98
  51.3 2.5 %all-gather.4 = bf16[4,256,256]{2,1,0:T(8,128)(2,1)S(1)} all-gather(bf16[2,256,256]{2,1,0:T(8,128)(2,1)S(1)} %get-tuple-element.52), channel_id=6, replica_groups={{0,16},{32,48},{64,80},{96,112},{128,144},{160,176},{192,208},{224,240}..., dimensions={0}, use_global_device_ids=true | all-gather | bytes 786432 | tf_op jit(solution)/shard_map/all_gather | solution.py:24
  53.7 0.0 collective-permute-done.5.back4_ref
  53.7 0.0 collective-permute-done.4.back3_ref
  53.7 0.1 shard_map.101
  53.8 3.8 %collective-permute-start.6 = (bf16[256,256]{1,0:T(8,128)(2,1)S(1)}, bf16[256,256]{1,0:T(8,128)(2,1)S(1)}, u32[]{:S(2)}, u32[]{:S(2)}) collective-permute-start(bf16[256,256]{1,0:T(8,128)(2,1)S(1)} %get-tuple-element.55), channel_id=1, source_target_pairs={{0,448},{16,464},{32,480},{48,496},{64,0},{80,16},{96,32},{112,48}... | collective-permute-start | bytes 393224 | tf_op jit(solution)/shard_map/ppermute | solution.py:19
  57.7 5.3 %collective-permute-start.7 = (bf16[256,256]{1,0:T(8,128)(2,1)S(1)}, bf16[256,256]{1,0:T(8,128)(2,1)S(1)}, u32[]{:S(2)}, u32[]{:S(2)}) collective-permute-start(bf16[256,256]{1,0:T(8,128)(2,1)S(1)} %get-tuple-element.56), channel_id=1, source_target_pairs={{0,480},{16,496},{32,0},{48,16},{64,32},{80,48},{96,64},{112,80},{... | collective-permute-start | bytes 393224 | tf_op jit(solution)/shard_map/ppermute | solution.py:19
  62.9 2.8 %shard_map.99 = (f32[256,256]{1,0:T(8,128)S(1)}, bf16[256,1024]{1,0:T(8,128)(2,1)}) custom-call(bf16[256,1024]{1,0:T(8,128)(2,1)S(1)} %copy-done.1, bf16[256,1024]{1,0:T(8,128)(2,1)S(1)} %copy-done.3, s32[1,16]{1,0:T(1,128)S(1)} %copy-done.5, s32[8,256]{1,0:T(8,128)S(1)} %get-tuple-element.31.start_ref, f32[8,256]{1,0:T(8,128)S(1)} %get-tuple-element.38.delta_ref, ...), custom_call_target="tpu_custom_call" | custom-call | flops 671088640 | bytes 3039296 | tf_op jit(solution)/shard_map/pallas_call | solution.py:262
  65.7 0.0 collective-permute-done.6.back2_ref
  65.7 3.4 %collective-permute-done.7.back1_ref = bf16[256,256]{1,0:T(8,128)(2,1)S(1)} collective-permute-done((bf16[256,256]{1,0:T(8,128)(2,1)S(1)}, bf16[256,256]{1,0:T(8,128)(2,1)S(1)}, u32[]{:S(2)}, u32[]{:S(2)}) %collective-permute-start.7) | collective-permute-done | bytes 131104 | tf_op jit(solution)/shard_map/ppermute | solution.py:19
  69.1 0.7 shard_map.102
  (3 shorter events, 0.1 us)
Async XLA Ops:
  0.6 11.5 %copy-start = (bf16[256,1024]{1,0:T(8,128)(2,1)S(1)}, bf16[256,1024]{1,0:T(8,128)(2,1)}, u32[]{:S(2)}) copy-start(bf16[256,1024]{1,0:T(8,128)(2,1)} %o_ref.1) | copy-start | bytes 1572868
  1.7 10.5 %copy-start.4 = (s32[51]{0:T(128)S(1)}, s32[51]{0:T(128)}, u32[]{:S(2)}) copy-start(s32[51]{0:T(128)} %doc_ref.1) | copy-start | bytes 616
  1.7 17.0 %collective-permute-start = (bf16[2,256,128]{2,1,0:T(8,128)(2,1)S(1)}, bf16[2,256,128]{2,1,0:T(8,128)(2,1)S(1)}, u32[]{:S(2)}, u32[]{:S(2)}) collective-permute-start(bf16[2,256,128]{2,1,0:T(8,128)(2,1)S(1)} %broadcast_select_fusion.kv_in), channel_id=1, source_target_pairs={{0,64},{16,80},{32,96},{48,112},{64,128},{80,144},{96,160},{112,17... | collective-permute-start | bytes 393224 | tf_op jit(solution)/shard_map/ppermute | solution.py:19
  12.1 1.0 %copy-start.2 = (bf16[256,1024]{1,0:T(8,128)(2,1)S(1)}, bf16[256,1024]{1,0:T(8,128)(2,1)}, u32[]{:S(2)}) copy-start(bf16[256,1024]{1,0:T(8,128)(2,1)} %g_ref.7) | copy-start | bytes 1572868
  13.2 1.2 %copy-start.1 = (bf16[256,1024]{1,0:T(8,128)(2,1)S(1)}, bf16[256,1024]{1,0:T(8,128)(2,1)}, u32[]{:S(2)}) copy-start(bf16[256,1024]{1,0:T(8,128)(2,1)} %q_ref.9) | copy-start | bytes 1572868
  14.4 0.7 copy-start.5
  16.7 10.9 %collective-permute-start.1 = (bf16[2,256,128]{2,1,0:T(8,128)(2,1)S(1)}, bf16[2,256,128]{2,1,0:T(8,128)(2,1)S(1)}, u32[]{:S(2)}, u32[]{:S(2)}) collective-permute-start(bf16[2,256,128]{2,1,0:T(8,128)(2,1)S(1)} %broadcast_select_fusion.kv_in), channel_id=1, source_target_pairs={{0,32},{16,48},{32,64},{48,80},{64,96},{80,112},{96,128},{112,144}... | collective-permute-start | bytes 393224 | tf_op jit(solution)/shard_map/ppermute | solution.py:19
  18.7 16.2 %collective-permute-start.3 = (bf16[2,256,128]{2,1,0:T(8,128)(2,1)S(1)}, bf16[2,256,128]{2,1,0:T(8,128)(2,1)S(1)}, u32[]{:S(2)}, u32[]{:S(2)}) collective-permute-start(bf16[2,256,128]{2,1,0:T(8,128)(2,1)S(1)} %collective-permute-done), channel_id=1, source_target_pairs={{16,64},{48,96},{80,128},{112,160},{144,192},{176,224},{208,256},{... | collective-permute-start | bytes 393224 | tf_op jit(solution)/shard_map/ppermute | solution.py:19
  24.1 8.8 %collective-permute-start.2 = (bf16[2,256,128]{2,1,0:T(8,128)(2,1)S(1)}, bf16[2,256,128]{2,1,0:T(8,128)(2,1)S(1)}, u32[]{:S(2)}, u32[]{:S(2)}) collective-permute-start(bf16[2,256,128]{2,1,0:T(8,128)(2,1)S(1)} %collective-permute-done), channel_id=1, source_target_pairs={{0,32},{16,48},{32,64},{48,80},{64,96},{80,112},{96,128},{112,144}... | collective-permute-start | bytes 393224 | tf_op jit(solution)/shard_map/ppermute | solution.py:19
  29.8 5.0 %copy-start.3 = (bf16[256,1024]{1,0:T(8,128)(2,1)S(1)}, bf16[256,1024]{1,0:T(8,128)(2,1)}, u32[]{:S(2)}) copy-start(bf16[256,1024]{1,0:T(8,128)(2,1)} %g_ref.7) | copy-start | bytes 1572868
  36.8 16.9 %collective-permute-start.5 = (bf16[256,256]{1,0:T(8,128)(2,1)S(1)}, bf16[256,256]{1,0:T(8,128)(2,1)S(1)}, u32[]{:S(2)}, u32[]{:S(2)}) collective-permute-start(bf16[256,256]{1,0:T(8,128)(2,1)S(1)} %get-tuple-element.54), channel_id=1, source_target_pairs={{0,464},{32,496},{64,16},{96,48},{128,80},{160,112},{192,144},{224... | collective-permute-start | bytes 393224 | tf_op jit(solution)/shard_map/ppermute | solution.py:19
  42.7 11.1 %collective-permute-start.4 = (bf16[256,256]{1,0:T(8,128)(2,1)S(1)}, bf16[256,256]{1,0:T(8,128)(2,1)S(1)}, u32[]{:S(2)}, u32[]{:S(2)}) collective-permute-start(bf16[256,256]{1,0:T(8,128)(2,1)S(1)} %shard_map.100), channel_id=1, source_target_pairs={{0,480},{16,496},{32,0},{48,16},{64,32},{80,48},{96,64},{112,80},{... | collective-permute-start | bytes 393224 | tf_op jit(solution)/shard_map/ppermute | solution.py:19
  53.8 11.9 %collective-permute-start.6 = (bf16[256,256]{1,0:T(8,128)(2,1)S(1)}, bf16[256,256]{1,0:T(8,128)(2,1)S(1)}, u32[]{:S(2)}, u32[]{:S(2)}) collective-permute-start(bf16[256,256]{1,0:T(8,128)(2,1)S(1)} %get-tuple-element.55), channel_id=1, source_target_pairs={{0,448},{16,464},{32,480},{48,496},{64,0},{80,16},{96,32},{112,48}... | collective-permute-start | bytes 393224 | tf_op jit(solution)/shard_map/ppermute | solution.py:19
  57.7 11.4 %collective-permute-start.7 = (bf16[256,256]{1,0:T(8,128)(2,1)S(1)}, bf16[256,256]{1,0:T(8,128)(2,1)S(1)}, u32[]{:S(2)}, u32[]{:S(2)}) collective-permute-start(bf16[256,256]{1,0:T(8,128)(2,1)S(1)} %get-tuple-element.56), channel_id=1, source_target_pairs={{0,480},{16,496},{32,0},{48,16},{64,32},{80,48},{96,64},{112,80},{... | collective-permute-start | bytes 393224 | tf_op jit(solution)/shard_map/ppermute | solution.py:19

commit v5 on v4

--- a/solution.py
+++ b/solution.py
@@ -135,12 +135,15 @@
 
 def grad_entries(key_blocks, bits, kv_ref, q_ref, g_ref, start_ref, lse_ref, delta_ref, dq_ref, bias_ref, part_ref):
     heads = lse_ref.shape[0]
-    part_ref[...] = jnp.zeros_like(part_ref)
-
     def step(i, carry):
         key = pick(key_blocks, i)
-
-        @pl.when(listed(bits, key))
+        present = listed(bits, key)
+
+        @pl.when(jnp.logical_not(present))
+        def _():
+            part_ref[i] = jnp.zeros(part_ref.shape[1:], part_ref.dtype)
+
+        @pl.when(present)
         def _():
             write_bias(bias_ref, start_ref, key)
             keys = kv_ref[i, 0]
@@ -209,17 +212,29 @@
 
 
 def grad_mid_kernel(q_ref, g_ref, off_ref, start_ref, delta_ref, lse_ref, kv12, dq_in,
-                    p_own, p_other, dq_ref, bias_ref, kv_ref, part_ref):
-    for i in range(4):
-        kv_ref[i] = kv12[1 - i % 2, i // 2]
-    dq_ref[...] = dq_in[...]
-    keys = [key_block(1, i) for i in range(4)]
+                    p2_own, p_other, dq_ref, bias_ref, kv_ref, part_ref):
+    del dq_in
+    core = core_parity()
+    kv_ref[0] = kv12[1, 1]
+    kv_ref[1] = kv12[0, 1]
+    kv_ref[2] = kv12[1 - core, 0]
+    keys = [key_block(2, 0), key_block(2, 1), key_block(1, core)]
     bits = listed_bits(off_ref)
     grad_entries(keys, bits, kv_ref, q_ref, g_ref, start_ref, lse_ref, delta_ref, dq_ref, bias_ref, part_ref)
+    p2_own[...] = part_ref[1 - core]
+    p_other[0] = part_ref[2].astype(p_other.dtype)
+    p_other[1] = part_ref[core].astype(p_other.dtype)
+
+
+def grad_near_kernel(q_ref, g_ref, off_ref, start_ref, delta_ref, lse_ref, kv_in, gathered_ref, dq_in,
+                     p1_ref, dq_ref, bias_ref, kv_ref, part_ref):
+    del dq_in
     core = core_parity()
-    for i in range(2):
-        p_own[i] = part_ref[2 * i + 1 - core]
-        p_other[i] = part_ref[2 * i + core].astype(p_other.dtype)
+    kv_ref[0] = kv_in[...]
+    keys = [key_block(1, 1 - core)]
+    bits = listed_bits(off_ref)
+    grad_entries(keys, bits, kv_ref, q_ref, g_ref, start_ref, lse_ref, delta_ref, dq_ref, bias_ref, part_ref)
+    p1_ref[...] = (part_ref[0] + gathered_ref[1 - core, 0].astype(jnp.float32)).astype(p1_ref.dtype)
 
 
 def grad_own_kernel(q_ref, g_ref, off_ref, start_ref, delta_ref, lse_ref, kv_in, dq_in,
@@ -240,22 +255,20 @@
     out_ref[...] = total.astype(out_ref.dtype)
 
 
-def merge_mid_kernel(own_ref, gathered_ref, back3_ref, back4_ref, p1_ref, p2_ref):
-    other = gathered_ref.at[1 - core_parity()]
-    p1_ref[...] = (own_ref[0] + other[0].astype(jnp.float32)).astype(p1_ref.dtype)
-    total = own_ref[1] + other[1].astype(jnp.float32)
+def merge_mid_kernel(own_ref, gathered_ref, back3_ref, back4_ref, p2_ref):
+    total = own_ref[...] + gathered_ref[1 - core_parity(), 1].astype(jnp.float32)
     total += back3_ref[...].astype(jnp.float32) + back4_ref[...].astype(jnp.float32)
     p2_ref[...] = total.astype(p2_ref.dtype)
 
 
-def final_kernel(own_ref, gathered_ref, back2_ref, back1_ref, dk_ref, dv_ref):
+def final_kernel(own_ref, gathered_ref, back1_ref, dk_ref, dv_ref):
     total = own_ref[...] + gathered_ref[1 - core_parity(), 1].astype(jnp.float32)
-    total += back1_ref[...].astype(jnp.float32) + back2_ref[...].astype(jnp.float32)
+    total += back1_ref[...].astype(jnp.float32)
     dk_ref[...] = total[:, 0:HD].astype(dk_ref.dtype)
     dv_ref[...] = total[:, HD:].astype(dv_ref.dtype)
 
 
-def call(kernel, outs, scratch, units, *args, smem_args=0):
+def call(kernel, outs, scratch, units, *args, smem_args=0, aliases=None):
     pair = 2 * 8 * 256 * 256
     moved = sum(a.size * a.dtype.itemsize for a in args) + sum(o.size * o.dtype.itemsize for o in outs)
     spaces = [pltpu.SMEM] * smem_args + [pltpu.VMEM] * (len(args) - smem_args)
@@ -265,6 +278,7 @@
         in_specs=[pl.BlockSpec(memory_space=space) for space in spaces],
         out_specs=[pl.BlockSpec(memory_space=pltpu.VMEM) for _ in outs],
         scratch_shapes=scratch,
+        input_output_aliases=aliases or {},
         compiler_params=pltpu.CompilerParams(vmem_limit_bytes=VMEM_BYTES),
         cost_estimate=pl.CostEstimate(flops=units * pair * HD, bytes_accessed=moved, transcendentals=pair),
     )(*args)
@@ -315,17 +329,21 @@
     far_both = gather_pair(far_other)
     (p3,) = call(merge_far_kernel, [piece16], [], 0, p3_own, far_both)
     back3 = shift(p3, -2)
-    p12_own, mid_other, dq = call(
-        grad_mid_kernel, [struct((2, rows, 2 * HD), f32), pair16, dq_part],
-        [bias, stack(4), parts(4)], 20, *known, lse, both12, dq)
-    p1, p2 = call(merge_mid_kernel, [piece16, piece16], [], 0, p12_own, gather_pair(mid_other), back3, back4)
+    p2_own, mid_other, dq = call(
+        grad_mid_kernel, [piece32, pair16, dq_part], [bias, stack(3), parts(3)], 15,
+        *known, lse, both12, dq, aliases={7: 2})
+    mid_both = gather_pair(mid_other)
+    (p2,) = call(merge_mid_kernel, [piece16], [], 0, p2_own, mid_both, back3, back4)
     back2 = shift(p2, -4)
+    p1, dq = call(
+        grad_near_kernel, [piece16, dq_part], [bias, stack(1), parts(1)], 5,
+        *known, lse, kv1, mid_both, dq, aliases={8: 1})
     back1 = shift(p1, -2)
     p0_own, grad_queries = call(
         grad_own_kernel, [piece32, struct((rows, width), bf16)],
         [bias, stack(1), parts(1), pltpu.VMEM((width, rows), f32)], 5, *known, lse, kv, dq)
     piece = struct((rows, HD), bf16)
-    grad_keys, grad_values = call(final_kernel, [piece, piece], [], 0, p0_own, far_both, back2, back1)
+    grad_keys, grad_values = call(final_kernel, [piece, piece], [], 0, p0_own + back2.astype(f32), far_both, back1)
     return grad_queries, grad_keys, grad_values
 
 

time: 70.2 us -> 66.9 us (0.953)
  the two profiles are of different devices: /device:TPU:1 before, /device:TPU:98 now
where the time goes in v5:
time: 66.9 us; the launch traced here: 66.5 us
  starting transfers between devices  22.4 us (33%)
  Pallas kernels  16 us (24%)
  blocking collectives  15.7 us (23%)
  waiting for transfers between devices  8.85 us (13%)
  local copies, waits for them, and re-layouts  1.7 us (3%)
  other arithmetic  1.07 us (2%)
  between operations  0.82 us (1%)
    ppermute x8, starting transfers between devices, shift(): return lax.ppermute(array, 'cp', pairs)  22.4 us
    pallas_call x10, Pallas kernels, call(): pl.pallas_call(kernel, out_shape=outs, in_specs=[pl.BlockSpec(memory_spac...  16 us
    all_gather x5, blocking collectives, gather_pair(): lax.all_gather(array, 'cp', axis_index_groups=[[i, i + 1] for i in range(...  15.7 us
    ppermute x8, waiting for transfers between devices, shift(): return lax.ppermute(array, 'cp', pairs)  8.85 us
    unnamed x10, local copies, waits for them, and re-layouts  1.7 us
  transfers between devices with their start and end apart: 8, of which 3 were waited for; matrix products, arithmetic and copies ran while one was open for 0% of the time, Pallas kernels for 22%

profile of v5, /device:TPU:98, one launch (start us, length us, event | category | flops | bytes accessed | tf_op | source)
XLA Modules:
  0.0 66.5 jit_solution(9041829100849708951)
XLA Ops:
  0.6 0.0 copy-start.1
  0.7 1.0 %broadcast_select_fusion.kv_in = bf16[2,256,128]{2,1,0:T(8,128)(2,1)S(1)} fusion(pred[2]{0:T(512)(128)(4,1)S(1)} %iota_compare_fusion, bf16[256,128]{1,0:T(8,128)(2,1)} %param.9, bf16[256,128]{1,0:T(8,128)(2,1)} %param.8), kind=kLoop, calls=%fused_computation.2 | loop fusion | flops 65536 | bytes 262146 | tf_op jit(solution)/shard_map/jit(_where)/select_n | solution.py:305
  1.7 0.0 copy-start.4
  1.7 6.4 %collective-permute-start = (bf16[2,256,128]{2,1,0:T(8,128)(2,1)S(1)}, bf16[2,256,128]{2,1,0:T(8,128)(2,1)S(1)}, u32[]{:S(2)}, u32[]{:S(2)}) collective-permute-start(bf16[2,256,128]{2,1,0:T(8,128)(2,1)S(1)} %broadcast_select_fusion.kv_in), channel_id=1, source_target_pairs={{0,64},{16,80},{32,96},{48,112},{64,128},{80,144},{96,160},{112,17... | collective-permute-start | bytes 393224 | tf_op jit(solution)/shard_map/ppermute | solution.py:19
  8.1 2.0 %all-gather = bf16[4,256,128]{2,1,0:T(8,128)(2,1)S(1)} all-gather(bf16[2,256,128]{2,1,0:T(8,128)(2,1)S(1)} %broadcast_select_fusion.kv_in), channel_id=2, replica_groups={{0,16},{32,48},{64,80},{96,112},{128,144},{160,176},{192,208},{224,240}..., dimensions={0}, use_global_device_ids=true | all-gather | bytes 393216 | tf_op jit(solution)/shard_map/all_gather | solution.py:24
  10.1 0.0 copy-done.1
  10.1 0.0 copy-done.4
  10.1 0.0 copy-start.3
  10.1 1.0 %copy-done.3 = bf16[256,1024]{1,0:T(8,128)(2,1)S(1)} copy-done((bf16[256,1024]{1,0:T(8,128)(2,1)S(1)}, bf16[256,1024]{1,0:T(8,128)(2,1)}, u32[]{:S(2)}) %copy-start.3) | copy-done | bytes 524312
  11.1 0.0 copy-start
  11.1 1.2 %shard_map.94 = (s32[8,256]{1,0:T(8,128)S(1)}, f32[8,256]{1,0:T(8,128)S(1)}) custom-call(s32[51]{0:T(128)S(1)} %copy-done.4, bf16[256,1024]{1,0:T(8,128)(2,1)S(1)} %copy-done.1, bf16[256,1024]{1,0:T(8,128)(2,1)S(1)} %copy-done.3), custom_call_target="tpu_custom_call" | custom-call | flops 134217728 | bytes 1065164 | tf_op jit(solution)/shard_map/pallas_call | solution.py:275
  12.3 0.0 copy-start.2
  12.3 0.0 copy-done
  12.3 0.6 copy-done.2
  13.0 0.9 %shard_map.95 = (f32[8,256]{1,0:T(8,128)S(1)}, f32[8,256]{1,0:T(8,128)S(1)}) custom-call(bf16[256,1024]{1,0:T(8,128)(2,1)S(1)} %copy-done, s32[1,16]{1,0:T(1,128)S(1)} %copy-done.2, s32[8,256]{1,0:T(8,128)S(1)} %get-tuple-element.31.start_ref, bf16[2,2,256,128]{3,2,1,0:T(8,128)(2,1)S(1)} %bitcast.14), custom_call_target="tpu_custom_call" | custom-call | flops 268435456 | bytes 811072 | tf_op jit(solution)/shard_map/pallas_call | solution.py:275
  13.9 3.8 %collective-permute-start.1 = (bf16[2,256,128]{2,1,0:T(8,128)(2,1)S(1)}, bf16[2,256,128]{2,1,0:T(8,128)(2,1)S(1)}, u32[]{:S(2)}, u32[]{:S(2)}) collective-permute-start(bf16[2,256,128]{2,1,0:T(8,128)(2,1)S(1)} %broadcast_select_fusion.kv_in), channel_id=1, source_target_pairs={{0,32},{16,48},{32,64},{48,80},{64,96},{80,112},{96,128},{112,144}... | collective-permute-start | bytes 393224 | tf_op jit(solution)/shard_map/ppermute | solution.py:19
  17.7 0.0 collective-permute-done
  17.8 1.3 %collective-permute-start.3 = (bf16[2,256,128]{2,1,0:T(8,128)(2,1)S(1)}, bf16[2,256,128]{2,1,0:T(8,128)(2,1)S(1)}, u32[]{:S(2)}, u32[]{:S(2)}) collective-permute-start(bf16[2,256,128]{2,1,0:T(8,128)(2,1)S(1)} %collective-permute-done), channel_id=1, source_target_pairs={{16,64},{48,96},{80,128},{112,160},{144,192},{176,224},{208,256},{... | collective-permute-start | bytes 393224 | tf_op jit(solution)/shard_map/ppermute | solution.py:19
  19.1 3.8 %collective-permute-start.2 = (bf16[2,256,128]{2,1,0:T(8,128)(2,1)S(1)}, bf16[2,256,128]{2,1,0:T(8,128)(2,1)S(1)}, u32[]{:S(2)}, u32[]{:S(2)}) collective-permute-start(bf16[2,256,128]{2,1,0:T(8,128)(2,1)S(1)} %collective-permute-done), channel_id=1, source_target_pairs={{0,32},{16,48},{32,64},{48,80},{64,96},{80,112},{96,128},{112,144}... | collective-permute-start | bytes 393224 | tf_op jit(solution)/shard_map/ppermute | solution.py:19
  22.9 0.0 collective-permute-done.1.kv_in
  22.9 5.8 %all-gather.1 = bf16[4,2,256,128]{3,2,1,0:T(8,128)(2,1)S(1)} all-gather(bf16[2,2,256,128]{3,2,1,0:T(8,128)(2,1)S(1)} %pad_maximum_fusion), channel_id=3, replica_groups={{0,16},{32,48},{64,80},{96,112},{128,144},{160,176},{192,208},{224,240}..., dimensions={0}, use_global_device_ids=true | all-gather | bytes 786432 | tf_op jit(solution)/shard_map/all_gather | solution.py:24
  28.8 3.3 %shard_map.96 = (f32[8,256]{1,0:T(8,128)S(1)}, f32[8,256]{1,0:T(8,128)S(1)}) custom-call(bf16[256,1024]{1,0:T(8,128)(2,1)S(1)} %copy-done, s32[1,16]{1,0:T(1,128)S(1)} %copy-done.2, s32[8,256]{1,0:T(8,128)S(1)} %get-tuple-element.31.start_ref, f32[8,256]{1,0:T(8,128)S(1)} %get-tuple-element.39.m_in, f32[8,256]{1,0:T(8,128)S(1)} %get-tuple-element.40.l_in, ...), custom_call_target="tpu_custom_call" | custom-call | flops 536870912 | bytes 1089600 | tf_op jit(solution)/shard_map/pallas_call | solution.py:275
  32.1 0.0 collective-permute-done.2
  32.1 2.0 %all-gather.2 = bf16[4,256,128]{2,1,0:T(8,128)(2,1)S(1)} all-gather(bf16[2,256,128]{2,1,0:T(8,128)(2,1)S(1)} %collective-permute-done.2), channel_id=4, replica_groups={{0,16},{32,48},{64,80},{96,112},{128,144},{160,176},{192,208},{224,240}..., dimensions={0}, use_global_device_ids=true | all-gather | bytes 393216 | tf_op jit(solution)/shard_map/all_gather | solution.py:24
  34.1 0.0 collective-permute-done.3.kv4
  34.1 0.4 shard_map.97
  34.5 1.3 %collective-permute-start.5 = (bf16[256,256]{1,0:T(8,128)(2,1)S(1)}, bf16[256,256]{1,0:T(8,128)(2,1)S(1)}, u32[]{:S(2)}, u32[]{:S(2)}) collective-permute-start(bf16[256,256]{1,0:T(8,128)(2,1)S(1)} %get-tuple-element.55), channel_id=1, source_target_pairs={{0,464},{32,496},{64,16},{96,48},{128,80},{160,112},{192,144},{224... | collective-permute-start | bytes 393224 | tf_op jit(solution)/shard_map/ppermute | solution.py:19
  35.8 3.7 %all-gather.4 = bf16[4,256,256]{2,1,0:T(8,128)(2,1)S(1)} all-gather(bf16[2,256,256]{2,1,0:T(8,128)(2,1)S(1)} %get-tuple-element.54), channel_id=6, replica_groups={{0,16},{32,48},{64,80},{96,112},{128,144},{160,176},{192,208},{224,240}..., dimensions={0}, use_global_device_ids=true | all-gather | bytes 786432 | tf_op jit(solution)/shard_map/all_gather | solution.py:24
  39.5 1.9 %collective-permute-start.4 = (bf16[256,256]{1,0:T(8,128)(2,1)S(1)}, bf16[256,256]{1,0:T(8,128)(2,1)S(1)}, u32[]{:S(2)}, u32[]{:S(2)}) collective-permute-start(bf16[256,256]{1,0:T(8,128)(2,1)S(1)} %shard_map.101), channel_id=1, source_target_pairs={{0,480},{16,496},{32,0},{48,16},{64,32},{80,48},{96,64},{112,80},{... | collective-permute-start | bytes 393224 | tf_op jit(solution)/shard_map/ppermute | solution.py:19
  41.5 4.9 %shard_map.98 = (f32[256,256]{1,0:T(8,128)S(1)}, bf16[2,256,256]{2,1,0:T(8,128)(2,1)S(1)}, f32[1024,256]{1,0:T(8,128)S(1)}) custom-call(bf16[256,1024]{1,0:T(8,128)(2,1)S(1)} %copy-done, bf16[256,1024]{1,0:T(8,128)(2,1)S(1)} %copy-done.1, s32[1,16]{1,0:T(1,128)S(1)} %copy-done.2, ...), custom_call_target="tpu_custom_call", output_to_operand_aliasing={{2}: (7, {})} | custom-call | flops 2013265920 | bytes 4218944 | tf_op jit(solution)/shard_map/pallas_call | solution.py:275
  46.4 2.2 %all-gather.3 = bf16[4,256,256]{2,1,0:T(8,128)(2,1)S(1)} all-gather(bf16[2,256,256]{2,1,0:T(8,128)(2,1)S(1)} %get-tuple-element.47), channel_id=5, replica_groups={{0,16},{32,48},{64,80},{96,112},{128,144},{160,176},{192,208},{224,240}..., dimensions={0}, use_global_device_ids=true | all-gather | bytes 786432 | tf_op jit(solution)/shard_map/all_gather | solution.py:24
  48.6 0.0 collective-permute-done.5.back4_ref
  48.6 2.5 %collective-permute-done.4.back3_ref = bf16[256,256]{1,0:T(8,128)(2,1)S(1)} collective-permute-done((bf16[256,256]{1,0:T(8,128)(2,1)S(1)}, bf16[256,256]{1,0:T(8,128)(2,1)S(1)}, u32[]{:S(2)}, u32[]{:S(2)}) %collective-permute-start.4) | collective-permute-done | bytes 131104 | tf_op jit(solution)/shard_map/ppermute | solution.py:19
  51.1 0.1 shard_map.102
  51.2 1.9 %collective-permute-start.6 = (bf16[256,256]{1,0:T(8,128)(2,1)S(1)}, bf16[256,256]{1,0:T(8,128)(2,1)S(1)}, u32[]{:S(2)}, u32[]{:S(2)}) collective-permute-start(bf16[256,256]{1,0:T(8,128)(2,1)S(1)} %shard_map.102), channel_id=1, source_target_pairs={{0,448},{16,464},{32,480},{48,496},{64,0},{80,16},{96,32},{112,48}... | collective-permute-start | bytes 393224 | tf_op jit(solution)/shard_map/ppermute | solution.py:19
  53.1 1.7 %shard_map.99 = (bf16[256,256]{1,0:T(8,128)(2,1)S(1)}, f32[1024,256]{1,0:T(8,128)S(1)}) custom-call(bf16[256,1024]{1,0:T(8,128)(2,1)S(1)} %copy-done, bf16[256,1024]{1,0:T(8,128)(2,1)S(1)} %copy-done.1, s32[1,16]{1,0:T(1,128)S(1)} %copy-done.2, s32[8,256]{1,0:T(8,128)S(1)} %get-tuple-element.31.start_ref, ...), custom_call_target="tpu_custom_call", output_to_operand_aliasing={{1}: (8, {})} | custom-call | flops 671088640 | bytes 3956800 | tf_op jit(solution)/shard_map/pallas_call | solution.py:275
  54.8 1.9 %collective-permute-start.7 = (bf16[256,256]{1,0:T(8,128)(2,1)S(1)}, bf16[256,256]{1,0:T(8,128)(2,1)S(1)}, u32[]{:S(2)}, u32[]{:S(2)}) collective-permute-start(bf16[256,256]{1,0:T(8,128)(2,1)S(1)} %get-tuple-element.56), channel_id=1, source_target_pairs={{0,480},{16,496},{32,0},{48,16},{64,32},{80,48},{96,64},{112,80},{... | collective-permute-start | bytes 393224 | tf_op jit(solution)/shard_map/ppermute | solution.py:19
  56.7 2.8 %shard_map.100 = (f32[256,256]{1,0:T(8,128)S(1)}, bf16[256,1024]{1,0:T(8,128)(2,1)}) custom-call(bf16[256,1024]{1,0:T(8,128)(2,1)S(1)} %copy-done, bf16[256,1024]{1,0:T(8,128)(2,1)S(1)} %copy-done.1, s32[1,16]{1,0:T(1,128)S(1)} %copy-done.2, s32[8,256]{1,0:T(8,128)S(1)} %get-tuple-element.31.start_ref, f32[8,256]{1,0:T(8,128)S(1)} %get-tuple-element.38.delta_ref, ...), custom_call_target="tpu_custom_call" | custom-call | flops 671088640 | bytes 3039296 | tf_op jit(solution)/shard_map/pallas_call | solution.py:275
  59.5 1.0 %collective-permute-done.6 = bf16[256,256]{1,0:T(8,128)(2,1)S(1)} collective-permute-done((bf16[256,256]{1,0:T(8,128)(2,1)S(1)}, bf16[256,256]{1,0:T(8,128)(2,1)S(1)}, u32[]{:S(2)}, u32[]{:S(2)}) %collective-permute-start.6) | collective-permute-done | bytes 131104 | tf_op jit(solution)/shard_map/ppermute | solution.py:19
  60.5 5.3 %collective-permute-done.7.back1_ref = bf16[256,256]{1,0:T(8,128)(2,1)S(1)} collective-permute-done((bf16[256,256]{1,0:T(8,128)(2,1)S(1)}, bf16[256,256]{1,0:T(8,128)(2,1)S(1)}, u32[]{:S(2)}, u32[]{:S(2)}) %collective-permute-start.7) | collective-permute-done | bytes 131104 | tf_op jit(solution)/shard_map/ppermute | solution.py:19
  65.8 0.7 %shard_map.103 = (bf16[256,128]{1,0:T(8,128)(2,1)}, bf16[256,128]{1,0:T(8,128)(2,1)}) custom-call(f32[256,256]{1,0:T(8,128)S(1)} %convert_add_fusion.own_ref, bf16[2,2,256,256]{3,2,1,0:T(8,128)(2,1)S(1)} %bitcast.10, bf16[256,256]{1,0:T(8,128)(2,1)S(1)} %collective-permute-done.7.back1_ref), custom_call_target="tpu_custom_call" | custom-call | bytes 1048576 | tf_op jit(solution)/shard_map/pallas_call | solution.py:275
  (4 shorter events, 0.1 us)
Async XLA Ops:
  0.6 9.4 %copy-start.1 = (bf16[256,1024]{1,0:T(8,128)(2,1)S(1)}, bf16[256,1024]{1,0:T(8,128)(2,1)}, u32[]{:S(2)}) copy-start(bf16[256,1024]{1,0:T(8,128)(2,1)} %g_ref.9) | copy-start | bytes 1572868
  1.7 8.4 %copy-start.4 = (s32[51]{0:T(128)S(1)}, s32[51]{0:T(128)}, u32[]{:S(2)}) copy-start(s32[51]{0:T(128)} %doc_ref.1) | copy-start | bytes 616
  1.7 16.1 %collective-permute-start = (bf16[2,256,128]{2,1,0:T(8,128)(2,1)S(1)}, bf16[2,256,128]{2,1,0:T(8,128)(2,1)S(1)}, u32[]{:S(2)}, u32[]{:S(2)}) collective-permute-start(bf16[2,256,128]{2,1,0:T(8,128)(2,1)S(1)} %broadcast_select_fusion.kv_in), channel_id=1, source_target_pairs={{0,64},{16,80},{32,96},{48,112},{64,128},{80,144},{96,160},{112,17... | collective-permute-start | bytes 393224 | tf_op jit(solution)/shard_map/ppermute | solution.py:19
  10.1 1.0 %copy-start.3 = (bf16[256,1024]{1,0:T(8,128)(2,1)S(1)}, bf16[256,1024]{1,0:T(8,128)(2,1)}, u32[]{:S(2)}) copy-start(bf16[256,1024]{1,0:T(8,128)(2,1)} %o_ref.1) | copy-start | bytes 1572868
  11.1 1.2 %copy-start = (bf16[256,1024]{1,0:T(8,128)(2,1)S(1)}, bf16[256,1024]{1,0:T(8,128)(2,1)}, u32[]{:S(2)}) copy-start(bf16[256,1024]{1,0:T(8,128)(2,1)} %q_ref.11) | copy-start | bytes 1572868
  12.3 0.7 copy-start.2
  13.9 9.0 %collective-permute-start.1 = (bf16[2,256,128]{2,1,0:T(8,128)(2,1)S(1)}, bf16[2,256,128]{2,1,0:T(8,128)(2,1)S(1)}, u32[]{:S(2)}, u32[]{:S(2)}) collective-permute-start(bf16[2,256,128]{2,1,0:T(8,128)(2,1)S(1)} %broadcast_select_fusion.kv_in), channel_id=1, source_target_pairs={{0,32},{16,48},{32,64},{48,80},{64,96},{80,112},{96,128},{112,144}... | collective-permute-start | bytes 393224 | tf_op jit(solution)/shard_map/ppermute | solution.py:19
  17.8 16.3 %collective-permute-start.3 = (bf16[2,256,128]{2,1,0:T(8,128)(2,1)S(1)}, bf16[2,256,128]{2,1,0:T(8,128)(2,1)S(1)}, u32[]{:S(2)}, u32[]{:S(2)}) collective-permute-start(bf16[2,256,128]{2,1,0:T(8,128)(2,1)S(1)} %collective-permute-done), channel_id=1, source_target_pairs={{16,64},{48,96},{80,128},{112,160},{144,192},{176,224},{208,256},{... | collective-permute-start | bytes 393224 | tf_op jit(solution)/shard_map/ppermute | solution.py:19
  19.1 13.0 %collective-permute-start.2 = (bf16[2,256,128]{2,1,0:T(8,128)(2,1)S(1)}, bf16[2,256,128]{2,1,0:T(8,128)(2,1)S(1)}, u32[]{:S(2)}, u32[]{:S(2)}) collective-permute-start(bf16[2,256,128]{2,1,0:T(8,128)(2,1)S(1)} %collective-permute-done), channel_id=1, source_target_pairs={{0,32},{16,48},{32,64},{48,80},{64,96},{80,112},{96,128},{112,144}... | collective-permute-start | bytes 393224 | tf_op jit(solution)/shard_map/ppermute | solution.py:19
  34.5 14.0 %collective-permute-start.5 = (bf16[256,256]{1,0:T(8,128)(2,1)S(1)}, bf16[256,256]{1,0:T(8,128)(2,1)S(1)}, u32[]{:S(2)}, u32[]{:S(2)}) collective-permute-start(bf16[256,256]{1,0:T(8,128)(2,1)S(1)} %get-tuple-element.55), channel_id=1, source_target_pairs={{0,464},{32,496},{64,16},{96,48},{128,80},{160,112},{192,144},{224... | collective-permute-start | bytes 393224 | tf_op jit(solution)/shard_map/ppermute | solution.py:19
  39.5 11.5 %collective-permute-start.4 = (bf16[256,256]{1,0:T(8,128)(2,1)S(1)}, bf16[256,256]{1,0:T(8,128)(2,1)S(1)}, u32[]{:S(2)}, u32[]{:S(2)}) collective-permute-start(bf16[256,256]{1,0:T(8,128)(2,1)S(1)} %shard_map.101), channel_id=1, source_target_pairs={{0,480},{16,496},{32,0},{48,16},{64,32},{80,48},{96,64},{112,80},{... | collective-permute-start | bytes 393224 | tf_op jit(solution)/shard_map/ppermute | solution.py:19
  51.2 9.4 %collective-permute-start.6 = (bf16[256,256]{1,0:T(8,128)(2,1)S(1)}, bf16[256,256]{1,0:T(8,128)(2,1)S(1)}, u32[]{:S(2)}, u32[]{:S(2)}) collective-permute-start(bf16[256,256]{1,0:T(8,128)(2,1)S(1)} %shard_map.102), channel_id=1, source_target_pairs={{0,448},{16,464},{32,480},{48,496},{64,0},{80,16},{96,32},{112,48}... | collective-permute-start | bytes 393224 | tf_op jit(solution)/shard_map/ppermute | solution.py:19
  54.8 11.0 %collective-permute-start.7 = (bf16[256,256]{1,0:T(8,128)(2,1)S(1)}, bf16[256,256]{1,0:T(8,128)(2,1)S(1)}, u32[]{:S(2)}, u32[]{:S(2)}) collective-permute-start(bf16[256,256]{1,0:T(8,128)(2,1)S(1)} %get-tuple-element.56), channel_id=1, source_target_pairs={{0,480},{16,496},{32,0},{48,16},{64,32},{80,48},{96,64},{112,80},{... | collective-permute-start | bytes 393224 | tf_op jit(solution)/shard_map/ppermute | solution.py:19

commit v6 on v5

--- a/solution.py
+++ b/solution.py
@@ -15,7 +15,7 @@
 
 def shift(array, by, parity=None):
     n = lax.axis_size("cp")
-    pairs = [(i, (i + by) % n) for i in range(n) if parity is None or i % 2 == parity]
+    pairs = [(i, i + by) for i in range(n) if 0 <= i + by < n and parity in (None, i % 2)]
     return lax.ppermute(array, "cp", pairs)
 
 

time: 66.9 us -> 65 us (0.972)
  the two profiles are of different devices: /device:TPU:98 before, /device:TPU:96 now
where the time goes in v6:
time: 65 us; the launch traced here: 64.6 us
  starting transfers between devices  22.9 us (35%)
  blocking collectives  15.3 us (24%)
  waiting for transfers between devices  11.5 us (18%)
  Pallas kernels  11.4 us (18%)
  local copies, waits for them, and re-layouts  1.7 us (3%)
  other arithmetic  1.07 us (2%)
  between operations  0.82 us (1%)
    ppermute x8, starting transfers between devices, shift(): return lax.ppermute(array, 'cp', pairs)  22.9 us
    all_gather x5, blocking collectives, gather_pair(): lax.all_gather(array, 'cp', axis_index_groups=[[i, i + 1] for i in range(...  15.3 us
    ppermute x8, waiting for transfers between devices, shift(): return lax.ppermute(array, 'cp', pairs)  11.5 us
    pallas_call x10, Pallas kernels, call(): pl.pallas_call(kernel, out_shape=outs, in_specs=[pl.BlockSpec(memory_spac...  11.4 us
    unnamed x10, local copies, waits for them, and re-layouts  1.7 us
  transfers between devices with their start and end apart: 8, of which 3 were waited for; matrix products, arithmetic and copies ran while one was open for 0% of the time, Pallas kernels for 16%

profile of v6, /device:TPU:96, one launch (start us, length us, event | category | flops | bytes accessed | tf_op | source)
XLA Modules:
  0.0 64.6 jit_solution(11500415359853652731)
XLA Ops:
  0.6 0.0 copy-start.1
  0.7 1.0 %broadcast_select_fusion.kv_in = bf16[2,256,128]{2,1,0:T(8,128)(2,1)S(1)} fusion(pred[2]{0:T(512)(128)(4,1)S(1)} %iota_compare_fusion, bf16[256,128]{1,0:T(8,128)(2,1)} %param.9, bf16[256,128]{1,0:T(8,128)(2,1)} %param.8), kind=kLoop, calls=%fused_computation.2 | loop fusion | flops 65536 | bytes 262146 | tf_op jit(solution)/shard_map/jit(_where)/select_n | solution.py:305
  1.7 0.0 copy-start.4
  1.7 6.4 %collective-permute-start = (bf16[2,256,128]{2,1,0:T(8,128)(2,1)S(1)}, bf16[2,256,128]{2,1,0:T(8,128)(2,1)S(1)}, u32[]{:S(2)}, u32[]{:S(2)}) collective-permute-start(bf16[2,256,128]{2,1,0:T(8,128)(2,1)S(1)} %broadcast_select_fusion.kv_in), channel_id=1, source_target_pairs={{0,64},{16,80},{32,96},{48,112},{64,128},{80,144},{96,160},{112,17... | collective-permute-start | bytes 393224 | tf_op jit(solution)/shard_map/ppermute | solution.py:19
  8.1 2.0 %all-gather = bf16[4,256,128]{2,1,0:T(8,128)(2,1)S(1)} all-gather(bf16[2,256,128]{2,1,0:T(8,128)(2,1)S(1)} %broadcast_select_fusion.kv_in), channel_id=2, replica_groups={{0,16},{32,48},{64,80},{96,112},{128,144},{160,176},{192,208},{224,240}..., dimensions={0}, use_global_device_ids=true | all-gather | bytes 393216 | tf_op jit(solution)/shard_map/all_gather | solution.py:24
  10.1 0.0 copy-done.1
  10.1 0.0 copy-done.4
  10.1 0.0 copy-start.3
  10.1 1.0 %copy-done.3 = bf16[256,1024]{1,0:T(8,128)(2,1)S(1)} copy-done((bf16[256,1024]{1,0:T(8,128)(2,1)S(1)}, bf16[256,1024]{1,0:T(8,128)(2,1)}, u32[]{:S(2)}) %copy-start.3) | copy-done | bytes 524312
  11.1 0.0 copy-start
  11.1 1.2 %shard_map.94 = (s32[8,256]{1,0:T(8,128)S(1)}, f32[8,256]{1,0:T(8,128)S(1)}) custom-call(s32[51]{0:T(128)S(1)} %copy-done.4, bf16[256,1024]{1,0:T(8,128)(2,1)S(1)} %copy-done.1, bf16[256,1024]{1,0:T(8,128)(2,1)S(1)} %copy-done.3), custom_call_target="tpu_custom_call" | custom-call | flops 134217728 | bytes 1065164 | tf_op jit(solution)/shard_map/pallas_call | solution.py:275
  12.3 0.0 copy-start.2
  12.3 0.0 copy-done
  12.3 0.6 copy-done.2
  13.0 0.9 %shard_map.95 = (f32[8,256]{1,0:T(8,128)S(1)}, f32[8,256]{1,0:T(8,128)S(1)}) custom-call(bf16[256,1024]{1,0:T(8,128)(2,1)S(1)} %copy-done, s32[1,16]{1,0:T(1,128)S(1)} %copy-done.2, s32[8,256]{1,0:T(8,128)S(1)} %get-tuple-element.31.start_ref, bf16[2,2,256,128]{3,2,1,0:T(8,128)(2,1)S(1)} %bitcast.14), custom_call_target="tpu_custom_call" | custom-call | flops 268435456 | bytes 811072 | tf_op jit(solution)/shard_map/pallas_call | solution.py:275
  13.9 3.9 %collective-permute-start.1 = (bf16[2,256,128]{2,1,0:T(8,128)(2,1)S(1)}, bf16[2,256,128]{2,1,0:T(8,128)(2,1)S(1)}, u32[]{:S(2)}, u32[]{:S(2)}) collective-permute-start(bf16[2,256,128]{2,1,0:T(8,128)(2,1)S(1)} %broadcast_select_fusion.kv_in), channel_id=1, source_target_pairs={{0,32},{16,48},{32,64},{48,80},{64,96},{80,112},{96,128},{112,144}... | collective-permute-start | bytes 393224 | tf_op jit(solution)/shard_map/ppermute | solution.py:19
  17.8 0.0 collective-permute-done
  17.8 1.3 %collective-permute-start.3 = (bf16[2,256,128]{2,1,0:T(8,128)(2,1)S(1)}, bf16[2,256,128]{2,1,0:T(8,128)(2,1)S(1)}, u32[]{:S(2)}, u32[]{:S(2)}) collective-permute-start(bf16[2,256,128]{2,1,0:T(8,128)(2,1)S(1)} %collective-permute-done), channel_id=1, source_target_pairs={{16,64},{48,96},{80,128},{112,160},{144,192},{176,224},{208,256},{... | collective-permute-start | bytes 393224 | tf_op jit(solution)/shard_map/ppermute | solution.py:19
  19.1 3.8 %collective-permute-start.2 = (bf16[2,256,128]{2,1,0:T(8,128)(2,1)S(1)}, bf16[2,256,128]{2,1,0:T(8,128)(2,1)S(1)}, u32[]{:S(2)}, u32[]{:S(2)}) collective-permute-start(bf16[2,256,128]{2,1,0:T(8,128)(2,1)S(1)} %collective-permute-done), channel_id=1, source_target_pairs={{0,32},{16,48},{32,64},{48,80},{64,96},{80,112},{96,128},{112,144}... | collective-permute-start | bytes 393224 | tf_op jit(solution)/shard_map/ppermute | solution.py:19
  22.9 0.0 collective-permute-done.1.kv_in
  22.9 5.8 %all-gather.1 = bf16[4,2,256,128]{3,2,1,0:T(8,128)(2,1)S(1)} all-gather(bf16[2,2,256,128]{3,2,1,0:T(8,128)(2,1)S(1)} %pad_maximum_fusion), channel_id=3, replica_groups={{0,16},{32,48},{64,80},{96,112},{128,144},{160,176},{192,208},{224,240}..., dimensions={0}, use_global_device_ids=true | all-gather | bytes 786432 | tf_op jit(solution)/shard_map/all_gather | solution.py:24
  28.8 1.7 %shard_map.96 = (f32[8,256]{1,0:T(8,128)S(1)}, f32[8,256]{1,0:T(8,128)S(1)}) custom-call(bf16[256,1024]{1,0:T(8,128)(2,1)S(1)} %copy-done, s32[1,16]{1,0:T(1,128)S(1)} %copy-done.2, s32[8,256]{1,0:T(8,128)S(1)} %get-tuple-element.31.start_ref, f32[8,256]{1,0:T(8,128)S(1)} %get-tuple-element.39.m_in, f32[8,256]{1,0:T(8,128)S(1)} %get-tuple-element.40.l_in, ...), custom_call_target="tpu_custom_call" | custom-call | flops 536870912 | bytes 1089600 | tf_op jit(solution)/shard_map/pallas_call | solution.py:275
  30.5 0.0 collective-permute-done.2
  30.5 2.0 %all-gather.2 = bf16[4,256,128]{2,1,0:T(8,128)(2,1)S(1)} all-gather(bf16[2,256,128]{2,1,0:T(8,128)(2,1)S(1)} %collective-permute-done.2), channel_id=4, replica_groups={{0,16},{32,48},{64,80},{96,112},{128,144},{160,176},{192,208},{224,240}..., dimensions={0}, use_global_device_ids=true | all-gather | bytes 393216 | tf_op jit(solution)/shard_map/all_gather | solution.py:24
  32.6 0.0 collective-permute-done.3.kv4
  32.6 0.4 shard_map.97
  33.0 1.8 %collective-permute-start.5 = (bf16[256,256]{1,0:T(8,128)(2,1)S(1)}, bf16[256,256]{1,0:T(8,128)(2,1)S(1)}, u32[]{:S(2)}, u32[]{:S(2)}) collective-permute-start(bf16[256,256]{1,0:T(8,128)(2,1)S(1)} %get-tuple-element.55), channel_id=1, source_target_pairs={{64,16},{96,48},{128,80},{160,112},{192,144},{224,176},{256,208},{... | collective-permute-start | bytes 393224 | tf_op jit(solution)/shard_map/ppermute | solution.py:19
  34.8 3.2 %all-gather.4 = bf16[4,256,256]{2,1,0:T(8,128)(2,1)S(1)} all-gather(bf16[2,256,256]{2,1,0:T(8,128)(2,1)S(1)} %get-tuple-element.54), channel_id=6, replica_groups={{0,16},{32,48},{64,80},{96,112},{128,144},{160,176},{192,208},{224,240}..., dimensions={0}, use_global_device_ids=true | all-gather | bytes 786432 | tf_op jit(solution)/shard_map/all_gather | solution.py:24
  38.0 1.9 %collective-permute-start.4 = (bf16[256,256]{1,0:T(8,128)(2,1)S(1)}, bf16[256,256]{1,0:T(8,128)(2,1)S(1)}, u32[]{:S(2)}, u32[]{:S(2)}) collective-permute-start(bf16[256,256]{1,0:T(8,128)(2,1)S(1)} %shard_map.101), channel_id=1, source_target_pairs={{32,0},{48,16},{64,32},{80,48},{96,64},{112,80},{128,96},{144,112}... | collective-permute-start | bytes 393224 | tf_op jit(solution)/shard_map/ppermute | solution.py:19
  40.0 1.8 %shard_map.98 = (f32[256,256]{1,0:T(8,128)S(1)}, bf16[2,256,256]{2,1,0:T(8,128)(2,1)S(1)}, f32[1024,256]{1,0:T(8,128)S(1)}) custom-call(bf16[256,1024]{1,0:T(8,128)(2,1)S(1)} %copy-done, bf16[256,1024]{1,0:T(8,128)(2,1)S(1)} %copy-done.1, s32[1,16]{1,0:T(1,128)S(1)} %copy-done.2, ...), custom_call_target="tpu_custom_call", output_to_operand_aliasing={{2}: (7, {})} | custom-call | flops 2013265920 | bytes 4218944 | tf_op jit(solution)/shard_map/pallas_call | solution.py:275
  41.8 2.2 %all-gather.3 = bf16[4,256,256]{2,1,0:T(8,128)(2,1)S(1)} all-gather(bf16[2,256,256]{2,1,0:T(8,128)(2,1)S(1)} %get-tuple-element.47), channel_id=5, replica_groups={{0,16},{32,48},{64,80},{96,112},{128,144},{160,176},{192,208},{224,240}..., dimensions={0}, use_global_device_ids=true | all-gather | bytes 786432 | tf_op jit(solution)/shard_map/all_gather | solution.py:24
  44.0 0.0 collective-permute-done.5.back4_ref
  44.0 4.3 %collective-permute-done.4.back3_ref = bf16[256,256]{1,0:T(8,128)(2,1)S(1)} collective-permute-done((bf16[256,256]{1,0:T(8,128)(2,1)S(1)}, bf16[256,256]{1,0:T(8,128)(2,1)S(1)}, u32[]{:S(2)}, u32[]{:S(2)}) %collective-permute-start.4) | collective-permute-done | bytes 131104 | tf_op jit(solution)/shard_map/ppermute | solution.py:19
  48.3 0.1 shard_map.102
  48.3 1.9 %collective-permute-start.6 = (bf16[256,256]{1,0:T(8,128)(2,1)S(1)}, bf16[256,256]{1,0:T(8,128)(2,1)S(1)}, u32[]{:S(2)}, u32[]{:S(2)}) collective-permute-start(bf16[256,256]{1,0:T(8,128)(2,1)S(1)} %shard_map.102), channel_id=1, source_target_pairs={{64,0},{80,16},{96,32},{112,48},{128,64},{144,80},{160,96},{176,11... | collective-permute-start | bytes 393224 | tf_op jit(solution)/shard_map/ppermute | solution.py:19
  50.2 1.7 %shard_map.99 = (bf16[256,256]{1,0:T(8,128)(2,1)S(1)}, f32[1024,256]{1,0:T(8,128)S(1)}) custom-call(bf16[256,1024]{1,0:T(8,128)(2,1)S(1)} %copy-done, bf16[256,1024]{1,0:T(8,128)(2,1)S(1)} %copy-done.1, s32[1,16]{1,0:T(1,128)S(1)} %copy-done.2, s32[8,256]{1,0:T(8,128)S(1)} %get-tuple-element.31.start_ref, ...), custom_call_target="tpu_custom_call", output_to_operand_aliasing={{1}: (8, {})} | custom-call | flops 671088640 | bytes 3956800 | tf_op jit(solution)/shard_map/pallas_call | solution.py:275
  52.0 1.9 %collective-permute-start.7 = (bf16[256,256]{1,0:T(8,128)(2,1)S(1)}, bf16[256,256]{1,0:T(8,128)(2,1)S(1)}, u32[]{:S(2)}, u32[]{:S(2)}) collective-permute-start(bf16[256,256]{1,0:T(8,128)(2,1)S(1)} %get-tuple-element.56), channel_id=1, source_target_pairs={{32,0},{48,16},{64,32},{80,48},{96,64},{112,80},{128,96},{144,112}... | collective-permute-start | bytes 393224 | tf_op jit(solution)/shard_map/ppermute | solution.py:19
  53.9 2.8 %shard_map.100 = (f32[256,256]{1,0:T(8,128)S(1)}, bf16[256,1024]{1,0:T(8,128)(2,1)}) custom-call(bf16[256,1024]{1,0:T(8,128)(2,1)S(1)} %copy-done, bf16[256,1024]{1,0:T(8,128)(2,1)S(1)} %copy-done.1, s32[1,16]{1,0:T(1,128)S(1)} %copy-done.2, s32[8,256]{1,0:T(8,128)S(1)} %get-tuple-element.31.start_ref, f32[8,256]{1,0:T(8,128)S(1)} %get-tuple-element.38.delta_ref, ...), custom_call_target="tpu_custom_call" | custom-call | flops 671088640 | bytes 3039296 | tf_op jit(solution)/shard_map/pallas_call | solution.py:275
  56.7 6.3 %collective-permute-done.6 = bf16[256,256]{1,0:T(8,128)(2,1)S(1)} collective-permute-done((bf16[256,256]{1,0:T(8,128)(2,1)S(1)}, bf16[256,256]{1,0:T(8,128)(2,1)S(1)}, u32[]{:S(2)}, u32[]{:S(2)}) %collective-permute-start.6) | collective-permute-done | bytes 131104 | tf_op jit(solution)/shard_map/ppermute | solution.py:19
  63.0 0.9 %collective-permute-done.7.back1_ref = bf16[256,256]{1,0:T(8,128)(2,1)S(1)} collective-permute-done((bf16[256,256]{1,0:T(8,128)(2,1)S(1)}, bf16[256,256]{1,0:T(8,128)(2,1)S(1)}, u32[]{:S(2)}, u32[]{:S(2)}) %collective-permute-start.7) | collective-permute-done | bytes 131104 | tf_op jit(solution)/shard_map/ppermute | solution.py:19
  63.9 0.7 %shard_map.103 = (bf16[256,128]{1,0:T(8,128)(2,1)}, bf16[256,128]{1,0:T(8,128)(2,1)}) custom-call(f32[256,256]{1,0:T(8,128)S(1)} %convert_add_fusion.own_ref, bf16[2,2,256,256]{3,2,1,0:T(8,128)(2,1)S(1)} %bitcast.10, bf16[256,256]{1,0:T(8,128)(2,1)S(1)} %collective-permute-done.7.back1_ref), custom_call_target="tpu_custom_call" | custom-call | bytes 1048576 | tf_op jit(solution)/shard_map/pallas_call | solution.py:275
  (4 shorter events, 0.1 us)
Async XLA Ops:
  0.6 9.4 %copy-start.1 = (bf16[256,1024]{1,0:T(8,128)(2,1)S(1)}, bf16[256,1024]{1,0:T(8,128)(2,1)}, u32[]{:S(2)}) copy-start(bf16[256,1024]{1,0:T(8,128)(2,1)} %g_ref.9) | copy-start | bytes 1572868
  1.7 8.4 %copy-start.4 = (s32[51]{0:T(128)S(1)}, s32[51]{0:T(128)}, u32[]{:S(2)}) copy-start(s32[51]{0:T(128)} %doc_ref.1) | copy-start | bytes 616
  1.7 16.1 %collective-permute-start = (bf16[2,256,128]{2,1,0:T(8,128)(2,1)S(1)}, bf16[2,256,128]{2,1,0:T(8,128)(2,1)S(1)}, u32[]{:S(2)}, u32[]{:S(2)}) collective-permute-start(bf16[2,256,128]{2,1,0:T(8,128)(2,1)S(1)} %broadcast_select_fusion.kv_in), channel_id=1, source_target_pairs={{0,64},{16,80},{32,96},{48,112},{64,128},{80,144},{96,160},{112,17... | collective-permute-start | bytes 393224 | tf_op jit(solution)/shard_map/ppermute | solution.py:19
  10.1 1.0 %copy-start.3 = (bf16[256,1024]{1,0:T(8,128)(2,1)S(1)}, bf16[256,1024]{1,0:T(8,128)(2,1)}, u32[]{:S(2)}) copy-start(bf16[256,1024]{1,0:T(8,128)(2,1)} %o_ref.1) | copy-start | bytes 1572868
  11.1 1.2 %copy-start = (bf16[256,1024]{1,0:T(8,128)(2,1)S(1)}, bf16[256,1024]{1,0:T(8,128)(2,1)}, u32[]{:S(2)}) copy-start(bf16[256,1024]{1,0:T(8,128)(2,1)} %q_ref.11) | copy-start | bytes 1572868
  12.3 0.7 %copy-start.2 = (s32[1,16]{1,0:T(1,128)S(1)}, s32[1,16]{1,0:T(1,128)}, u32[]{:S(2)}) copy-start(s32[1,16]{1,0:T(1,128)} %off_ref.11) | copy-start | bytes 196
  13.9 9.0 %collective-permute-start.1 = (bf16[2,256,128]{2,1,0:T(8,128)(2,1)S(1)}, bf16[2,256,128]{2,1,0:T(8,128)(2,1)S(1)}, u32[]{:S(2)}, u32[]{:S(2)}) collective-permute-start(bf16[2,256,128]{2,1,0:T(8,128)(2,1)S(1)} %broadcast_select_fusion.kv_in), channel_id=1, source_target_pairs={{0,32},{16,48},{32,64},{48,80},{64,96},{80,112},{96,128},{112,144}... | collective-permute-start | bytes 393224 | tf_op jit(solution)/shard_map/ppermute | solution.py:19
  17.8 14.8 %collective-permute-start.3 = (bf16[2,256,128]{2,1,0:T(8,128)(2,1)S(1)}, bf16[2,256,128]{2,1,0:T(8,128)(2,1)S(1)}, u32[]{:S(2)}, u32[]{:S(2)}) collective-permute-start(bf16[2,256,128]{2,1,0:T(8,128)(2,1)S(1)} %collective-permute-done), channel_id=1, source_target_pairs={{16,64},{48,96},{80,128},{112,160},{144,192},{176,224},{208,256},{... | collective-permute-start | bytes 393224 | tf_op jit(solution)/shard_map/ppermute | solution.py:19
  19.1 11.5 %collective-permute-start.2 = (bf16[2,256,128]{2,1,0:T(8,128)(2,1)S(1)}, bf16[2,256,128]{2,1,0:T(8,128)(2,1)S(1)}, u32[]{:S(2)}, u32[]{:S(2)}) collective-permute-start(bf16[2,256,128]{2,1,0:T(8,128)(2,1)S(1)} %collective-permute-done), channel_id=1, source_target_pairs={{0,32},{16,48},{32,64},{48,80},{64,96},{80,112},{96,128},{112,144}... | collective-permute-start | bytes 393224 | tf_op jit(solution)/shard_map/ppermute | solution.py:19
  33.0 11.0 %collective-permute-start.5 = (bf16[256,256]{1,0:T(8,128)(2,1)S(1)}, bf16[256,256]{1,0:T(8,128)(2,1)S(1)}, u32[]{:S(2)}, u32[]{:S(2)}) collective-permute-start(bf16[256,256]{1,0:T(8,128)(2,1)S(1)} %get-tuple-element.55), channel_id=1, source_target_pairs={{64,16},{96,48},{128,80},{160,112},{192,144},{224,176},{256,208},{... | collective-permute-start | bytes 393224 | tf_op jit(solution)/shard_map/ppermute | solution.py:19
  38.0 10.2 %collective-permute-start.4 = (bf16[256,256]{1,0:T(8,128)(2,1)S(1)}, bf16[256,256]{1,0:T(8,128)(2,1)S(1)}, u32[]{:S(2)}, u32[]{:S(2)}) collective-permute-start(bf16[256,256]{1,0:T(8,128)(2,1)S(1)} %shard_map.101), channel_id=1, source_target_pairs={{32,0},{48,16},{64,32},{80,48},{96,64},{112,80},{128,96},{144,112}... | collective-permute-start | bytes 393224 | tf_op jit(solution)/shard_map/ppermute | solution.py:19
  48.3 14.6 %collective-permute-start.6 = (bf16[256,256]{1,0:T(8,128)(2,1)S(1)}, bf16[256,256]{1,0:T(8,128)(2,1)S(1)}, u32[]{:S(2)}, u32[]{:S(2)}) collective-permute-start(bf16[256,256]{1,0:T(8,128)(2,1)S(1)} %shard_map.102), channel_id=1, source_target_pairs={{64,0},{80,16},{96,32},{112,48},{128,64},{144,80},{160,96},{176,11... | collective-permute-start | bytes 393224 | tf_op jit(solution)/shard_map/ppermute | solution.py:19
  52.0 12.0 %collective-permute-start.7 = (bf16[256,256]{1,0:T(8,128)(2,1)S(1)}, bf16[256,256]{1,0:T(8,128)(2,1)S(1)}, u32[]{:S(2)}, u32[]{:S(2)}) collective-permute-start(bf16[256,256]{1,0:T(8,128)(2,1)S(1)} %get-tuple-element.56), channel_id=1, source_target_pairs={{32,0},{48,16},{64,32},{80,48},{96,64},{112,80},{128,96},{144,112}... | collective-permute-start | bytes 393224 | tf_op jit(solution)/shard_map/ppermute | solution.py:19
